TPU v7x, 32 devices: a whole 2x2x4 slice. The times are simulated.
32 devices in a mesh: dp: 4 (over y, x), blk: 8 (over z, core).
Axes of the slice: x: 2, y: 2, z: 4, core: 2. Of those that a mesh axis runs over, the one named last changes fastest.
Arguments:
- tokens: bfloat16 [8, 512, 1024], P('dp', 'blk'), may hold values from -6 to 6
- doc_ids: int32 [8, 512], P('dp', 'blk'), may hold values from 0 to 7, as said below
- w_query: float32 [1024, 1024], P(('dp', 'blk')), may hold values from -0.1875 to 0.1875
- w_key: float32 [1024, 1024], P(('dp', 'blk')), may hold values from -0.1875 to 0.1875
- w_value: float32 [1024, 1024], P(('dp', 'blk')), may hold values from -0.1875 to 0.1875
- w_out: float32 [1024, 1024], P(('dp', 'blk')), may hold values from -0.1875 to 0.1875
- w_up: float32 [1024, 4096], P(('dp', 'blk')), may hold values from -0.1875 to 0.1875
- w_gate: float32 [1024, 4096], P(('dp', 'blk')), may hold values from -0.1875 to 0.1875
- w_down: float32 [4096, 1024], P(('dp', 'blk')), may hold values from -0.09375 to 0.09375
- s_qk: float32 [1024], replicated, may hold values from 1 to 2
- alpha_attn: float32 [1024], replicated, may hold values from 0.2 to 0.8
- s_up: float32 [4096], replicated, may hold values from 0.5 to 2
- s_gate: float32 [4096], replicated, may hold values from 0.5 to 2
- alpha_mlp: float32 [1024], replicated, may hold values from 0.2 to 0.8
- cotangent: bfloat16 [8, 512, 1024], P('dp', 'blk'), may hold values from -6 to 6
Outputs:
- hidden_out: bfloat16 [8, 512, 1024], P('dp', 'blk')
- tokens_grad: float32 [8, 512, 1024], P('dp', 'blk')
- g_query: float32 [1024, 1024], P(('dp', 'blk'))
- g_key: float32 [1024, 1024], P(('dp', 'blk'))
- g_value: float32 [1024, 1024], P(('dp', 'blk'))
- g_out: float32 [1024, 1024], P(('dp', 'blk'))
- g_up: float32 [1024, 4096], P(('dp', 'blk'))
- g_gate: float32 [1024, 4096], P(('dp', 'blk'))
- g_down: float32 [4096, 1024], P(('dp', 'blk'))
- g_sqk: float32 [1024], P(('dp', 'blk'))
- g_alpha_attn: float32 [1024], P(('dp', 'blk'))
- g_s_up: float32 [4096], P(('dp', 'blk'))
- g_s_gate: float32 [4096], P(('dp', 'blk'))
- g_alpha_mlp: float32 [1024], P(('dp', 'blk'))
Inputs may be any that keep to these rules, and one draw needn't show every extreme that they name: `doc_ids`: along each row the ids never fall, and every id from 0 to 7 occurs in every row.
All inputs are finite; a program needn't handle non-finite values.
Results may differ from a plain program's by a relative error of at most 0.03.
Values may be sent and summed in bfloat16 or wider, within the bound.
No kernel may reach another device: no remote copies, remote signals or barrier semaphores. Data moves between devices by JAX's collectives and lax.ppermute only.
A program may use at most 320 MiB of HBM per device.

v0:
```python
import math

import jax
import jax.numpy as jnp
from jax import lax
from jax.experimental import pallas as pl
from jax.experimental.pallas import tpu as pltpu
from jax.sharding import Mesh
from jax.sharding import PartitionSpec as P

HEADS = 16
HEAD_DIM = 64
EPS = 1e-06
NEG = -1e30
BF = jnp.bfloat16
F32 = jnp.float32


def dot(a, b):
    return jnp.dot(a, b, preferred_element_type=F32)


def dot_t(a, b):
    return lax.dot_general(a, b, (((1,), (1,)), ((), ())), preferred_element_type=F32)


def tdot(a, b):
    return lax.dot_general(a, b, (((0,), (0,)), ((), ())), preferred_element_type=F32)


def rotate(tensor, cosines, sines):
    half_dim = tensor.shape[-1] // 2
    front = tensor[..., :half_dim]
    behind = tensor[..., half_dim:]
    return jnp.concatenate(
        [front * cosines - behind * sines, behind * cosines + front * sines], axis=-1
    )


def sphere(tensor):
    return tensor * lax.rsqrt(jnp.mean(tensor * tensor, axis=-1, keepdims=True) + EPS)


def head_unit(tensor, gains):
    return gains * tensor * lax.rsqrt(jnp.sum(tensor * tensor, axis=-1, keepdims=True) + EPS)


def residual_step(branch, residual_in, alpha):
    return sphere(residual_in + alpha * (sphere(branch) - residual_in))


def gating(up_proj, gate_proj, scale_up, scale_gate):
    return scale_up * up_proj * jax.nn.silu(scale_gate * gate_proj)


def make_plain(sizes):
    ny, nx, nw, nz, nc = sizes
    ndev = ny * nx * nw * nz * nc
    line = ("w", "z")
    nline = nw * nz
    quad = ("x", "z")
    nquad = nx * nz

    def swap(value, axes, count, k):
        return lax.ppermute(value, axes, [(i, i ^ k) for i in range(count)])

    def gather_rel(value, axes, count):
        return [value] + [swap(value, axes, count, k) for k in range(1, count)]

    def exchange_rel(chunks, axes, count):
        return [chunks[0]] + [swap(chunks[k], axes, count, k) for k in range(1, count)]

    def sum_rel(chunks, axes, count, kind=BF):
        got = exchange_rel([c.astype(kind) for c in chunks], axes, count)
        total = chunks[0].astype(F32)
        for piece in got[1:]:
            total = total + piece.astype(F32)
        return total

    def double(value, stages):
        for axis, count, k in stages:
            value = jnp.concatenate([value, swap(value, axis, count, k)], axis=0)
        return value

    def halve(value, stages, kind=BF):
        for axis, count, k in stages[::-1]:
            half = value.shape[0] // 2
            other = swap(value[half:].astype(kind), axis, count, k)
            value = value[:half].astype(F32) + other.astype(F32)
        return value

    def bits(axis, count):
        return [(axis, count, 1 << b) for b in range(count.bit_length() - 1)]

    def ranks(order):
        count = dict(y=ny, x=nx, w=nw, z=nz, c=nc)
        shape = [count[axis] for axis in order]
        found = {}
        for i, axis in enumerate(order):
            shifted = jnp.arange(count[axis]) ^ lax.axis_index(axis)
            found[axis] = shifted.reshape((-1,) + (1,) * (len(order) - 1 - i))
        flat = jnp.zeros(shape, jnp.int32)
        return found, flat

    def reorder(order, target):
        found, flat = ranks(order)
        count = dict(y=ny, x=nx, w=nw, z=nz, c=nc)
        index = flat
        for axis in target:
            index = index * count[axis] + found[axis]
        return index.reshape(-1)

    def place(pieces, rank):
        stack = jnp.stack(pieces)
        order = rank ^ jnp.arange(len(pieces))
        return jnp.take(stack, order, axis=0)

    def pick(array, rank, count):
        return [lax.dynamic_index_in_dim(array, rank ^ k, 0, False) for k in range(count)]

    def body(
        tokens, doc_ids, w_query, w_key, w_value, w_out, w_up, w_gate, w_down,
        s_qk, alpha_attn, s_up, s_gate, alpha_mlp, cotangent,
    ):
        nseq, seg, dm = tokens.shape
        rows = w_query.shape[0]
        ff = w_up.shape[1]
        ffq = ff // nquad
        ffb = ff // ndev
        hcols = dm // nline
        nheads = HEADS // nline
        score_scale = math.sqrt(HEAD_DIM)
        c_at = lax.axis_index("c")
        line_at = lax.axis_index(line)
        quad_at = lax.axis_index(quad)

        def by_line(w):
            return w.astype(BF).reshape(rows, nline, hcols)

        w_qkv = jnp.stack([by_line(w_query), by_line(w_key), by_line(w_value)], axis=2)
        w_qkv = w_qkv.transpose(1, 0, 2, 3).reshape(nline, rows, 3 * hcols)
        got = jnp.stack(exchange_rel(pick(w_qkv, line_at, nline), line, nline))
        got = jnp.stack(gather_rel(got, ("y", "x"), ny * nx))
        full = double(got[None], bits("c", nc)).reshape(ndev, rows, 3 * hcols)
        full_qkv = jnp.take(full, reorder("yxwzc", "cyxwz"), axis=0).reshape(dm, 3 * hcols)
        full_out = lax.all_gather(w_out.astype(BF), ("y", "x", "w", "z", "c"), axis=0, tiled=True)

        def by_quad(w):
            w = w.astype(BF).reshape(rows, ny, nx, nw, nz, nc, ffb)
            return w.transpose(2, 4, 0, 1, 3, 5, 6).reshape(nquad, rows, ffq)

        w_ug = jnp.concatenate([by_quad(w_up), by_quad(w_gate)], axis=2)
        got = jnp.stack(exchange_rel(pick(w_ug, quad_at, nquad), quad, nquad))
        stages = bits("w", nw) + bits("y", ny) + bits("c", nc)

        def ff_full(part):
            full = double(part[None], stages).reshape(ndev, rows, ffq)
            return jnp.take(full, reorder("yxwzc", "cywxz"), axis=0).reshape(dm, ffq)

        full_up, full_gate = ff_full(got[:, :, :ffq]), ff_full(got[:, :, ffq:])
        full_down = double(w_down.astype(BF)[None], stages)
        full_down = jnp.take(full_down, reorder("ywc", "cyw"), axis=0).reshape(ffq, dm)

        def my_ff(vec):
            v = vec.reshape(ny, nx, nw, nz, nc, ffb).transpose(1, 3, 0, 2, 4, 5)
            return lax.dynamic_index_in_dim(v.reshape(nquad, ffq), quad_at, 0, False)

        my_s_up, my_s_gate = my_ff(s_up), my_ff(s_gate)
        my_gain = lax.dynamic_index_in_dim(s_qk.reshape(nline, hcols), line_at, 0, False)

        def to_row(value):
            keep = lax.dynamic_index_in_dim(value, c_at, 0, False)
            send = lax.dynamic_index_in_dim(value, 1 - c_at, 0, False)
            return jnp.concatenate([keep, lax.ppermute(send, "c", [(0, 1), (1, 0)])], axis=0)

        def from_row(value, send_type):
            keep, send = value[:seg], value[seg:]
            other = lax.ppermute(send.astype(send_type), "c", [(0, 1), (1, 0)])
            pair = jnp.stack([keep, other.astype(value.dtype)])
            return jnp.where(c_at == 0, pair, pair[::-1])

        docs = doc_ids.astype(BF)
        extra = jnp.zeros((nseq, 16, dm), BF).at[:, 0, :seg].set(docs)
        ext = jnp.concatenate([tokens, extra], axis=1)
        mine = to_row(ext).reshape(2, seg + 16, dm)
        everyone = jnp.stack(gather_rel(mine, line, nline))
        row_tokens = everyone[:, :, :seg].reshape(nline * 2 * seg, dm)
        row_docs = everyone[:, :, seg, :seg].reshape(-1).astype(F32)
        peers = line_at ^ jnp.arange(nline)
        seg_at = 2 * peers[:, None] + jnp.stack([c_at, 1 - c_at])[None, :]
        index = (seg_at[:, :, None] * seg + jnp.arange(seg)).reshape(-1)
        start = jnp.sum((row_docs[None, :] < row_docs[:, None]).astype(jnp.int32), axis=1)
        pos = index - start
        allowed = (index[None, :] <= index[:, None]) & (index[None, :] >= start[:, None])
        frequency = 10000.0 ** (-jnp.arange(HEAD_DIM // 2, dtype=F32) / (HEAD_DIM // 2))
        angles = pos.astype(F32)[:, None] * frequency
        cosines, sines = jnp.cos(angles)[:, None, :], jnp.sin(angles)[:, None, :]
        nt = row_tokens.shape[0]
        x_low = mine[:, :seg].reshape(2 * seg, dm)
        x_row = x_low.astype(F32)

        pre = dot(row_tokens, full_qkv)

        def heads(t):
            return t.reshape(nt, nheads, HEAD_DIM)

        def unit_pair(q_pre, k_pre, gains):
            gains = gains.reshape(nheads, HEAD_DIM)
            return (
                head_unit(rotate(heads(q_pre), cosines, sines), gains),
                head_unit(rotate(heads(k_pre), cosines, sines), gains),
            )

        (q_unit, k_unit), unit_pull = jax.vjp(
            unit_pair, pre[:, :hcols], pre[:, hcols : 2 * hcols], my_gain
        )
        q_low, k_low = q_unit.astype(BF), k_unit.astype(BF)
        v_low = heads(pre[:, 2 * hcols :].astype(BF))
        scores = jnp.einsum("qhd,khd->hqk", q_low, k_low, preferred_element_type=F32) * score_scale
        scores = jnp.where(allowed[None], scores, NEG)
        peak = jnp.max(scores, axis=-1, keepdims=True)
        raw = jnp.where(allowed[None], jnp.exp(scores - peak), 0.0)
        probs = raw / jnp.sum(raw, axis=-1, keepdims=True)
        p_low = probs.astype(BF)
        attended = jnp.einsum("hqk,khd->qhd", p_low, v_low, preferred_element_type=F32)
        att_low = attended.astype(BF).reshape(nline, 2 * seg, hcols)
        got = place(exchange_rel([att_low[k] for k in range(nline)], line, nline), line_at)
        att_mine = got.transpose(1, 0, 2).reshape(2 * seg, dm)

        h_attn = dot(att_mine, full_out)
        h_one, attn_pull = jax.vjp(residual_step, h_attn, x_row, alpha_attn)
        h_low = jnp.concatenate(gather_rel(h_one.astype(BF), quad, nquad), axis=0)
        up, gate = dot(h_low, full_up), dot(h_low, full_gate)
        mixed, gate_pull = jax.vjp(gating, up, gate, my_s_up, my_s_gate)
        mixed_low = mixed.astype(BF)
        part = dot(mixed_low, full_down).reshape(nquad, 2 * seg, dm)
        h_mlp = sum_rel([part[k] for k in range(nquad)], quad, nquad)
        result, out_pull = jax.vjp(residual_step, h_mlp, h_one, alpha_mlp)
        hidden_out = from_row(result.astype(BF), BF)

        d_result = to_row(cotangent).astype(F32)
        d_hmlp, d_hone, g_alpha_mlp = out_pull(d_result)
        dm_low = jnp.concatenate(gather_rel(d_hmlp.astype(BF), quad, nquad), axis=0)
        d_mixed = dot_t(dm_low, full_down)
        d_up, d_gate, g_s_up, g_s_gate = gate_pull(d_mixed)
        du_low, dg_low = d_up.astype(BF), d_gate.astype(BF)
        part = dot_t(du_low, full_up) + dot_t(dg_low, full_gate)
        part = part.reshape(nquad, 2 * seg, dm)
        d_hone = d_hone + sum_rel([part[k] for k in range(nquad)], quad, nquad)
        g_down = tdot(mixed_low, dm_low).reshape(ny * nw * nc, ffb, dm)
        g_down = halve(jnp.take(g_down, reorder("cyw", "ywc"), axis=0), stages)[0]

        def ff_scatter(left, right):
            part = tdot(left, right).reshape(ndev, rows, ffq)
            part = jnp.take(part, reorder("cywxz", "yxwzc"), axis=0)
            part = halve(part.reshape(ny * nw * nc, nquad, rows, ffq), stages)[0].astype(BF)
            got = place(exchange_rel([part[k] for k in range(nquad)], quad, nquad), quad_at)
            got = got.reshape(nx, nz, rows, ny, nw, nc, ffb).transpose(2, 3, 0, 4, 1, 5, 6)
            return got.reshape(rows, ff).astype(F32)

        g_up, g_gate = ff_scatter(h_low, du_low), ff_scatter(h_low, dg_low)

        d_hattn, d_tokens, g_alpha_attn = attn_pull(d_hone)
        dh_low = d_hattn.astype(BF)

        def to_owner(part, kind=BF):
            part = jnp.take(part, reorder("cyxwz", "yxwzc"), axis=0)
            part = halve(part.reshape((nc, ny * nx, nline) + part.shape[1:]), bits("c", nc), kind)[0]
            part = sum_rel([part[k] for k in range(ny * nx)], ("y", "x"), ny * nx, kind)
            return sum_rel([part[k] for k in range(nline)], line, nline, kind)

        g_out = to_owner(tdot(att_mine, dh_low).reshape(ndev, rows, dm))
        d_att = dot_t(dh_low, full_out).astype(BF).reshape(2 * seg, nline, hcols).transpose(1, 0, 2)
        d_att = jnp.concatenate(
            exchange_rel(pick(d_att, line_at, nline), line, nline), axis=0
        ).reshape(nt, nheads, HEAD_DIM)
        delta = jnp.sum(d_att.astype(F32) * attended, axis=-1)
        d_probs = jnp.einsum("qhd,khd->hqk", d_att, v_low, preferred_element_type=F32)
        d_scores = (probs * (d_probs - delta.T[:, :, None])).astype(BF)
        d_q = score_scale * jnp.einsum("hqk,khd->qhd", d_scores, k_low, preferred_element_type=F32)
        d_k = score_scale * jnp.einsum("hqk,qhd->khd", d_scores, q_low, preferred_element_type=F32)
        d_v = jnp.einsum("hqk,qhd->khd", p_low, d_att, preferred_element_type=F32)
        d_qpre, d_kpre, g_sqk = unit_pull((d_q, d_k))
        d_qkv = jnp.concatenate([d_qpre, d_kpre, d_v.reshape(nt, hcols)], axis=1).astype(BF)
        part = dot_t(d_qkv, full_qkv).reshape(nline, 2 * seg, dm)
        tokens_grad = d_tokens + sum_rel([part[k] for k in range(nline)], line, nline)
        tokens_grad = from_row(tokens_grad, BF)
        g_qkv = tdot(row_tokens, d_qkv).reshape(ndev, rows, 3 * hcols)
        g_qkv = jnp.take(g_qkv, reorder("cyxwz", "yxwzc"), axis=0)
        g_qkv = halve(g_qkv.reshape(nc, ny * nx, nline, rows, 3 * hcols), bits("c", nc))[0]
        g_qkv = sum_rel([g_qkv[k] for k in range(ny * nx)], ("y", "x"), ny * nx).astype(BF)
        got = place(exchange_rel([g_qkv[k] for k in range(nline)], line, nline), line_at)
        got = got.reshape(nline, rows, 3, hcols).transpose(2, 1, 0, 3).reshape(3, rows, dm)
        g_query, g_key, g_value = got.astype(F32)

        def spread(vec, rank, count):
            return jnp.where(jnp.arange(count)[:, None] == rank, vec[None], 0.0)

        def ff_order(vec):
            v = spread(vec, quad_at, nquad).reshape(nx, nz, ny, nw, nc, ffb)
            return v.transpose(2, 0, 3, 1, 4, 5).reshape(ndev, ffb)

        vecs = jnp.concatenate(
            [
                spread(g_sqk, line_at, nline).reshape(ndev, -1),
                g_alpha_attn.reshape(ndev, -1),
                ff_order(g_s_up),
                ff_order(g_s_gate),
                g_alpha_mlp.reshape(ndev, -1),
            ],
            axis=1,
        )
        vecs = to_owner(vecs, F32)
        cuts = [rows, 2 * rows, 2 * rows + ffb, 2 * rows + 2 * ffb]
        g_sqk, g_alpha_attn, g_s_up, g_s_gate, g_alpha_mlp = jnp.split(vecs, cuts)
        return (
            hidden_out, tokens_grad, g_query, g_key, g_value, g_out, g_up, g_gate, g_down,
            g_sqk, g_alpha_attn, g_s_up, g_s_gate, g_alpha_mlp,
        )

    return body


VM = pl.BlockSpec(memory_space=pltpu.VMEM)
SM = pl.BlockSpec(memory_space=pltpu.SMEM)
HB = pl.BlockSpec(memory_space=pltpu.HBM)


def call(kernel, outs, args, hbm=(), hbm_out=(), scratch=(), flops=0, mib=60, after=()):
    moved = sum(math.prod(a.shape) * a.dtype.itemsize for a in args)
    moved += sum(math.prod(s) * jnp.dtype(d).itemsize for s, d in outs)
    count = len(args)

    def run(*refs):
        kernel(*refs[:count], *refs[count + len(after) :])

    specs = [SM] + [HB if i in hbm else VM for i in range(1, count)]
    specs += [pl.BlockSpec(memory_space=pl.ANY)] * len(after)
    return pl.pallas_call(
        run,
        out_shape=[jax.ShapeDtypeStruct(s, d) for s, d in outs],
        in_specs=specs,
        out_specs=[HB if i in hbm_out else VM for i in range(len(outs))],
        scratch_shapes=list(scratch),
        compiler_params=pltpu.CompilerParams(vmem_limit_bytes=mib << 20),
        cost_estimate=pl.CostEstimate(flops=flops, bytes_accessed=moved, transcendentals=0),
    )(*args, *after)


def row_norm(v):
    return lax.rsqrt(jnp.mean(v * v, axis=-1, keepdims=True) + EPS)


def sphere_back(dy, y, norm):
    return (dy - y * jnp.mean(dy * y, axis=-1, keepdims=True)) * norm


def make_kernels(sizes):
    ny, nx, nw, nz, nc = sizes
    ndev = ny * nx * nw * nz * nc
    nyx, nline = ny * nx, nw * nz
    ndpc = nyx * nc
    line, yx, dpc = ("w", "z"), ("y", "x"), ("y", "x", "c")

    def swap(value, axes, count, k):
        return lax.ppermute(value, axes, [(i, i ^ k) for i in range(count)])

    def exchange(chunks, axes, count):
        return [chunks[0]] + [swap(chunks[k], axes, count, k) for k in range(1, count)]

    def gather(value, axes, count):
        return exchange([value] * count, axes, count)

    def body(
        tokens, doc_ids, w_query, w_key, w_value, w_out, w_up, w_gate, w_down,
        s_qk, alpha_attn, s_up, s_gate, alpha_mlp, cotangent,
    ):
        nseq, seg, dm = tokens.shape
        rows = w_query.shape[0]
        ff = w_up.shape[1]
        ffq, ffb = ff // nline, ff // ndev
        sub = nc * ffb
        hc = dm // nline
        nheads = HEADS // nline
        nt = nline * 2 * seg
        tk = 2 * seg
        pad = 16
        ext = seg + pad
        scale = math.sqrt(HEAD_DIM)
        tile = 256

        at = [lax.axis_index(a) for a in "yxwzc"]
        ranks = jnp.stack(at + [lax.axis_index(yx), lax.axis_index(line)])
        ranks = ranks.astype(jnp.int32)

        def pack_tokens(rk, tok, docs, keep, send):
            c = rk[4]
            first = lax.broadcasted_iota(jnp.int32, (pad, dm), 0) == 0
            for out, which in ((keep, c), (send, 1 - c)):
                out[:seg] = tok[which]
                out[seg:] = jnp.where(first, docs[which], 0.0).astype(BF)

        def ff_cols(rk, k):
            runs = [(d * nline + (rk[6] ^ k)) * sub for d in range(nyx)]
            return [pl.ds(pl.multiple_of(run, 128), sub) for run in runs]

        def pack_qkv(rk, wq, wk, wv, *outs):
            for k in range(nline):
                cols = pl.ds(pl.multiple_of((rk[6] ^ k) * hc, 128), hc)
                for i, w in enumerate((wq, wk, wv)):
                    outs[k][:, i * hc : (i + 1) * hc] = w[:, cols].astype(BF)

        def pack_weights(rk, wu, wg, wo, gain, su, sg, *outs):
            for k in range(nline):
                out_ff = outs[k]
                for d, cols in enumerate(ff_cols(rk, k)):
                    for i, w in enumerate((wu, wg)):
                        here = i * ffq + d * sub
                        out_ff[:, here : here + sub] = w[:, cols].astype(BF)
                out_ff[:, 2 * ffq :] = wo[...].astype(BF)
            outs[nline][...] = gain[:, pl.ds(pl.multiple_of(rk[6] * hc, 128), hc)]
            for d, cols in enumerate(ff_cols(rk, 0)):
                here = slice(d * sub, (d + 1) * sub)
                outs[nline + 1][:, here] = su[:, cols]
                outs[nline + 2][:, here] = sg[:, cols]

        docs = jnp.pad(doc_ids.astype(F32), ((0, 0), (0, dm - seg))).reshape(nseq, 1, dm)
        packed = call(
            pack_qkv, [((rows, 3 * hc), BF)] * nline, (ranks, w_query, w_key, w_value)
        )
        keep, send = call(pack_tokens, [((ext, dm), BF)] * 2, (ranks, tokens, docs), after=(packed[0],))

        def join_tokens(rk, near, far, out):
            out[:seg] = near[:seg]
            out[seg:tk] = far[:seg]
            row = lax.broadcasted_iota(jnp.int32, (pad, dm), 0)
            ids = far[seg:].astype(F32)[:1]
            out[tk:] = jnp.where(row == 1, ids, near[seg:].astype(F32)).astype(BF)

        (mine,) = call(join_tokens, [((tk + pad, dm), BF)], (ranks, keep, swap(send, "c", nc, 1)))
        packed_ff = call(
            pack_weights,
            [((rows, 2 * ffq + dm), BF)] * nline
            + [((1, hc), F32)]
            + [((1, ffq), F32)] * 2,
            (ranks, w_up, w_gate, w_out, s_qk.reshape(1, dm))
            + (s_up.reshape(1, ff), s_gate.reshape(1, ff)),
            after=(keep,),
        )
        packed_ff, (my_gain, my_su, my_sg) = packed_ff[:nline], packed_ff[nline:]

        w_got = exchange(packed, line, nline)
        ff_got = exchange(packed_ff, line, nline)
        pieces = gather(mine, line, nline)

        def stack(rk, *refs):
            for k in range(nline):
                refs[nline][k * rows : (k + 1) * rows, :] = refs[k][...]

        (got,) = call(stack, [((ffb, 3 * hc), BF)], (ranks, *w_got))
        qkv_full = lax.all_gather(got, dpc, axis=0, tiled=True)

        def stack_ff(rk, *refs):
            parts, (wd, out) = refs[:nline], refs[nline:]
            for k in range(nline):
                out[k * rows : (k + 1) * rows, : 2 * ffq + dm] = parts[k][...]
            out[:, 2 * ffq + dm :] = wd[...].astype(BF)

        (got,) = call(
            stack_ff,
            [((ffb, 2 * ffq + 2 * dm), BF)],
            (ranks, *ff_got, w_down),
            after=(got, mine),
        )
        ff_full = lax.all_gather(got, dpc, axis=0, tiled=True)

        place = jnp.arange(nt, dtype=F32)[:, None]
        freq = 10000.0 ** (-jnp.arange(HEAD_DIM // 2, dtype=F32) / (HEAD_DIM // 2))
        angles = place * freq
        cosines, sines = jnp.cos(angles), jnp.sin(angles)
        reps = 128 // HEAD_DIM
        table = jnp.concatenate(
            [cosines] * (2 * reps) + [-sines, sines] * reps, axis=1
        )
        table_hi = table.astype(BF)
        table_lo = (table - table_hi.astype(F32)).astype(BF)

        def natural(rk, src, cols, dst, sems):
            copies = []
            for b in range(ndpc):
                for k in range(nline):
                    row = ((b // nc) * nline + (rk[6] ^ k)) * nc + b % nc
                    row = pl.ds(pl.multiple_of(row * rows, 32), rows)
                    block = src.at[pl.ds((b * nline + k) * rows, rows), cols]
                    copies.append(pltpu.make_async_copy(block, dst.at[row], sems.at[len(copies)]))
            return copies

        def heads_swap(v, low):
            width = v.shape[1]
            half = HEAD_DIM // 2
            return jnp.where(low, pltpu.roll(v, width - half, 1), pltpu.roll(v, half, 1))

        def low_half():
            lane = lax.broadcasted_iota(jnp.int32, (nt, hc), 1)
            return lane % HEAD_DIM < HEAD_DIM // 2

        def token_index(rk, axis, shape):
            t = lax.broadcasted_iota(jnp.int32, shape, axis)
            peer = (t // tk) ^ rk[6]
            core = ((t // seg) % 2) ^ rk[4]
            return (peer * 2 + core) * seg + t % seg

        def allowed_keys(rk, start):
            key = token_index(rk, 1, (1, nt))
            query = token_index(rk, 0, (nt, 1))
            return (key <= query) & (key.astype(F32) >= start)

        def attn_forward(rk, *refs):
            ext_refs, refs = refs[:nline], refs[nline:]
            stack, gain, t_hi, t_lo = refs[:4]
            att_ref, refs = refs[4], refs[5:]
            x_ref, w_ref, rq_ref, rk_ref, q_ref, k_ref, v_ref, bias_ref, cs_ref = refs[:9]
            full_ref, inv_ref, sems = refs[9:]
            copies = natural(rk, stack, pl.ds(0, 3 * hc), w_ref, sems)
            for copy in copies:
                copy.start()
            ids = []
            for k in range(nline):
                x_ref[k * tk : (k + 1) * tk, :] = ext_refs[k][:tk, :]
                tail = ext_refs[k][tk:, :128].astype(F32)
                ids += [tail[:1, :seg], tail[1:2, :seg]]
            ids = jnp.concatenate(ids, axis=1)
            same = lax.broadcasted_iota(jnp.int32, (nt, nt), 0) == lax.broadcasted_iota(
                jnp.int32, (nt, nt), 1
            )
            ids_col = jnp.sum(jnp.where(same, ids, 0.0), axis=1, keepdims=True)
            start = jnp.sum(jnp.where(ids < ids_col, 1.0, 0.0), axis=1, keepdims=True)
            pos = token_index(rk, 0, (nt, 1)) - start.astype(jnp.int32)
            hot = (lax.broadcasted_iota(jnp.int32, (nt, nt), 1) == pos).astype(F32).astype(BF)
            cs = dot(hot, t_hi[...]) + dot(hot, t_lo[...])
            cs_ref[...] = cs
            cos = jnp.concatenate([cs[:, :128]] * (hc // 128), axis=1)
            sin = jnp.concatenate([cs[:, 128:]] * (hc // 128), axis=1)
            bias_ref[...] = jnp.where(allowed_keys(rk, start), 0.0, NEG).astype(BF)
            for copy in copies:
                copy.wait()
            low = low_half()
            for i, (raw_ref, unit_ref) in enumerate(((rq_ref, q_ref), (rk_ref, k_ref))):
                pre = dot(x_ref[...], w_ref[:, i * hc : (i + 1) * hc])
                turned = pre * cos + heads_swap(pre, low) * sin
                raw_ref[...] = turned
                for h in range(nheads):
                    at_h = slice(h * HEAD_DIM, (h + 1) * HEAD_DIM)
                    part = turned[:, at_h]
                    norm = lax.rsqrt(jnp.sum(part * part, axis=1, keepdims=True) + EPS)
                    unit = (gain[:, at_h] * part * norm).astype(BF)
                    unit_ref[:, at_h] = unit * (scale if i == 0 else 1)
            v_ref[...] = dot(x_ref[...], w_ref[:, 2 * hc :]).astype(BF)
            for h in range(nheads):
                at_h = slice(h * HEAD_DIM, (h + 1) * HEAD_DIM)
                raw = jnp.exp(dot_t(q_ref[:, at_h], k_ref[:, at_h]) + bias_ref[...].astype(F32))
                inv = 1.0 / jnp.sum(raw, axis=1, keepdims=True)
                att_h = dot(raw.astype(BF), v_ref[:, at_h]) * inv
                full_ref[:, at_h] = att_h
                att_ref[:, at_h] = att_h.astype(BF)
                inv_ref[:, h : h + 1] = inv

        unit = ((nt, hc), BF)
        outs = call(
            attn_forward,
            [unit, ((nt, dm), BF), ((dm, 3 * hc), BF), ((nt, hc), F32), ((nt, hc), F32)]
            + [unit, unit, unit, ((nt, nt), BF), ((nt, 256), F32), ((nt, hc), F32), ((nt, 128), F32)],
            (ranks, *pieces, qkv_full, my_gain, table_hi, table_lo),
            hbm=(1 + nline,),
            scratch=[pltpu.SemaphoreType.DMA((ndev,))],
            flops=2 * nt * dm * 3 * hc + 4 * nt * nt * hc,
        )
        att, outs = outs[0], outs[1:]
        x_all, w_qkv, r_q, r_k, q_low, k_low, v_low, bias, cs, att_full, inv = outs
        att_got = gather(att, line, nline)

        def own_x(ext_ref):
            return ext_ref[:tk].astype(F32)

        alpha_a, alpha_m = alpha_attn.reshape(1, dm), alpha_mlp.reshape(1, dm)
        full = ((tk, dm), F32)

        def load_out(rk, stack, wo, sems):
            return natural(rk, stack, pl.ds(2 * ffq, dm), wo, sems)

        def load_ff(rk, stack, scratch):
            wug, wd, sems, sem_d = scratch
            down = stack.at[:, pl.ds(2 * ffq + dm, dm)]
            return (
                natural(rk, stack, pl.ds(0, 2 * ffq), wug, sems),
                [pltpu.make_async_copy(down, wd, sem_d.at[0])],
            )

        w_scratch = [pltpu.VMEM((dm, 2 * ffq), BF), pltpu.VMEM((ffq, dm), BF)]
        w_scratch += [pltpu.SemaphoreType.DMA((ndev,)), pltpu.SemaphoreType.DMA((1,))]
        out_scratch = [pltpu.VMEM((dm, dm), BF), pltpu.SemaphoreType.DMA((ndev,))]

        def gate_terms(gate, sg):
            v = sg * gate
            s = 1.0 / (1.0 + jnp.exp(-v))
            return v, s

        def forward(rk, *refs):
            att_refs, refs = refs[:nline], refs[nline:]
            x_ref, alpha, stack, su, sg = refs[:5]
            parts, refs = refs[5 : 5 + nline], refs[5 + nline :]
            h_all, up_ref, gate_ref, mixed_ref, one_ref, raw_ref = refs[:6]
            scratch = refs[6:]
            wug, wd = scratch[:2]
            w, a_ref = scratch[4], scratch[6]
            first, third = load_ff(rk, stack, scratch[:4])
            out_copies = load_out(rk, stack, w, scratch[5])
            for copy in out_copies + first + third:
                copy.start()
            for k in range(nline):
                spot = pl.ds(pl.multiple_of((rk[6] ^ k) * hc, hc), hc)
                for m in range(nline):
                    block = att_refs[k][(m ^ k) * tk : ((m ^ k) + 1) * tk, :]
                    a_ref[m * tk : (m + 1) * tk, spot] = block
            for copy in out_copies:
                copy.wait()
            for m in range(nline):
                total = dot(a_ref[m * tk : (m + 1) * tk, :], w[...])
                x = x_ref[m * tk : (m + 1) * tk, :].astype(F32)
                z = x + alpha[...] * (total * row_norm(total) - x)
                one = z * row_norm(z)
                h_all[m * tk : (m + 1) * tk, :] = one.astype(BF)
                if m == 0:
                    one_ref[...] = one
                    raw_ref[...] = total
            for copy in first:
                copy.wait()

            @pl.loop(0, ffq // tile, unroll=True)
            def _(j):
                cols = pl.ds(pl.multiple_of(j * tile, tile), tile)
                up = dot(h_all[...], wug[:, cols])
                gate = dot(h_all[...], wug[:, pl.ds(pl.multiple_of(ffq + j * tile, tile), tile)])
                up_ref[:, cols] = up.astype(BF)
                gate_ref[:, cols] = gate.astype(BF)
                v, s = gate_terms(gate, sg[:, cols])
                mixed_ref[:, cols] = (su[:, cols] * up * (v * s)).astype(BF)

            for copy in third:
                copy.wait()

            @pl.loop(0, dm // tile, unroll=True)
            def _(j):
                cols = pl.ds(pl.multiple_of(j * tile, tile), tile)
                part = dot(mixed_ref[...], wd[:, cols])
                for k in range(nline):
                    parts[k][:, cols] = part[k * tk : (k + 1) * tk].astype(parts[k].dtype)

        part_shapes = [((tk, dm), F32)] + [((tk, dm), BF)] * (nline - 1)
        outs = call(
            forward,
            part_shapes
            + [((nt, dm), BF), ((nt, ffq), BF), ((nt, ffq), BF), ((nt, ffq), BF), full, full],
            (ranks, *att_got, x_all, alpha_a, ff_full, my_su, my_sg),
            hbm=(3 + nline,),
            scratch=w_scratch + out_scratch + [pltpu.VMEM((nt, dm), BF)],
            flops=6 * nt * dm * ffq + 2 * nt * dm * dm,
        )
        mlp_parts, (h_all, up, gate, mixed, h_one, h_attn) = outs[:nline], outs[nline:]
        mlp_got = exchange(mlp_parts, line, nline)

        def split_rows(rk, cot, keep, send):
            keep[...] = cot[rk[4]]
            send[...] = cot[1 - rk[4]]

        half_low = ((seg, dm), BF)
        cot_keep, cot_send = call(split_rows, [half_low] * 2, (ranks, cotangent))
        cot_recv = swap(cot_send, "c", nc, 1)

        def mlp_update(rk, *refs):
            parts, refs = refs[:nline], refs[nline:]
            one_ref, alpha_ref, ck, cr, hid_keep, hid_send, dm_ref, direct, g_alpha = refs
            h = parts[0][...]
            for k in range(1, nline):
                h = h + parts[k][...].astype(F32)
            one, alpha = one_ref[...], alpha_ref[...]
            norm_h = row_norm(h)
            b = h * norm_h
            gap = b - one
            z = one + alpha * gap
            norm_z = row_norm(z)
            y = z * norm_z
            low = y.astype(BF)
            hid_keep[...] = low[:seg]
            hid_send[...] = low[seg:]
            dy = jnp.concatenate([ck[...], cr[...]], axis=0).astype(F32)
            dz = sphere_back(dy, y, norm_z)
            g_alpha[...] = jnp.sum(dz * gap, axis=0, keepdims=True)
            direct[...] = dz * (1.0 - alpha)
            dm_ref[...] = sphere_back(dz * alpha, b, norm_h).astype(BF)

        outs = call(
            mlp_update,
            [half_low, half_low, ((tk, dm), BF), full, ((1, dm), F32)],
            (ranks, *mlp_got, h_one, alpha_m, cot_keep, cot_recv),
        )
        hid_keep, hid_send, dm_low, d_one_direct, g_alpha_mlp = outs
        hid_recv = swap(hid_send, "c", nc, 1)
        dm_got = gather(dm_low, line, nline)

        def ff_back(rk, late, *refs):
            d_refs, stack = refs[:nline], refs[nline]
            su_ref, sg_ref, up_ref, gate_ref = refs[nline + 1 : nline + 5]
            refs = refs[nline + 5 :]
            parts, (d_all, dug, g_su, g_sg) = refs[:nline], refs[nline : nline + 4]
            scratch = refs[nline + 4 :]
            wug, wd = scratch[:2]
            first, third = load_ff(rk, stack, scratch)
            for copy in third + late[:2] + first + late[2:]:
                copy.start()
            for k in range(nline):
                d_all[k * tk : (k + 1) * tk, :] = d_refs[k][...]
            for copy in third + late[:2]:
                copy.wait()

            @pl.loop(0, ffq // tile)
            def _(j):
                cols = pl.ds(pl.multiple_of(j * tile, tile), tile)
                d_mixed = dot_t(d_all[...], wd[cols, :])
                up, gate = up_ref[:, cols].astype(F32), gate_ref[:, cols].astype(F32)
                su, sg = su_ref[:, cols], sg_ref[:, cols]
                v, s = gate_terms(gate, sg)
                silu = v * s
                dug[:, cols] = (d_mixed * su * silu).astype(BF)
                slope = d_mixed * su * up * (s * (1.0 + v * (1.0 - s)))
                other = pl.ds(pl.multiple_of(ffq + j * tile, tile), tile)
                dug[:, other] = (slope * sg).astype(BF)
                g_su[:, cols] = jnp.sum(d_mixed * up * silu, axis=0, keepdims=True)
                g_sg[:, cols] = jnp.sum(slope * gate, axis=0, keepdims=True)

            for copy in first:
                copy.wait()

            @pl.loop(0, dm // tile)
            def _(j):
                cols = pl.ds(pl.multiple_of(j * tile, tile), tile)
                part = dot_t(dug[...], wug[cols, :])
                for k in range(nline):
                    parts[k][:, cols] = part[k * tk : (k + 1) * tk].astype(parts[k].dtype)


        def stored(rk, g_ref, out, width, block, sems):
            d, peer, c = block // (nline * nc), (block // nc) % nline, block % nc
            spot = ((d * nc + c) * nline + (peer ^ rk[6])) * rows
            src = g_ref.at[pl.ds(pl.multiple_of(block * rows, 32), rows)]
            dst = out.at[pl.ds(pl.multiple_of(spot, 32), rows), pl.ds(0, width)]
            return pltpu.make_async_copy(src, dst, sems.at[block])

        def outer_ff(rk, h, dug, mixed_ref, d_all, out, g_ref, g_down_ref, sems, sem_d):
            def store(block):
                return stored(rk, g_ref, out, 2 * ffq, block, sems)

            @pl.loop(0, dm // tile, unroll=True)
            def _(j):
                cols = pl.ds(pl.multiple_of(j * tile, tile), tile)
                g_ref[cols, :] = tdot(h[:, cols], dug[...]).astype(BF)
                for i in range(tile // rows):
                    store(j * (tile // rows) + i).start()

            @pl.loop(0, ffq // tile, unroll=True)
            def _(j):
                cols = pl.ds(pl.multiple_of(j * tile, tile), tile)
                g_down_ref[cols, :] = tdot(mixed_ref[:, cols], d_all[...]).astype(BF)

            down = pltpu.make_async_copy(g_down_ref, out.at[:, pl.ds(2 * ffq, dm)], sem_d.at[0])
            down.start()
            down.wait()

            @pl.loop(0, ndev)
            def _(block):
                store(block).wait()

        def ff_back_all(rk, *refs):
            ins, refs = list(refs[: nline + 7]), refs[nline + 7 :]
            parts, (g_su, g_sg, out) = refs[:nline], refs[nline : nline + 3]
            d_all, dug, wug, wd, s_u, s_d, g_ref, g_down_ref, sems, sem_d = refs[nline + 3 : nline + 13]
            *held, late_sems = refs[nline + 13 :]
            late = []
            for i, dst in enumerate(held):
                late.append(pltpu.make_async_copy(ins[nline + 3 + i], dst, late_sems.at[i]))
            ins[nline + 3 :] = held
            scratch = (d_all, dug, g_su, g_sg, wug, wd, s_u, s_d)
            ff_back(rk, late, *ins[: nline + 5], *parts, *scratch)
            h, mixed_ref = ins[nline + 5 :]
            for copy in late[2:]:
                copy.wait()
            outer_ff(rk, h, dug, mixed_ref, d_all, out, g_ref, g_down_ref, sems, sem_d)

        *one_parts, g_su, g_sg, g_ff = call(
            ff_back_all,
            part_shapes + [((1, ffq), F32)] * 2 + [((dm, 2 * ffq + dm), BF)],
            (ranks, *dm_got, ff_full, my_su, my_sg, up, gate, h_all, mixed),
            hbm=(1 + nline, 4 + nline, 5 + nline, 6 + nline, 7 + nline),
            hbm_out=(nline + 2,),
            scratch=[pltpu.VMEM((nt, dm), BF), pltpu.VMEM((nt, 2 * ffq), BF)]
            + w_scratch
            + [pltpu.VMEM((dm, 2 * ffq), BF), pltpu.VMEM((ffq, dm), BF)]
            + [pltpu.SemaphoreType.DMA((ndev,)), pltpu.SemaphoreType.DMA((1,))]
            + [pltpu.VMEM((nt, ffq), BF)] * 2
            + [pltpu.VMEM((nt, dm), BF), pltpu.VMEM((nt, ffq), BF)]
            + [pltpu.SemaphoreType.DMA((4,))],
            flops=12 * nt * dm * ffq,
        )
        one_got = exchange(one_parts, line, nline)
        g_ff = lax.psum_scatter(g_ff, dpc, scatter_dimension=0, tiled=True)
        def attn_update_back(rk, *refs):
            parts, refs = refs[:nline], refs[nline:]
            direct_in, one_ref, raw_ref, ext_ref, alpha_ref, stack = refs[:6]
            d_outs, (dh_ref, direct, g_alpha, w, sems) = refs[6 : 6 + nline], refs[6 + nline :]
            copies = load_out(rk, stack, w, sems)
            for copy in copies:
                copy.start()
            d = direct_in[...] + parts[0][...]
            for k in range(1, nline):
                d = d + parts[k][...].astype(F32)
            one, raw, alpha = one_ref[...], raw_ref[...], alpha_ref[...]
            x = own_x(ext_ref)
            norm_raw = row_norm(raw)
            b = raw * norm_raw
            gap = b - x
            norm_z = row_norm(x + alpha * gap)
            dz = sphere_back(d, one, norm_z)
            g_alpha[...] = jnp.sum(dz * gap, axis=0, keepdims=True)
            direct[...] = dz * (1.0 - alpha)
            dh_ref[...] = sphere_back(dz * alpha, b, norm_raw).astype(BF)
            for copy in copies:
                copy.wait()
            for k in range(nline):
                w_k = w[pl.ds(pl.multiple_of((rk[6] ^ k) * hc, hc), hc), :]
                d_outs[k][...] = dot_t(dh_ref[...], w_k).astype(BF)

        outs = call(
            attn_update_back,
            [((tk, hc), BF)] * nline + [((tk, dm), BF), full, ((1, dm), F32)],
            (ranks, *one_got, d_one_direct, h_one, h_attn, mine, alpha_a, ff_full),
            hbm=(6 + nline,),
            scratch=out_scratch,
            flops=2 * tk * dm * dm,
        )
        d_att_parts, (dh_low, d_x_direct, g_alpha_attn) = outs[:nline], outs[nline:]
        d_att = exchange(d_att_parts, line, nline)

        def attn_back(rk, late, *refs):
            d_refs, refs = refs[:nline], refs[nline:]
            w_ref, rq_ref, rk_ref, q_ref, k_ref, v_ref, bias_ref, cs_ref, gain = refs[:9]
            full_ref, inv_ref, refs = refs[9], refs[10], refs[11:]
            parts, (d_ref, g_gain, do_ref, dq_ref, dk_ref) = refs[:nline], refs[nline:]
            for k in range(nline):
                do_ref[k * tk : (k + 1) * tk, :] = d_refs[k][...]
            for h in range(nheads):
                at_h = slice(h * HEAD_DIM, (h + 1) * HEAD_DIM)
                q, key, do = q_ref[:, at_h], k_ref[:, at_h], do_ref[:, at_h]
                raw = jnp.exp(dot_t(q, key) + bias_ref[...].astype(F32))
                p = raw * inv_ref[:, h : h + 1]
                delta = jnp.sum(do.astype(F32) * full_ref[:, at_h], axis=1, keepdims=True)
                ds = (p * (dot_t(do, v_ref[:, at_h]) - delta)).astype(BF)
                p = p.astype(BF)
                at_v = slice(2 * hc + h * HEAD_DIM, 2 * hc + (h + 1) * HEAD_DIM)
                d_ref[:, at_v] = tdot(p, do).astype(BF)
                dq_ref[:, at_h] = scale * dot(ds, key)
                dk_ref[:, at_h] = tdot(ds, q)
            for copy in late:
                copy.wait()
            cs = cs_ref[...]
            cos = jnp.concatenate([cs[:, :128]] * (hc // 128), axis=1)
            sin = jnp.concatenate([cs[:, 128:]] * (hc // 128), axis=1)
            low = low_half()
            for i, (raw_ref, g_ref) in enumerate(((rq_ref, dq_ref), (rk_ref, dk_ref))):
                for h in range(nheads):
                    at_h = slice(h * HEAD_DIM, (h + 1) * HEAD_DIM)
                    turned, g = raw_ref[:, at_h], g_ref[:, at_h]
                    norm = lax.rsqrt(jnp.sum(turned * turned, axis=1, keepdims=True) + EPS)
                    unit = turned * norm
                    term = jnp.sum(g * unit, axis=0, keepdims=True)
                    g_gain[:, at_h] = term if i == 0 else g_gain[:, at_h] + term
                    g = g * gain[:, at_h]
                    g_ref[:, at_h] = norm * (g - unit * jnp.sum(unit * g, axis=1, keepdims=True))
                g = g_ref[...]
                d_ref[:, i * hc : (i + 1) * hc] = (g * cos - heads_swap(g, low) * sin).astype(BF)

            @pl.loop(0, dm // tile)
            def _(j):
                cols = pl.ds(pl.multiple_of(j * tile, tile), tile)
                part = dot_t(d_ref[...], w_ref[cols, :])
                for k in range(nline):
                    parts[k][:, cols] = part[k * tk : (k + 1) * tk].astype(parts[k].dtype)


        at_line = ranks[6]
        mine_ff = (jnp.arange(nline) == at_line)[None, :, None, None]

        def ff_owner(vec):
            return jnp.where(mine_ff, vec.reshape(nyx, 1, nc, ffb), 0.0).reshape(ndev, ffb)

        misc = [v.reshape(ndev, rows) for v in (g_alpha_attn, g_alpha_mlp)]
        misc = jnp.pad(jnp.concatenate(misc, axis=1), ((0, 0), (0, ffb - 2 * rows)))
        vecs = jnp.stack([ff_owner(g_su), ff_owner(g_sg), misc], axis=1).astype(BF)
        vecs = jnp.pad(vecs, ((0, 0), (0, rows - 3), (0, 0))).reshape(dm, ffb)

        wide = 3 * hc + ffb

        def outer_out(rk, dh, *refs):
            parts, outs, (g_ref, sems) = refs[:nline], refs[nline : nline + 2], refs[nline + 2 :]
            for k in range(nline):
                spot = pl.ds(pl.multiple_of((rk[6] ^ k) * hc, hc), hc)
                own = parts[k][k * tk : (k + 1) * tk, :]
                g_ref[spot, :] = tdot(own, dh[...]).astype(BF)
            copies = []
            for cr in range(nc):
                for a in range(nyx):
                    for b in range(nline):
                        row = ((rk[5] ^ a) * nline + (rk[6] ^ b)) * nc + (rk[4] ^ cr)
                        src = g_ref.at[pl.ds(pl.multiple_of(row * rows, 32), rows)]
                        dst = outs[cr].at[pl.ds((a * nline + b) * rows, rows)]
                        copies.append(pltpu.make_async_copy(src, dst, sems.at[len(copies)]))
            for copy in copies:
                copy.start()
            for copy in copies:
                copy.wait()

        keep, send = call(
            outer_out,
            [((dm // nc, dm), BF)] * nc,
            (ranks, dh_low, *att_got),
            hbm_out=(0, 1),
            scratch=[pltpu.VMEM((dm, dm), BF), pltpu.SemaphoreType.DMA((ndev,))],
            flops=2 * tk * dm * dm,
        )

        def core_add(rk, a, b, *outs):
            for i in range(nyx):
                here = slice(i * ffb, (i + 1) * ffb)
                outs[i][...] = (a[here, :].astype(F32) + b[here, :].astype(F32)).astype(BF)

        out_sum = call(
            core_add, [((ffb, dm), BF)] * nyx, (ranks, keep, swap(send, "c", nc, 1))
        )
        out_got = exchange(out_sum, yx, nyx)

        def outer_last(rk, x_ref, d_ref, vec_ref, g_gain, out, g_ref, sems):

            def store(block):
                return stored(rk, g_ref, out, wide, block, sems)

            g_ref[:, 3 * hc : wide] = vec_ref[...]
            third = lax.broadcasted_iota(jnp.int32, (16, ffb), 0) == 2
            for i in range(hc // rows):
                spot = pl.ds(pl.multiple_of((rk[6] * (hc // rows) + i) * rows, 32), 16)
                run = [jnp.zeros((1, 2 * rows), F32), g_gain[:, i * rows : (i + 1) * rows]]
                run = jnp.concatenate(run + [jnp.zeros((1, ffb - 3 * rows), F32)], axis=1)
                held = g_ref[spot, 3 * hc : wide].astype(F32)
                g_ref[spot, 3 * hc : wide] = (held + jnp.where(third, run, 0.0)).astype(BF)

            @pl.loop(0, dm // tile)
            def _(j):
                cols = pl.ds(pl.multiple_of(j * tile, tile), tile)
                g_ref[cols, : 3 * hc] = tdot(x_ref[:, cols], d_ref[...]).astype(BF)
                for i in range(tile // rows):
                    store(j * (tile // rows) + i).start()

            @pl.loop(0, ndev)
            def _(block):
                store(block).wait()

        def attn_back_all(rk, *refs):
            ins, refs = list(refs[: nline + 13]), refs[nline + 13 :]
            parts, out = refs[:nline], refs[nline]
            d_ref, g_gain, do_ref, dq_ref, dk_ref, g_ref, sems = refs[nline + 1 : nline + 8]
            *held, late_sems = refs[nline + 8 :]
            late = []
            for i, (at_in, dst) in enumerate(zip(late_back, held)):
                late.append(pltpu.make_async_copy(ins[at_in - 1], dst, late_sems.at[i]))
                ins[at_in - 1] = dst
            for copy in late:
                copy.start()
            x_ref, vec_ref = ins[nline + 11 :]
            scratch = (d_ref, g_gain, do_ref, dq_ref, dk_ref)
            attn_back(rk, late, *ins[: nline + 11], *parts, *scratch)
            outer_last(rk, x_ref, d_ref, vec_ref, g_gain, out, g_ref, sems)

        late_back = [1 + nline, 2 + nline, 3 + nline, 8 + nline, 12 + nline]
        late_shapes = [((dm, 3 * hc), BF), ((nt, hc), F32), ((nt, hc), F32), ((nt, 256), F32)]
        late_shapes.append(((nt, dm), BF))

        *x_parts, g_last = call(
            attn_back_all,
            part_shapes + [((dm, wide), BF)],
            (ranks, *d_att, w_qkv, r_q, r_k, q_low, k_low, v_low, bias, cs, my_gain, att_full, inv)
            + (x_all, vecs),
            hbm=late_back,
            hbm_out=(nline,),
            scratch=[
                pltpu.VMEM((nt, 3 * hc), BF), pltpu.VMEM((1, hc), F32),
                pltpu.VMEM((nt, hc), BF), pltpu.VMEM((nt, hc), F32), pltpu.VMEM((nt, hc), F32),
                pltpu.VMEM((dm, wide), BF), pltpu.SemaphoreType.DMA((ndev,)),
                *[pltpu.VMEM(*shape) for shape in late_shapes], pltpu.SemaphoreType.DMA((5,)),
            ],
            flops=4 * nt * dm * 3 * hc + 10 * nt * nt * hc,
        )
        x_got = exchange(x_parts, line, nline)

        def finish_tokens(rk, *refs):
            parts, (direct, keep, send) = refs[:nline], refs[nline:]
            d = direct[...] + parts[0][...]
            for k in range(1, nline):
                d = d + parts[k][...].astype(F32)
            keep[...] = d[:seg]
            send[...] = d[seg:].astype(BF)

        x_keep, x_send = call(
            finish_tokens, [((seg, dm), F32), half_low], (ranks, *x_got, d_x_direct)
        )
        x_recv = swap(x_send, "c", nc, 1)

        def join_rows(rk, keep, recv, out):
            out[rk[4]] = keep[...].astype(out.dtype)
            out[1 - rk[4]] = recv[...].astype(out.dtype)

        (tokens_grad,) = call(join_rows, [((nseq, seg, dm), F32)], (ranks, x_keep, x_recv))
        (hidden_out,) = call(join_rows, [((nseq, seg, dm), BF)], (ranks, hid_keep, hid_recv))

        g_last = lax.psum_scatter(g_last, dpc, scatter_dimension=0, tiled=True)

        def split_ff(rk, g_ref, down, *outs):
            down[...] = g_ref[:, 2 * ffq :].astype(F32)
            for k in range(nline):
                outs[k][...] = g_ref[k * rows : (k + 1) * rows, : 2 * ffq]

        g_down, *g_parts = call(
            split_ff,
            [((ffb, dm), F32)] + [((rows, 2 * ffq), BF)] * nline,
            (ranks, g_ff),
            after=tuple(x_got[1:]),
        )
        g_parts = exchange(g_parts, line, nline)

        def place_ff(rk, *refs):
            parts, outs = refs[:nline], refs[nline:]
            for k in range(nline):
                for d, cols in enumerate(ff_cols(rk, k)):
                    for i in range(2):
                        here = i * ffq + d * sub
                        outs[i][:, cols] = parts[k][:, here : here + sub].astype(F32)

        g_up, g_gate = call(place_ff, [((rows, ff), F32)] * 2, (ranks, *g_parts))

        def sum_out(rk, *refs):
            parts, outs = refs[:nyx], refs[nyx:]
            for k in range(nline):
                here = slice(k * rows, (k + 1) * rows)
                total = parts[0][here, :].astype(F32)
                for j in range(1, nyx):
                    total = total + parts[j][here, :].astype(F32)
                outs[k][...] = total.astype(BF)

        out_sum = call(sum_out, [((rows, dm), BF)] * nline, (ranks, *out_got))
        out_got = exchange(out_sum, line, nline)

        def split_last(rk, g_ref, *outs):
            for k in range(nline):
                outs[k][...] = g_ref[k * rows : (k + 1) * rows, :]

        last = call(
            split_last,
            [((rows, wide), BF)] * nline,
            (ranks, g_last),
            after=(g_up, *out_got[1:]),
        )
        last = exchange(last, line, nline)

        def place_last(rk, *refs):
            parts, out_parts = refs[:nline], refs[nline : 2 * nline]
            outs, refs = refs[2 * nline : 2 * nline + 3], refs[2 * nline + 3 :]
            g_o, vec_outs = refs[0], refs[1:]
            g_sum, v_sum = None, None
            for k in range(nline):
                cols = pl.ds(pl.multiple_of((rk[6] ^ k) * hc, 128), hc)
                for i in range(3):
                    outs[i][:, cols] = parts[k][:, i * hc : (i + 1) * hc].astype(F32)
                vec = parts[k][:16, 3 * hc : wide].astype(F32)
                part = out_parts[k][...].astype(F32)
                g_sum = part if g_sum is None else g_sum + part
                v_sum = vec if v_sum is None else v_sum + vec
            g_o[...] = g_sum
            vec_outs[0][...] = v_sum[:1]
            vec_outs[1][...] = v_sum[1:2]
            for i in range(3):
                vec_outs[2 + i][...] = v_sum[2:3, i * rows : (i + 1) * rows]

        g_query, g_key, g_value, g_out, *vecs = call(
            place_last,
            [((rows, dm), F32)] * 4
            + [((1, ffb), F32)] * 2
            + [((1, rows), F32)] * 3,
            (ranks, *last, *out_got),
        )
        g_s_up, g_s_gate, g_aa, g_am, g_sqk = [v.reshape(-1) for v in vecs]
        return (
            hidden_out, tokens_grad, g_query, g_key, g_value, g_out, g_up, g_gate, g_down,
            g_sqk, g_aa, g_s_up, g_s_gate, g_am,
        )

    return body


def make_body(sizes):
    plain, kernels = make_plain(sizes), make_kernels(sizes)
    ndev = math.prod(sizes)
    nline = sizes[2] * sizes[3]

    def body(*args):
        tokens, w_query, w_up = args[0], args[2], args[6]
        fits = w_query.shape[0] % 32 == 0 and (w_up.shape[1] // ndev) % 128 == 0
        fits = fits and (tokens.shape[2] // nline) % 256 == 0 and tokens.shape[1] == 64
        return (kernels if fits else plain)(*args)

    return body


def solution(mesh):
    ndp, nblk = mesh.shape["dp"], mesh.shape["blk"]
    sizes = (ndp // 2, 2, nblk // 4, 2, 2)
    fine = Mesh(mesh.devices.reshape(sizes), ("y", "x", "w", "z", "c"))
    rows, cols = ("y", "x"), ("w", "z", "c")
    flat = rows + cols
    seq = P(rows, cols, None)
    weight = P(flat, None)
    return jax.shard_map(
        make_body(sizes),
        mesh=fine,
        in_specs=(seq, P(rows, cols)) + (weight,) * 7 + (P(),) * 5 + (seq,),
        out_specs=(seq, seq) + (weight,) * 7 + (P(flat),) * 5,
        check_vma=False,
    )
```

profile of v0, /device:TPU:0, one launch (start us, length us, event | category | flops | bytes accessed | tf_op | source)
XLA Modules:
  0.0 328.4 jit_solution(8143864938689854154)
XLA Ops:
  9.6 3.0 collective-permute-start.4
  12.7 2.6 collective-permute-start.5
  15.3 3.5 %collective-permute-done.5.refs_3_ = bf16[32,768]{1,0:T(8,128)(2,1)S(1)} collective-permute-done((bf16[32,768]{1,0:T(8,128)(2,1)}, bf16[32,768]{1,0:T(8,128)(2,1)S(1)}, u32[]{:S(2)}, u32[]{:S(2)}) %collective-permute-start.5) | collective-permute-done | bytes 49184 | tf_op jit(solution)/shard_map/ppermute | solution.py:366
  30.2 3.1 collective-permute-start.12
  38.0 7.3 %collective-permute-done.11.refs_3_ = bf16[32,3072]{1,0:T(8,128)(2,1)S(1)} collective-permute-done((bf16[32,3072]{1,0:T(8,128)(2,1)}, bf16[32,3072]{1,0:T(8,128)(2,1)S(1)}, u32[]{:S(2)}, u32[]{:S(2)}) %collective-permute-start.11) | collective-permute-done | bytes 196640 | tf_op jit(solution)/shard_map/ppermute | solution.py:366
  48.7 3.0 collective-permute-start.1
  57.0 5.3 %collective-permute-done.1.refs_2_ = bf16[144,1024]{1,0:T(8,128)(2,1)S(1)} collective-permute-done((bf16[144,1024]{1,0:T(8,128)(2,1)S(1)}, bf16[144,1024]{1,0:T(8,128)(2,1)S(1)}, u32[]{:S(2)}, u32[]{:S(2)}) %collective-permute-start.1) | collective-permute-done | bytes 294944 | tf_op jit(solution)/shard_map/ppermute | solution.py:366
  62.3 12.3 %collective-permute-done.2.refs_3_ = bf16[144,1024]{1,0:T(8,128)(2,1)S(1)} collective-permute-done((bf16[144,1024]{1,0:T(8,128)(2,1)S(1)}, bf16[144,1024]{1,0:T(8,128)(2,1)S(1)}, u32[]{:S(2)}, u32[]{:S(2)}) %collective-permute-start.2) | collective-permute-done | bytes 294944 | tf_op jit(solution)/shard_map/ppermute | solution.py:366
  75.3 9.1 %shard_map.259 = (bf16[512,256]{1,0:T(8,128)(2,1)}, bf16[512,1024]{1,0:T(8,128)(2,1)}, bf16[1024,768]{1,0:T(8,128)(2,1)}, f32[512,256]{1,0:T(8,128)}, f32[512,25...) custom-call(s32[7]{0:T(128)} %stack.39.refs_0_, ...), custom_call_target="tpu_custom_call" | custom-call | flops 1073741824 | bytes 9831452 | tf_op jit(solution)/shard_map/pallas_call | solution.py:339
  84.5 4.3 %collective-permute-start.7 = (bf16[512,256]{1,0:T(8,128)(2,1)}, bf16[512,256]{1,0:T(8,128)(2,1)S(1)}, u32[]{:S(2)}, u32[]{:S(2)}) collective-permute-start(bf16[512,256]{1,0:T(8,128)(2,1)} %get-tuple-element.114.refs_1_.refs_2_), channel_id=1, source_target_pairs={{0,2},{2,0},{4,6},{6,4},{1,3},{3,1},{5,7},{7,5},{8,10},{10,8},{12,... | collective-permute-start | bytes 786440 | tf_op jit(solution)/shard_map/ppermute | solution.py:366
  91.2 7.0 %collective-permute-done.7.refs_2_.refs_3_ = bf16[512,256]{1,0:T(8,128)(2,1)S(1)} collective-permute-done((bf16[512,256]{1,0:T(8,128)(2,1)}, bf16[512,256]{1,0:T(8,128)(2,1)S(1)}, u32[]{:S(2)}, u32[]{:S(2)}) %collective-permute-start.7) | collective-permute-done | bytes 262176 | tf_op jit(solution)/shard_map/ppermute | solution.py:366
  98.2 10.3 %collective-permute-done.8.refs_3_.refs_4_ = bf16[512,256]{1,0:T(8,128)(2,1)S(1)} collective-permute-done((bf16[512,256]{1,0:T(8,128)(2,1)}, bf16[512,256]{1,0:T(8,128)(2,1)S(1)}, u32[]{:S(2)}, u32[]{:S(2)}) %collective-permute-start.8) | collective-permute-done | bytes 262176 | tf_op jit(solution)/shard_map/ppermute | solution.py:366
  109.3 12.2 %shard_map.261 = (f32[128,1024]{1,0:T(8,128)}, bf16[128,1024]{1,0:T(8,128)(2,1)}, bf16[128,1024]{1,0:T(8,128)(2,1)}, bf16[128,1024]{1,0:T(8,128)(2,1)}, bf16[512...) custom-call(s32[7]{0:T(128)} %stack.39.refs_0_, ...), custom_call_target="tpu_custom_call" | custom-call | flops 4294967296 | bytes 17051676 | tf_op jit(solution)/shard_map/pallas_call | solution.py:339
  121.5 5.1 %collective-permute-start.13 = (bf16[128,1024]{1,0:T(8,128)(2,1)}, bf16[128,1024]{1,0:T(8,128)(2,1)S(1)}, u32[]{:S(2)}, u32[]{:S(2)}) collective-permute-start(bf16[128,1024]{1,0:T(8,128)(2,1)} %get-tuple-element.123), channel_id=1, source_target_pairs={{0,2},{2,0},{4,6},{6,4},{1,3},{3,1},{5,7},{7,5},{8,10},{10,8},{12,... | collective-permute-start | bytes 786440 | tf_op jit(solution)/shard_map/ppermute | solution.py:366
  132.3 3.7 %collective-permute-done.13.refs_2_ = bf16[128,1024]{1,0:T(8,128)(2,1)S(1)} collective-permute-done((bf16[128,1024]{1,0:T(8,128)(2,1)}, bf16[128,1024]{1,0:T(8,128)(2,1)S(1)}, u32[]{:S(2)}, u32[]{:S(2)}) %collective-permute-start.13) | collective-permute-done | bytes 262176 | tf_op jit(solution)/shard_map/ppermute | solution.py:366
  136.0 12.0 %collective-permute-done.14.refs_3_ = bf16[128,1024]{1,0:T(8,128)(2,1)S(1)} collective-permute-done((bf16[128,1024]{1,0:T(8,128)(2,1)}, bf16[128,1024]{1,0:T(8,128)(2,1)S(1)}, u32[]{:S(2)}, u32[]{:S(2)}) %collective-permute-start.14) | collective-permute-done | bytes 262176 | tf_op jit(solution)/shard_map/ppermute | solution.py:366
  148.8 2.9 shard_map.263
  151.7 4.2 %collective-permute-start.18 = (bf16[128,1024]{1,0:T(8,128)(2,1)}, bf16[128,1024]{1,0:T(8,128)(2,1)S(1)}, u32[]{:S(2)}, u32[]{:S(2)}) collective-permute-start(bf16[128,1024]{1,0:T(8,128)(2,1)} %get-tuple-element.131.refs_1_), channel_id=1, source_target_pairs={{0,2},{2,0},{4,6},{6,4},{1,3},{3,1},{5,7},{7,5},{8,10},{10,8},{12,... | collective-permute-start | bytes 786440 | tf_op jit(solution)/shard_map/ppermute | solution.py:366
  158.3 6.5 %collective-permute-done.18.refs_2_ = bf16[128,1024]{1,0:T(8,128)(2,1)S(1)} collective-permute-done((bf16[128,1024]{1,0:T(8,128)(2,1)}, bf16[128,1024]{1,0:T(8,128)(2,1)S(1)}, u32[]{:S(2)}, u32[]{:S(2)}) %collective-permute-start.18) | collective-permute-done | bytes 262176 | tf_op jit(solution)/shard_map/ppermute | solution.py:366
  164.8 11.5 %collective-permute-done.19.refs_3_ = bf16[128,1024]{1,0:T(8,128)(2,1)S(1)} collective-permute-done((bf16[128,1024]{1,0:T(8,128)(2,1)}, bf16[128,1024]{1,0:T(8,128)(2,1)S(1)}, u32[]{:S(2)}, u32[]{:S(2)}) %collective-permute-start.19) | collective-permute-done | bytes 262176 | tf_op jit(solution)/shard_map/ppermute | solution.py:366
  177.1 17.8 %shard_map.265 = (f32[128,1024]{1,0:T(8,128)}, bf16[128,1024]{1,0:T(8,128)(2,1)}, bf16[128,1024]{1,0:T(8,128)(2,1)}, bf16[128,1024]{1,0:T(8,128)(2,1)}, f32[1,10...) custom-call(s32[7]{0:T(128)} %stack.39.refs_0_, bf16[128,1024]{1,0:T(8,128)(2,1)} %get-tuple-element.131.refs_1_, ...), custom_call_target="tpu_custom_call" | custom-call | flops 6442450944 | bytes 21250076 | tf_op jit(solution)/shard_map/pallas_call | solution.py:339
  195.9 4.2 %collective-permute-start.21 = (bf16[128,1024]{1,0:T(8,128)(2,1)S(1)}, bf16[128,1024]{1,0:T(8,128)(2,1)S(1)}, u32[]{:S(2)}, u32[]{:S(2)}) collective-permute-start(bf16[128,1024]{1,0:T(8,128)(2,1)S(1)} %copy-done.47), channel_id=1, source_target_pairs={{0,2},{2,0},{4,6},{6,4},{1,3},{3,1},{5,7},{7,5},{8,10},{10,8},{12,... | collective-permute-start | bytes 786440 | tf_op jit(solution)/shard_map/ppermute | solution.py:366
  202.7 6.0 %collective-permute-done.21.refs_2_ = bf16[128,1024]{1,0:T(8,128)(2,1)S(1)} collective-permute-done((bf16[128,1024]{1,0:T(8,128)(2,1)S(1)}, bf16[128,1024]{1,0:T(8,128)(2,1)S(1)}, u32[]{:S(2)}, u32[]{:S(2)}) %collective-permute-start.21) | collective-permute-done | bytes 262176 | tf_op jit(solution)/shard_map/ppermute | solution.py:366
  208.7 11.5 %collective-permute-done.22.refs_3_ = bf16[128,1024]{1,0:T(8,128)(2,1)S(1)} collective-permute-done((bf16[128,1024]{1,0:T(8,128)(2,1)S(1)}, bf16[128,1024]{1,0:T(8,128)(2,1)S(1)}, u32[]{:S(2)}, u32[]{:S(2)}) %collective-permute-start.22) | collective-permute-done | bytes 262176 | tf_op jit(solution)/shard_map/ppermute | solution.py:366
  221.0 5.4 %shard_map.266 = (bf16[128,256]{1,0:T(8,128)(2,1)}, bf16[128,256]{1,0:T(8,128)(2,1)}, bf16[128,256]{1,0:T(8,128)(2,1)}, bf16[128,256]{1,0:T(8,128)(2,1)}, bf16[1...) custom-call(s32[7]{0:T(128)} %stack.39.refs_0_, f32[128,1024]{1,0:T(8,128)} %get-tuple-element.136.refs_1_, ...), custom_call_target="tpu_custom_call" | custom-call | flops 268435456 | bytes 12623900 | tf_op jit(solution)/shard_map/pallas_call | solution.py:339
  227.2 4.0 %collective-permute-start.24 = (bf16[128,256]{1,0:T(8,128)(2,1)}, bf16[128,256]{1,0:T(8,128)(2,1)S(1)}, u32[]{:S(2)}, u32[]{:S(2)}) collective-permute-start(bf16[128,256]{1,0:T(8,128)(2,1)} %get-tuple-element.143), channel_id=1, source_target_pairs={{0,2},{2,0},{4,6},{6,4},{1,3},{3,1},{5,7},{7,5},{8,10},{10,8},{12,... | collective-permute-start | bytes 196616 | tf_op jit(solution)/shard_map/ppermute | solution.py:366
  238.3 14.7 %shard_map.267 = (f32[128,1024]{1,0:T(8,128)}, bf16[128,1024]{1,0:T(8,128)(2,1)}, bf16[128,1024]{1,0:T(8,128)(2,1)}, bf16[128,1024]{1,0:T(8,128)(2,1)}, bf16[1024,896]{1,0:T(8,128)(2,1)}) custom-call(s32[7]{0:T(128)} %stack.39.refs_0_, bf16[128,256]{1,0:T(8,128)(2,1)} %get-tuple-element.142.refs_1_, bf16[128,256]{1,0:T(8,128)(2,1)} %copy-done.52, ...), custom_call_target="tpu_custom_call" | custom-call | flops 2281701376 | bytes 9962524 | tf_op jit(solution)/shard_map/pallas_call | solution.py:339
  253.0 3.7 %shard_map.272 = (bf16[512,1024]{1,0:T(8,128)(2,1)}, bf16[512,1024]{1,0:T(8,128)(2,1)}) custom-call(s32[7]{0:T(128)} %stack.39.refs_0_, bf16[128,1024]{1,0:T(8,128)(2,1)} %get-tuple-element.174.refs_1_, bf16[512,256]{1,0:T(8,128)(2,1)} %get-tuple-element.114.refs_1_.refs_2_, bf16[512,256]{1,0:T(8,128)(2,1)} %copy-done.5, bf16[512,256]{1,0:T(8,128)(2,1)} %copy-done.6, ...), custom_call_target="tpu_custom_call" | custom-call | flops 268435456 | bytes 3407900 | tf_op jit(solution)/shard_map/pallas_call | solution.py:339
  272.9 6.6 %collective-permute-done.28.refs_3_ = bf16[128,1024]{1,0:T(8,128)(2,1)S(1)} collective-permute-done((bf16[128,1024]{1,0:T(8,128)(2,1)S(1)}, bf16[128,1024]{1,0:T(8,128)(2,1)S(1)}, u32[]{:S(2)}, u32[]{:S(2)}) %collective-permute-start.28) | collective-permute-done | bytes 262176 | tf_op jit(solution)/shard_map/ppermute | solution.py:366
  282.3 5.3 %collective-permute-start.31 = (bf16[32,2048]{1,0:T(8,128)(2,1)}, bf16[32,2048]{1,0:T(8,128)(2,1)S(1)}, u32[]{:S(2)}, u32[]{:S(2)}) collective-permute-start(bf16[32,2048]{1,0:T(8,128)(2,1)} %get-tuple-element.170), channel_id=1, source_target_pairs={{0,2},{2,0},{4,6},{6,4},{1,3},{3,1},{5,7},{7,5},{8,10},{10,8},{12,... | collective-permute-start | bytes 393224 | tf_op jit(solution)/shard_map/ppermute | solution.py:366
  296.2 4.0 %collective-permute-done.32.refs_3_ = bf16[32,2048]{1,0:T(8,128)(2,1)S(1)} collective-permute-done((bf16[32,2048]{1,0:T(8,128)(2,1)}, bf16[32,2048]{1,0:T(8,128)(2,1)S(1)}, u32[]{:S(2)}, u32[]{:S(2)}) %collective-permute-start.32) | collective-permute-done | bytes 131104 | tf_op jit(solution)/shard_map/ppermute | solution.py:366
  308.8 3.3 collective-permute-start.41
  (223 shorter events, 99.0 us)
Async XLA Ops:
  7.2 67.4 %all-gather.3.cloned.1.call-start = ((), (), s32[]{:S(2)}) async-start(), calls=%async_computation.2 | async-start | bytes 1769472 | tf_op jit(solution)/shard_map/all_gather | solution.py:461
  23.6 85.0 %all-gather.5.cloned.1.call-start = ((), (), s32[]{:S(2)}) async-start(), calls=%async_computation.3 | async-start | bytes 9437184 | tf_op jit(solution)/shard_map/all_gather | solution.py:475
  28.9 16.4 %collective-permute-start.11 = (bf16[32,3072]{1,0:T(8,128)(2,1)}, bf16[32,3072]{1,0:T(8,128)(2,1)S(1)}, u32[]{:S(2)}, u32[]{:S(2)}) collective-permute-start(bf16[32,3072]{1,0:T(8,128)(2,1)} %get-tuple-element.118), channel_id=1, source_target_pairs={{0,4},{2,6},{4,0},{6,2},{1,5},{3,7},{5,1},{7,3},{8,12},{10,14},{12... | collective-permute-start | bytes 589832 | tf_op jit(solution)/shard_map/ppermute | solution.py:366
  30.2 15.1 %collective-permute-start.12 = (bf16[32,3072]{1,0:T(8,128)(2,1)}, bf16[32,3072]{1,0:T(8,128)(2,1)S(1)}, u32[]{:S(2)}, u32[]{:S(2)}) collective-permute-start(bf16[32,3072]{1,0:T(8,128)(2,1)} %get-tuple-element.119), channel_id=1, source_target_pairs={{0,6},{2,4},{4,2},{6,0},{1,7},{3,5},{5,3},{7,1},{8,14},{10,12},{12... | collective-permute-start | bytes 589832 | tf_op jit(solution)/shard_map/ppermute | solution.py:366
  48.6 230.8 %reduce-scatter.5.cloned.1.call-start = ((), (), s32[]{:S(2)}) async-start(), calls=%async_computation.5 | async-start | bytes 7077888 | tf_op jit(solution)/shard_map/reduce_scatter | solution.py:815
  48.7 13.6 %collective-permute-start.1 = (bf16[144,1024]{1,0:T(8,128)(2,1)S(1)}, bf16[144,1024]{1,0:T(8,128)(2,1)S(1)}, u32[]{:S(2)}, u32[]{:S(2)}) collective-permute-start(bf16[144,1024]{1,0:T(8,128)(2,1)S(1)} %copy-done), channel_id=1, source_target_pairs={{0,2},{2,0},{4,6},{6,4},{1,3},{3,1},{5,7},{7,5},{8,10},{10,8},{12,... | collective-permute-start | bytes 884744 | tf_op jit(solution)/shard_map/ppermute | solution.py:366
  51.7 22.8 %collective-permute-start.2 = (bf16[144,1024]{1,0:T(8,128)(2,1)S(1)}, bf16[144,1024]{1,0:T(8,128)(2,1)S(1)}, u32[]{:S(2)}, u32[]{:S(2)}) collective-permute-start(bf16[144,1024]{1,0:T(8,128)(2,1)S(1)} %copy-done), channel_id=1, source_target_pairs={{0,4},{2,6},{4,0},{6,2},{1,5},{3,7},{5,1},{7,3},{8,12},{10,14},{12... | collective-permute-start | bytes 884744 | tf_op jit(solution)/shard_map/ppermute | solution.py:366
  51.7 22.8 %collective-permute-start.3 = (bf16[144,1024]{1,0:T(8,128)(2,1)S(1)}, bf16[144,1024]{1,0:T(8,128)(2,1)S(1)}, u32[]{:S(2)}, u32[]{:S(2)}) collective-permute-start(bf16[144,1024]{1,0:T(8,128)(2,1)S(1)} %copy-done), channel_id=1, source_target_pairs={{0,6},{2,4},{4,2},{6,0},{1,7},{3,5},{5,3},{7,1},{8,14},{10,12},{12... | collective-permute-start | bytes 884744 | tf_op jit(solution)/shard_map/ppermute | solution.py:366
  84.5 13.7 %collective-permute-start.7 = (bf16[512,256]{1,0:T(8,128)(2,1)}, bf16[512,256]{1,0:T(8,128)(2,1)S(1)}, u32[]{:S(2)}, u32[]{:S(2)}) collective-permute-start(bf16[512,256]{1,0:T(8,128)(2,1)} %get-tuple-element.114.refs_1_.refs_2_), channel_id=1, source_target_pairs={{0,2},{2,0},{4,6},{6,4},{1,3},{3,1},{5,7},{7,5},{8,10},{10,8},{12,... | collective-permute-start | bytes 786440 | tf_op jit(solution)/shard_map/ppermute | solution.py:366
  88.8 19.8 %collective-permute-start.8 = (bf16[512,256]{1,0:T(8,128)(2,1)}, bf16[512,256]{1,0:T(8,128)(2,1)S(1)}, u32[]{:S(2)}, u32[]{:S(2)}) collective-permute-start(bf16[512,256]{1,0:T(8,128)(2,1)} %get-tuple-element.114.refs_1_.refs_2_), channel_id=1, source_target_pairs={{0,4},{2,6},{4,0},{6,2},{1,5},{3,7},{5,1},{7,3},{8,12},{10,14},{12... | collective-permute-start | bytes 786440 | tf_op jit(solution)/shard_map/ppermute | solution.py:366
  88.8 19.8 %collective-permute-start.9 = (bf16[512,256]{1,0:T(8,128)(2,1)}, bf16[512,256]{1,0:T(8,128)(2,1)S(1)}, u32[]{:S(2)}, u32[]{:S(2)}) collective-permute-start(bf16[512,256]{1,0:T(8,128)(2,1)} %get-tuple-element.114.refs_1_.refs_2_), channel_id=1, source_target_pairs={{0,6},{2,4},{4,2},{6,0},{1,7},{3,5},{5,3},{7,1},{8,14},{10,12},{12... | collective-permute-start | bytes 786440 | tf_op jit(solution)/shard_map/ppermute | solution.py:366
  121.5 14.5 %collective-permute-start.13 = (bf16[128,1024]{1,0:T(8,128)(2,1)}, bf16[128,1024]{1,0:T(8,128)(2,1)S(1)}, u32[]{:S(2)}, u32[]{:S(2)}) collective-permute-start(bf16[128,1024]{1,0:T(8,128)(2,1)} %get-tuple-element.123), channel_id=1, source_target_pairs={{0,2},{2,0},{4,6},{6,4},{1,3},{3,1},{5,7},{7,5},{8,10},{10,8},{12,... | collective-permute-start | bytes 786440 | tf_op jit(solution)/shard_map/ppermute | solution.py:366
  126.6 21.3 %collective-permute-start.14 = (bf16[128,1024]{1,0:T(8,128)(2,1)}, bf16[128,1024]{1,0:T(8,128)(2,1)S(1)}, u32[]{:S(2)}, u32[]{:S(2)}) collective-permute-start(bf16[128,1024]{1,0:T(8,128)(2,1)} %get-tuple-element.124), channel_id=1, source_target_pairs={{0,4},{2,6},{4,0},{6,2},{1,5},{3,7},{5,1},{7,3},{8,12},{10,14},{12... | collective-permute-start | bytes 786440 | tf_op jit(solution)/shard_map/ppermute | solution.py:366
  126.6 21.3 %collective-permute-start.15 = (bf16[128,1024]{1,0:T(8,128)(2,1)}, bf16[128,1024]{1,0:T(8,128)(2,1)S(1)}, u32[]{:S(2)}, u32[]{:S(2)}) collective-permute-start(bf16[128,1024]{1,0:T(8,128)(2,1)} %get-tuple-element.125), channel_id=1, source_target_pairs={{0,6},{2,4},{4,2},{6,0},{1,7},{3,5},{5,3},{7,1},{8,14},{10,12},{12... | collective-permute-start | bytes 786440 | tf_op jit(solution)/shard_map/ppermute | solution.py:366
  151.7 13.1 %collective-permute-start.18 = (bf16[128,1024]{1,0:T(8,128)(2,1)}, bf16[128,1024]{1,0:T(8,128)(2,1)S(1)}, u32[]{:S(2)}, u32[]{:S(2)}) collective-permute-start(bf16[128,1024]{1,0:T(8,128)(2,1)} %get-tuple-element.131.refs_1_), channel_id=1, source_target_pairs={{0,2},{2,0},{4,6},{6,4},{1,3},{3,1},{5,7},{7,5},{8,10},{10,8},{12,... | collective-permute-start | bytes 786440 | tf_op jit(solution)/shard_map/ppermute | solution.py:366
  155.9 20.4 %collective-permute-start.19 = (bf16[128,1024]{1,0:T(8,128)(2,1)}, bf16[128,1024]{1,0:T(8,128)(2,1)S(1)}, u32[]{:S(2)}, u32[]{:S(2)}) collective-permute-start(bf16[128,1024]{1,0:T(8,128)(2,1)} %get-tuple-element.131.refs_1_), channel_id=1, source_target_pairs={{0,4},{2,6},{4,0},{6,2},{1,5},{3,7},{5,1},{7,3},{8,12},{10,14},{12... | collective-permute-start | bytes 786440 | tf_op jit(solution)/shard_map/ppermute | solution.py:366
  155.9 20.4 %collective-permute-start.20 = (bf16[128,1024]{1,0:T(8,128)(2,1)}, bf16[128,1024]{1,0:T(8,128)(2,1)S(1)}, u32[]{:S(2)}, u32[]{:S(2)}) collective-permute-start(bf16[128,1024]{1,0:T(8,128)(2,1)} %get-tuple-element.131.refs_1_), channel_id=1, source_target_pairs={{0,6},{2,4},{4,2},{6,0},{1,7},{3,5},{5,3},{7,1},{8,14},{10,12},{12... | collective-permute-start | bytes 786440 | tf_op jit(solution)/shard_map/ppermute | solution.py:366
  195.0 111.6 %reduce-scatter.3.cloned.1.call-start = ((), (), s32[]{:S(2)}) async-start(), calls=%async_computation.4 | async-start | bytes 2064384 | tf_op jit(solution)/shard_map/reduce_scatter | solution.py:1032
  195.9 12.8 %collective-permute-start.21 = (bf16[128,1024]{1,0:T(8,128)(2,1)S(1)}, bf16[128,1024]{1,0:T(8,128)(2,1)S(1)}, u32[]{:S(2)}, u32[]{:S(2)}) collective-permute-start(bf16[128,1024]{1,0:T(8,128)(2,1)S(1)} %copy-done.47), channel_id=1, source_target_pairs={{0,2},{2,0},{4,6},{6,4},{1,3},{3,1},{5,7},{7,5},{8,10},{10,8},{12,... | collective-permute-start | bytes 786440 | tf_op jit(solution)/shard_map/ppermute | solution.py:366
  200.0 20.2 %collective-permute-start.22 = (bf16[128,1024]{1,0:T(8,128)(2,1)S(1)}, bf16[128,1024]{1,0:T(8,128)(2,1)S(1)}, u32[]{:S(2)}, u32[]{:S(2)}) collective-permute-start(bf16[128,1024]{1,0:T(8,128)(2,1)S(1)} %copy-done.46), channel_id=1, source_target_pairs={{0,4},{2,6},{4,0},{6,2},{1,5},{3,7},{5,1},{7,3},{8,12},{10,14},{12... | collective-permute-start | bytes 786440 | tf_op jit(solution)/shard_map/ppermute | solution.py:366
  200.0 20.1 %collective-permute-start.23 = (bf16[128,1024]{1,0:T(8,128)(2,1)S(1)}, bf16[128,1024]{1,0:T(8,128)(2,1)S(1)}, u32[]{:S(2)}, u32[]{:S(2)}) collective-permute-start(bf16[128,1024]{1,0:T(8,128)(2,1)S(1)} %copy-done.45), channel_id=1, source_target_pairs={{0,6},{2,4},{4,2},{6,0},{1,7},{3,5},{5,3},{7,1},{8,14},{10,12},{12... | collective-permute-start | bytes 786440 | tf_op jit(solution)/shard_map/ppermute | solution.py:366
  256.8 13.6 %collective-permute-start.27 = (bf16[128,1024]{1,0:T(8,128)(2,1)S(1)}, bf16[128,1024]{1,0:T(8,128)(2,1)S(1)}, u32[]{:S(2)}, u32[]{:S(2)}) collective-permute-start(bf16[128,1024]{1,0:T(8,128)(2,1)S(1)} %copy-done.44), channel_id=1, source_target_pairs={{0,2},{2,0},{4,6},{6,4},{1,3},{3,1},{5,7},{7,5},{8,10},{10,8},{12,... | collective-permute-start | bytes 786440 | tf_op jit(solution)/shard_map/ppermute | solution.py:366
  258.1 21.3 %collective-permute-start.28 = (bf16[128,1024]{1,0:T(8,128)(2,1)S(1)}, bf16[128,1024]{1,0:T(8,128)(2,1)S(1)}, u32[]{:S(2)}, u32[]{:S(2)}) collective-permute-start(bf16[128,1024]{1,0:T(8,128)(2,1)S(1)} %copy-done.43), channel_id=1, source_target_pairs={{0,4},{2,6},{4,0},{6,2},{1,5},{3,7},{5,1},{7,3},{8,12},{10,14},{12... | collective-permute-start | bytes 786440 | tf_op jit(solution)/shard_map/ppermute | solution.py:366
  259.9 19.6 %collective-permute-start.29 = (bf16[128,1024]{1,0:T(8,128)(2,1)S(1)}, bf16[128,1024]{1,0:T(8,128)(2,1)S(1)}, u32[]{:S(2)}, u32[]{:S(2)}) collective-permute-start(bf16[128,1024]{1,0:T(8,128)(2,1)S(1)} %copy-done.42), channel_id=1, source_target_pairs={{0,6},{2,4},{4,2},{6,0},{1,7},{3,5},{5,3},{7,1},{8,14},{10,12},{12... | collective-permute-start | bytes 786440 | tf_op jit(solution)/shard_map/ppermute | solution.py:366
  264.9 23.3 %collective-permute-start.35 = (bf16[128,1024]{1,0:T(8,128)(2,1)}, bf16[128,1024]{1,0:T(8,128)(2,1)S(1)}, u32[]{:S(2)}, u32[]{:S(2)}) collective-permute-start(bf16[128,1024]{1,0:T(8,128)(2,1)} %get-tuple-element.178), channel_id=1, source_target_pairs={{0,8},{8,0},{16,24},{24,16},{1,9},{9,1},{17,25},{25,17},{2,10},{10... | collective-permute-start | bytes 786440 | tf_op jit(solution)/shard_map/ppermute | solution.py:366
  266.4 25.9 %collective-permute-start.36 = (bf16[128,1024]{1,0:T(8,128)(2,1)}, bf16[128,1024]{1,0:T(8,128)(2,1)S(1)}, u32[]{:S(2)}, u32[]{:S(2)}) collective-permute-start(bf16[128,1024]{1,0:T(8,128)(2,1)} %get-tuple-element.179), channel_id=1, source_target_pairs={{0,16},{8,24},{16,0},{24,8},{1,17},{9,25},{17,1},{25,9},{2,18},{10... | collective-permute-start | bytes 786440 | tf_op jit(solution)/shard_map/ppermute | solution.py:366
  270.4 22.0 %collective-permute-start.37 = (bf16[128,1024]{1,0:T(8,128)(2,1)}, bf16[128,1024]{1,0:T(8,128)(2,1)S(1)}, u32[]{:S(2)}, u32[]{:S(2)}) collective-permute-start(bf16[128,1024]{1,0:T(8,128)(2,1)} %get-tuple-element.180), channel_id=1, source_target_pairs={{0,24},{8,16},{16,8},{24,0},{1,25},{9,17},{17,9},{25,1},{2,26},{10... | collective-permute-start | bytes 786440 | tf_op jit(solution)/shard_map/ppermute | solution.py:366
  282.3 12.7 %collective-permute-start.31 = (bf16[32,2048]{1,0:T(8,128)(2,1)}, bf16[32,2048]{1,0:T(8,128)(2,1)S(1)}, u32[]{:S(2)}, u32[]{:S(2)}) collective-permute-start(bf16[32,2048]{1,0:T(8,128)(2,1)} %get-tuple-element.170), channel_id=1, source_target_pairs={{0,2},{2,0},{4,6},{6,4},{1,3},{3,1},{5,7},{7,5},{8,10},{10,8},{12,... | collective-permute-start | bytes 393224 | tf_op jit(solution)/shard_map/ppermute | solution.py:366
  287.7 12.6 %collective-permute-start.32 = (bf16[32,2048]{1,0:T(8,128)(2,1)}, bf16[32,2048]{1,0:T(8,128)(2,1)S(1)}, u32[]{:S(2)}, u32[]{:S(2)}) collective-permute-start(bf16[32,2048]{1,0:T(8,128)(2,1)} %get-tuple-element.171), channel_id=1, source_target_pairs={{0,4},{2,6},{4,0},{6,2},{1,5},{3,7},{5,1},{7,3},{8,12},{10,14},{12... | collective-permute-start | bytes 393224 | tf_op jit(solution)/shard_map/ppermute | solution.py:366
  288.1 12.1 %collective-permute-start.33 = (bf16[32,2048]{1,0:T(8,128)(2,1)}, bf16[32,2048]{1,0:T(8,128)(2,1)S(1)}, u32[]{:S(2)}, u32[]{:S(2)}) collective-permute-start(bf16[32,2048]{1,0:T(8,128)(2,1)} %get-tuple-element.172), channel_id=1, source_target_pairs={{0,6},{2,4},{4,2},{6,0},{1,7},{3,5},{5,3},{7,1},{8,14},{10,12},{12... | collective-permute-start | bytes 393224 | tf_op jit(solution)/shard_map/ppermute | solution.py:366
  292.3 22.2 %collective-permute-start.17 = (bf16[64,1024]{1,0:T(8,128)(2,1)S(1)}, bf16[64,1024]{1,0:T(8,128)(2,1)S(1)}, u32[]{:S(2)}, u32[]{:S(2)}) collective-permute-start(bf16[64,1024]{1,0:T(8,128)(2,1)S(1)} %copy-done.51), channel_id=1, source_target_pairs={{0,1},{1,0},{2,3},{3,2},{4,5},{5,4},{6,7},{7,6},{8,9},{9,8},{10,11... | collective-permute-start | bytes 393224 | tf_op jit(solution)/shard_map/ppermute | solution.py:366
  292.4 24.4 %collective-permute-start.30 = (bf16[64,1024]{1,0:T(8,128)(2,1)}, bf16[64,1024]{1,0:T(8,128)(2,1)S(1)}, u32[]{:S(2)}, u32[]{:S(2)}) collective-permute-start(bf16[64,1024]{1,0:T(8,128)(2,1)} %get-tuple-element.166), channel_id=1, source_target_pairs={{0,1},{1,0},{2,3},{3,2},{4,5},{5,4},{6,7},{7,6},{8,9},{9,8},{10,11... | collective-permute-start | bytes 393224 | tf_op jit(solution)/shard_map/ppermute | solution.py:366
  (71 other events, 319.9 us)
Sparse Core Ops, SparseCore 0:
  23.7 24.0 all-gather.2
  49.7 54.4 all-gather.4
  195.1 63.5 reduce-scatter.4
  262.3 39.6 reduce-scatter.2
where the time goes:
time: 329 us; the launch traced here: 328 us
  waiting for transfers between devices  122 us (37%)
  Pallas kernels  97.1 us (30%)
  starting transfers between devices  76.5 us (23%)
  local copies, waits for them, and re-layouts  15.3 us (5%)
  between operations  14.2 us (4%)
  other arithmetic  3.42 us (1%)
    ppermute x44, waiting for transfers between devices, swap(): return lax.ppermute(value, axes, [(i, i ^ k) for i in range(count)])  122 us
    pallas_call x23, Pallas kernels, call(): pl.pallas_call(run, out_shape=[jax.ShapeDtypeStruct(s, d) for s, d in out...  97.1 us
    ppermute x44, starting transfers between devices, swap(): return lax.ppermute(value, axes, [(i, i ^ k) for i in range(count)])  76.4 us
    unnamed x111, local copies, waits for them, and re-layouts  11.9 us
  transfers between devices with their start and end apart: 48, of which 23 were waited for; matrix products, arithmetic and copies ran while one was open for 2% of the time, Pallas kernels for 18%

commit v1 on v0

--- a/solution.py
+++ b/solution.py
@@ -1009,6 +1009,44 @@
         )
         x_got = exchange(x_parts, line, nline)
 
+
+        g_last = lax.psum_scatter(g_last, dpc, scatter_dimension=0, tiled=True)
+
+        def split_ff(rk, *refs):
+            parts, (g_ref, down), outs = refs[:nyx], refs[nyx : nyx + 2], refs[nyx + 2 :]
+            down[...] = g_ref[:, 2 * ffq :].astype(F32)
+            for k in range(nline):
+                here = slice(k * rows, (k + 1) * rows)
+                outs[k][:, : 2 * ffq] = g_ref[here, : 2 * ffq]
+                total = parts[0][here, :].astype(F32)
+                for j in range(1, nyx):
+                    total = total + parts[j][here, :].astype(F32)
+                outs[k][:, 2 * ffq :] = total.astype(BF)
+
+        g_down, *g_parts = call(
+            split_ff,
+            [((ffb, dm), F32)] + [((rows, 2 * ffq + dm), BF)] * nline,
+            (ranks, *out_got, g_ff),
+            after=tuple(x_got[1:]),
+        )
+        g_parts = exchange(g_parts, line, nline)
+
+        def place_ff(rk, *refs):
+            parts, outs, g_o = refs[:nline], refs[nline : nline + 2], refs[nline + 2]
+            total = parts[0][:, 2 * ffq :].astype(F32)
+            for k in range(nline):
+                for d, cols in enumerate(ff_cols(rk, k)):
+                    for i in range(2):
+                        here = i * ffq + d * sub
+                        outs[i][:, cols] = parts[k][:, here : here + sub].astype(F32)
+                if k:
+                    total = total + parts[k][:, 2 * ffq :].astype(F32)
+            g_o[...] = total
+
+        g_up, g_gate, g_out = call(
+            place_ff, [((rows, ff), F32)] * 2 + [((rows, dm), F32)], (ranks, *g_parts)
+        )
+
         def finish_tokens(rk, *refs):
             parts, (direct, keep, send) = refs[:nline], refs[nline:]
             d = direct[...] + parts[0][...]
@@ -1029,43 +1067,6 @@
         (tokens_grad,) = call(join_rows, [((nseq, seg, dm), F32)], (ranks, x_keep, x_recv))
         (hidden_out,) = call(join_rows, [((nseq, seg, dm), BF)], (ranks, hid_keep, hid_recv))
 
-        g_last = lax.psum_scatter(g_last, dpc, scatter_dimension=0, tiled=True)
-
-        def split_ff(rk, g_ref, down, *outs):
-            down[...] = g_ref[:, 2 * ffq :].astype(F32)
-            for k in range(nline):
-                outs[k][...] = g_ref[k * rows : (k + 1) * rows, : 2 * ffq]
-
-        g_down, *g_parts = call(
-            split_ff,
-            [((ffb, dm), F32)] + [((rows, 2 * ffq), BF)] * nline,
-            (ranks, g_ff),
-            after=tuple(x_got[1:]),
-        )
-        g_parts = exchange(g_parts, line, nline)
-
-        def place_ff(rk, *refs):
-            parts, outs = refs[:nline], refs[nline:]
-            for k in range(nline):
-                for d, cols in enumerate(ff_cols(rk, k)):
-                    for i in range(2):
-                        here = i * ffq + d * sub
-                        outs[i][:, cols] = parts[k][:, here : here + sub].astype(F32)
-
-        g_up, g_gate = call(place_ff, [((rows, ff), F32)] * 2, (ranks, *g_parts))
-
-        def sum_out(rk, *refs):
-            parts, outs = refs[:nyx], refs[nyx:]
-            for k in range(nline):
-                here = slice(k * rows, (k + 1) * rows)
-                total = parts[0][here, :].astype(F32)
-                for j in range(1, nyx):
-                    total = total + parts[j][here, :].astype(F32)
-                outs[k][...] = total.astype(BF)
-
-        out_sum = call(sum_out, [((rows, dm), BF)] * nline, (ranks, *out_got))
-        out_got = exchange(out_sum, line, nline)
-
         def split_last(rk, g_ref, *outs):
             for k in range(nline):
                 outs[k][...] = g_ref[k * rows : (k + 1) * rows, :]
@@ -1074,35 +1075,30 @@
             split_last,
             [((rows, wide), BF)] * nline,
             (ranks, g_last),
-            after=(g_up, *out_got[1:]),
+            after=(tokens_grad, hidden_out, g_parts[1]),
         )
         last = exchange(last, line, nline)
 
         def place_last(rk, *refs):
-            parts, out_parts = refs[:nline], refs[nline : 2 * nline]
-            outs, refs = refs[2 * nline : 2 * nline + 3], refs[2 * nline + 3 :]
-            g_o, vec_outs = refs[0], refs[1:]
-            g_sum, v_sum = None, None
+            parts, outs, vec_outs = refs[:nline], refs[nline : nline + 3], refs[nline + 3 :]
+            v_sum = None
             for k in range(nline):
                 cols = pl.ds(pl.multiple_of((rk[6] ^ k) * hc, 128), hc)
                 for i in range(3):
                     outs[i][:, cols] = parts[k][:, i * hc : (i + 1) * hc].astype(F32)
                 vec = parts[k][:16, 3 * hc : wide].astype(F32)
-                part = out_parts[k][...].astype(F32)
-                g_sum = part if g_sum is None else g_sum + part
                 v_sum = vec if v_sum is None else v_sum + vec
-            g_o[...] = g_sum
             vec_outs[0][...] = v_sum[:1]
             vec_outs[1][...] = v_sum[1:2]
             for i in range(3):
                 vec_outs[2 + i][...] = v_sum[2:3, i * rows : (i + 1) * rows]
 
-        g_query, g_key, g_value, g_out, *vecs = call(
+        g_query, g_key, g_value, *vecs = call(
             place_last,
-            [((rows, dm), F32)] * 4
+            [((rows, dm), F32)] * 3
             + [((1, ffb), F32)] * 2
             + [((1, rows), F32)] * 3,
-            (ranks, *last, *out_got),
+            (ranks, *last),
         )
         g_s_up, g_s_gate, g_aa, g_am, g_sqk = [v.reshape(-1) for v in vecs]
         return (

time: 329 us -> 324 us (0.985)
  starting transfers between devices: 76.5 us -> 72.1 us
    ppermute x44 -> x41, starting transfers between devices: 76.4 us -> 72 us  [swap(): return lax.ppermute(value, axes, [(i, i ^ k) for i in range(count)])]
    reduce_scatter x1, waiting for transfers between devices: 0.01 us -> 3.64 us  [body(): g_last = lax.psum_scatter(g_last, dpc, scatter_dimension=0, tiled=True)]
    ppermute x44 -> x41, waiting for transfers between devices: 122 us -> 118 us  [swap(): return lax.ppermute(value, axes, [(i, i ^ k) for i in range(count)])]
    pallas_call x23 -> x22, Pallas kernels: 97.1 us -> 95.6 us  [call(): pl.pallas_call(run, out_shape=[jax.ShapeDtypeStruct(s, d) for s, d in out...]
    unnamed x111 -> x105, local copies, waits for them, and re-layouts: 11.9 us -> 12.5 us
  transfers between devices with their start and end apart: 48 -> 45, of which waited for: 23 -> 24; matrix products, arithmetic and copies ran while one was open for 2% -> 2% of each run, Pallas kernels for 18% -> 18%
where the time goes in v1:
time: 324 us; the launch traced here: 323 us
  waiting for transfers between devices  122 us (38%)
  Pallas kernels  95.6 us (30%)
  starting transfers between devices  72.1 us (22%)
  local copies, waits for them, and re-layouts  15.8 us (5%)
  between operations  14.2 us (4%)
  other arithmetic  3.42 us (1%)
    ppermute x41, waiting for transfers between devices, swap(): return lax.ppermute(value, axes, [(i, i ^ k) for i in range(count)])  118 us
    pallas_call x22, Pallas kernels, call(): pl.pallas_call(run, out_shape=[jax.ShapeDtypeStruct(s, d) for s, d in out...  95.6 us
    ppermute x41, starting transfers between devices, swap(): return lax.ppermute(value, axes, [(i, i ^ k) for i in range(count)])  72 us
    unnamed x105, local copies, waits for them, and re-layouts  12.5 us
  transfers between devices with their start and end apart: 45, of which 24 were waited for; matrix products, arithmetic and copies ran while one was open for 2% of the time, Pallas kernels for 18%

profile of v1, /device:TPU:0, one launch (start us, length us, event | category | flops | bytes accessed | tf_op | source)
XLA Modules:
  0.0 323.2 jit_solution(1180975024945345071)
XLA Ops:
  9.6 3.0 collective-permute-start.4
  12.6 2.6 collective-permute-start.5
  15.2 3.5 %collective-permute-done.5.refs_3_ = bf16[32,768]{1,0:T(8,128)(2,1)S(1)} collective-permute-done((bf16[32,768]{1,0:T(8,128)(2,1)}, bf16[32,768]{1,0:T(8,128)(2,1)S(1)}, u32[]{:S(2)}, u32[]{:S(2)}) %collective-permute-start.5) | collective-permute-done | bytes 49184 | tf_op jit(solution)/shard_map/ppermute | solution.py:366
  30.1 3.1 collective-permute-start.12
  38.0 7.3 %collective-permute-done.11.refs_3_ = bf16[32,3072]{1,0:T(8,128)(2,1)S(1)} collective-permute-done((bf16[32,3072]{1,0:T(8,128)(2,1)}, bf16[32,3072]{1,0:T(8,128)(2,1)S(1)}, u32[]{:S(2)}, u32[]{:S(2)}) %collective-permute-start.11) | collective-permute-done | bytes 196640 | tf_op jit(solution)/shard_map/ppermute | solution.py:366
  48.6 3.0 collective-permute-start.1
  56.9 5.3 %collective-permute-done.1.refs_2_ = bf16[144,1024]{1,0:T(8,128)(2,1)S(1)} collective-permute-done((bf16[144,1024]{1,0:T(8,128)(2,1)S(1)}, bf16[144,1024]{1,0:T(8,128)(2,1)S(1)}, u32[]{:S(2)}, u32[]{:S(2)}) %collective-permute-start.1) | collective-permute-done | bytes 294944 | tf_op jit(solution)/shard_map/ppermute | solution.py:366
  62.2 12.3 %collective-permute-done.2.refs_3_ = bf16[144,1024]{1,0:T(8,128)(2,1)S(1)} collective-permute-done((bf16[144,1024]{1,0:T(8,128)(2,1)S(1)}, bf16[144,1024]{1,0:T(8,128)(2,1)S(1)}, u32[]{:S(2)}, u32[]{:S(2)}) %collective-permute-start.2) | collective-permute-done | bytes 294944 | tf_op jit(solution)/shard_map/ppermute | solution.py:366
  75.3 9.1 %shard_map.259 = (bf16[512,256]{1,0:T(8,128)(2,1)}, bf16[512,1024]{1,0:T(8,128)(2,1)}, bf16[1024,768]{1,0:T(8,128)(2,1)}, f32[512,256]{1,0:T(8,128)}, f32[512,25...) custom-call(s32[7]{0:T(128)} %stack.39.refs_0_, ...), custom_call_target="tpu_custom_call" | custom-call | flops 1073741824 | bytes 9831452 | tf_op jit(solution)/shard_map/pallas_call | solution.py:339
  84.4 4.3 %collective-permute-start.7 = (bf16[512,256]{1,0:T(8,128)(2,1)}, bf16[512,256]{1,0:T(8,128)(2,1)S(1)}, u32[]{:S(2)}, u32[]{:S(2)}) collective-permute-start(bf16[512,256]{1,0:T(8,128)(2,1)} %get-tuple-element.110.refs_1_.refs_2_), channel_id=1, source_target_pairs={{0,2},{2,0},{4,6},{6,4},{1,3},{3,1},{5,7},{7,5},{8,10},{10,8},{12,... | collective-permute-start | bytes 786440 | tf_op jit(solution)/shard_map/ppermute | solution.py:366
  91.1 6.9 %collective-permute-done.7.refs_2_.refs_3_ = bf16[512,256]{1,0:T(8,128)(2,1)S(1)} collective-permute-done((bf16[512,256]{1,0:T(8,128)(2,1)}, bf16[512,256]{1,0:T(8,128)(2,1)S(1)}, u32[]{:S(2)}, u32[]{:S(2)}) %collective-permute-start.7) | collective-permute-done | bytes 262176 | tf_op jit(solution)/shard_map/ppermute | solution.py:366
  98.1 10.4 %collective-permute-done.8.refs_3_.refs_4_ = bf16[512,256]{1,0:T(8,128)(2,1)S(1)} collective-permute-done((bf16[512,256]{1,0:T(8,128)(2,1)}, bf16[512,256]{1,0:T(8,128)(2,1)S(1)}, u32[]{:S(2)}, u32[]{:S(2)}) %collective-permute-start.8) | collective-permute-done | bytes 262176 | tf_op jit(solution)/shard_map/ppermute | solution.py:366
  109.3 12.1 %shard_map.261 = (f32[128,1024]{1,0:T(8,128)}, bf16[128,1024]{1,0:T(8,128)(2,1)}, bf16[128,1024]{1,0:T(8,128)(2,1)}, bf16[128,1024]{1,0:T(8,128)(2,1)}, bf16[512...) custom-call(s32[7]{0:T(128)} %stack.39.refs_0_, ...), custom_call_target="tpu_custom_call" | custom-call | flops 4294967296 | bytes 17051676 | tf_op jit(solution)/shard_map/pallas_call | solution.py:339
  121.4 5.1 %collective-permute-start.13 = (bf16[128,1024]{1,0:T(8,128)(2,1)}, bf16[128,1024]{1,0:T(8,128)(2,1)S(1)}, u32[]{:S(2)}, u32[]{:S(2)}) collective-permute-start(bf16[128,1024]{1,0:T(8,128)(2,1)} %get-tuple-element.119), channel_id=1, source_target_pairs={{0,2},{2,0},{4,6},{6,4},{1,3},{3,1},{5,7},{7,5},{8,10},{10,8},{12,... | collective-permute-start | bytes 786440 | tf_op jit(solution)/shard_map/ppermute | solution.py:366
  132.2 3.6 %collective-permute-done.13.refs_2_ = bf16[128,1024]{1,0:T(8,128)(2,1)S(1)} collective-permute-done((bf16[128,1024]{1,0:T(8,128)(2,1)}, bf16[128,1024]{1,0:T(8,128)(2,1)S(1)}, u32[]{:S(2)}, u32[]{:S(2)}) %collective-permute-start.13) | collective-permute-done | bytes 262176 | tf_op jit(solution)/shard_map/ppermute | solution.py:366
  135.8 12.0 %collective-permute-done.14.refs_3_ = bf16[128,1024]{1,0:T(8,128)(2,1)S(1)} collective-permute-done((bf16[128,1024]{1,0:T(8,128)(2,1)}, bf16[128,1024]{1,0:T(8,128)(2,1)S(1)}, u32[]{:S(2)}, u32[]{:S(2)}) %collective-permute-start.14) | collective-permute-done | bytes 262176 | tf_op jit(solution)/shard_map/ppermute | solution.py:366
  148.6 2.9 shard_map.263
  151.5 4.2 %collective-permute-start.18 = (bf16[128,1024]{1,0:T(8,128)(2,1)}, bf16[128,1024]{1,0:T(8,128)(2,1)S(1)}, u32[]{:S(2)}, u32[]{:S(2)}) collective-permute-start(bf16[128,1024]{1,0:T(8,128)(2,1)} %get-tuple-element.127.refs_1_), channel_id=1, source_target_pairs={{0,2},{2,0},{4,6},{6,4},{1,3},{3,1},{5,7},{7,5},{8,10},{10,8},{12,... | collective-permute-start | bytes 786440 | tf_op jit(solution)/shard_map/ppermute | solution.py:366
  158.1 6.5 %collective-permute-done.18.refs_2_ = bf16[128,1024]{1,0:T(8,128)(2,1)S(1)} collective-permute-done((bf16[128,1024]{1,0:T(8,128)(2,1)}, bf16[128,1024]{1,0:T(8,128)(2,1)S(1)}, u32[]{:S(2)}, u32[]{:S(2)}) %collective-permute-start.18) | collective-permute-done | bytes 262176 | tf_op jit(solution)/shard_map/ppermute | solution.py:366
  164.7 11.5 %collective-permute-done.19.refs_3_ = bf16[128,1024]{1,0:T(8,128)(2,1)S(1)} collective-permute-done((bf16[128,1024]{1,0:T(8,128)(2,1)}, bf16[128,1024]{1,0:T(8,128)(2,1)S(1)}, u32[]{:S(2)}, u32[]{:S(2)}) %collective-permute-start.19) | collective-permute-done | bytes 262176 | tf_op jit(solution)/shard_map/ppermute | solution.py:366
  177.0 17.9 %shard_map.265 = (f32[128,1024]{1,0:T(8,128)}, bf16[128,1024]{1,0:T(8,128)(2,1)}, bf16[128,1024]{1,0:T(8,128)(2,1)}, bf16[128,1024]{1,0:T(8,128)(2,1)}, f32[1,10...) custom-call(s32[7]{0:T(128)} %stack.39.refs_0_, bf16[128,1024]{1,0:T(8,128)(2,1)} %get-tuple-element.127.refs_1_, ...), custom_call_target="tpu_custom_call" | custom-call | flops 6442450944 | bytes 21250076 | tf_op jit(solution)/shard_map/pallas_call | solution.py:339
  195.8 4.1 %collective-permute-start.21 = (bf16[128,1024]{1,0:T(8,128)(2,1)S(1)}, bf16[128,1024]{1,0:T(8,128)(2,1)S(1)}, u32[]{:S(2)}, u32[]{:S(2)}) collective-permute-start(bf16[128,1024]{1,0:T(8,128)(2,1)S(1)} %copy-done.44), channel_id=1, source_target_pairs={{0,2},{2,0},{4,6},{6,4},{1,3},{3,1},{5,7},{7,5},{8,10},{10,8},{12,... | collective-permute-start | bytes 786440 | tf_op jit(solution)/shard_map/ppermute | solution.py:366
  202.6 6.0 %collective-permute-done.21.refs_2_ = bf16[128,1024]{1,0:T(8,128)(2,1)S(1)} collective-permute-done((bf16[128,1024]{1,0:T(8,128)(2,1)S(1)}, bf16[128,1024]{1,0:T(8,128)(2,1)S(1)}, u32[]{:S(2)}, u32[]{:S(2)}) %collective-permute-start.21) | collective-permute-done | bytes 262176 | tf_op jit(solution)/shard_map/ppermute | solution.py:366
  208.6 11.4 %collective-permute-done.22.refs_3_ = bf16[128,1024]{1,0:T(8,128)(2,1)S(1)} collective-permute-done((bf16[128,1024]{1,0:T(8,128)(2,1)S(1)}, bf16[128,1024]{1,0:T(8,128)(2,1)S(1)}, u32[]{:S(2)}, u32[]{:S(2)}) %collective-permute-start.22) | collective-permute-done | bytes 262176 | tf_op jit(solution)/shard_map/ppermute | solution.py:366
  220.9 5.5 %shard_map.266 = (bf16[128,256]{1,0:T(8,128)(2,1)}, bf16[128,256]{1,0:T(8,128)(2,1)}, bf16[128,256]{1,0:T(8,128)(2,1)}, bf16[128,256]{1,0:T(8,128)(2,1)}, bf16[1...) custom-call(s32[7]{0:T(128)} %stack.39.refs_0_, f32[128,1024]{1,0:T(8,128)} %get-tuple-element.132.refs_1_, ...), custom_call_target="tpu_custom_call" | custom-call | flops 268435456 | bytes 12623900 | tf_op jit(solution)/shard_map/pallas_call | solution.py:339
  227.2 4.0 %collective-permute-start.24 = (bf16[128,256]{1,0:T(8,128)(2,1)}, bf16[128,256]{1,0:T(8,128)(2,1)S(1)}, u32[]{:S(2)}, u32[]{:S(2)}) collective-permute-start(bf16[128,256]{1,0:T(8,128)(2,1)} %get-tuple-element.139), channel_id=1, source_target_pairs={{0,2},{2,0},{4,6},{6,4},{1,3},{3,1},{5,7},{7,5},{8,10},{10,8},{12,... | collective-permute-start | bytes 196616 | tf_op jit(solution)/shard_map/ppermute | solution.py:366
  238.2 14.7 %shard_map.267 = (f32[128,1024]{1,0:T(8,128)}, bf16[128,1024]{1,0:T(8,128)(2,1)}, bf16[128,1024]{1,0:T(8,128)(2,1)}, bf16[128,1024]{1,0:T(8,128)(2,1)}, bf16[1024,896]{1,0:T(8,128)(2,1)}) custom-call(s32[7]{0:T(128)} %stack.39.refs_0_, bf16[128,256]{1,0:T(8,128)(2,1)} %get-tuple-element.138.refs_1_, bf16[128,256]{1,0:T(8,128)(2,1)} %copy-done.49, ...), custom_call_target="tpu_custom_call" | custom-call | flops 2281701376 | bytes 9962524 | tf_op jit(solution)/shard_map/pallas_call | solution.py:339
  253.0 3.7 %shard_map.270 = (bf16[512,1024]{1,0:T(8,128)(2,1)}, bf16[512,1024]{1,0:T(8,128)(2,1)}) custom-call(s32[7]{0:T(128)} %stack.39.refs_0_, bf16[128,1024]{1,0:T(8,128)(2,1)} %get-tuple-element.164.refs_1_, bf16[512,256]{1,0:T(8,128)(2,1)} %get-tuple-element.110.refs_1_.refs_2_, bf16[512,256]{1,0:T(8,128)(2,1)} %copy-done.6, bf16[512,256]{1,0:T(8,128)(2,1)} %copy-done.7, ...), custom_call_target="tpu_custom_call" | custom-call | flops 268435456 | bytes 3407900 | tf_op jit(solution)/shard_map/pallas_call | solution.py:339
  262.3 2.6 shard_map.271
  272.9 6.6 %collective-permute-done.28.refs_3_.refs_7_ = bf16[128,1024]{1,0:T(8,128)(2,1)S(1)} collective-permute-done((bf16[128,1024]{1,0:T(8,128)(2,1)S(1)}, bf16[128,1024]{1,0:T(8,128)(2,1)S(1)}, u32[]{:S(2)}, u32[]{:S(2)}) %collective-permute-start.28) | collective-permute-done | bytes 262176 | tf_op jit(solution)/shard_map/ppermute | solution.py:366
  283.0 5.3 %collective-permute-start.35 = (bf16[32,3072]{1,0:T(8,128)(2,1)}, bf16[32,3072]{1,0:T(8,128)(2,1)S(1)}, u32[]{:S(2)}, u32[]{:S(2)}) collective-permute-start(bf16[32,3072]{1,0:T(8,128)(2,1)} %get-tuple-element.172), channel_id=1, source_target_pairs={{0,2},{2,0},{4,6},{6,4},{1,3},{3,1},{5,7},{7,5},{8,10},{10,8},{12,... | collective-permute-start | bytes 589832 | tf_op jit(solution)/shard_map/ppermute | solution.py:366
  298.3 3.6 %reduce-scatter.3.cloned.1.call-done.refs_1_ = bf16[128,896]{1,0:T(8,128)(2,1)} async-done(((bf16[1024,896]{1,0:T(8,128)(2,1)}), bf16[128,896]{1,0:T(8,128)(2,1)}) %reduce-scatter.3.cloned.1.call-update) | async-done | bytes 229392 | tf_op jit(solution)/shard_map/reduce_scatter | solution.py:1013
  (210 shorter events, 94.8 us)
Async XLA Ops:
  7.2 67.3 %all-gather.3.cloned.1.call-start = ((), (), s32[]{:S(2)}) async-start(), calls=%async_computation.2 | async-start | bytes 1769472 | tf_op jit(solution)/shard_map/all_gather | solution.py:461
  23.5 85.0 %all-gather.5.cloned.1.call-start = ((), (), s32[]{:S(2)}) async-start(), calls=%async_computation.3 | async-start | bytes 9437184 | tf_op jit(solution)/shard_map/all_gather | solution.py:475
  28.8 9.2 %collective-permute-start.10 = (bf16[32,3072]{1,0:T(8,128)(2,1)}, bf16[32,3072]{1,0:T(8,128)(2,1)S(1)}, u32[]{:S(2)}, u32[]{:S(2)}) collective-permute-start(bf16[32,3072]{1,0:T(8,128)(2,1)} %get-tuple-element.113), channel_id=1, source_target_pairs={{0,2},{2,0},{4,6},{6,4},{1,3},{3,1},{5,7},{7,5},{8,10},{10,8},{12,... | collective-permute-start | bytes 589832 | tf_op jit(solution)/shard_map/ppermute | solution.py:366
  28.8 16.4 %collective-permute-start.11 = (bf16[32,3072]{1,0:T(8,128)(2,1)}, bf16[32,3072]{1,0:T(8,128)(2,1)S(1)}, u32[]{:S(2)}, u32[]{:S(2)}) collective-permute-start(bf16[32,3072]{1,0:T(8,128)(2,1)} %get-tuple-element.114), channel_id=1, source_target_pairs={{0,4},{2,6},{4,0},{6,2},{1,5},{3,7},{5,1},{7,3},{8,12},{10,14},{12... | collective-permute-start | bytes 589832 | tf_op jit(solution)/shard_map/ppermute | solution.py:366
  30.1 15.1 %collective-permute-start.12 = (bf16[32,3072]{1,0:T(8,128)(2,1)}, bf16[32,3072]{1,0:T(8,128)(2,1)S(1)}, u32[]{:S(2)}, u32[]{:S(2)}) collective-permute-start(bf16[32,3072]{1,0:T(8,128)(2,1)} %get-tuple-element.115), channel_id=1, source_target_pairs={{0,6},{2,4},{4,2},{6,0},{1,7},{3,5},{5,3},{7,1},{8,14},{10,12},{12... | collective-permute-start | bytes 589832 | tf_op jit(solution)/shard_map/ppermute | solution.py:366
  48.5 231.2 %reduce-scatter.5.cloned.1.call-start = ((), (), s32[]{:S(2)}) async-start(), calls=%async_computation.5 | async-start | bytes 7077888 | tf_op jit(solution)/shard_map/reduce_scatter | solution.py:815
  48.6 13.6 %collective-permute-start.1 = (bf16[144,1024]{1,0:T(8,128)(2,1)S(1)}, bf16[144,1024]{1,0:T(8,128)(2,1)S(1)}, u32[]{:S(2)}, u32[]{:S(2)}) collective-permute-start(bf16[144,1024]{1,0:T(8,128)(2,1)S(1)} %copy-done), channel_id=1, source_target_pairs={{0,2},{2,0},{4,6},{6,4},{1,3},{3,1},{5,7},{7,5},{8,10},{10,8},{12,... | collective-permute-start | bytes 884744 | tf_op jit(solution)/shard_map/ppermute | solution.py:366
  51.6 22.8 %collective-permute-start.2 = (bf16[144,1024]{1,0:T(8,128)(2,1)S(1)}, bf16[144,1024]{1,0:T(8,128)(2,1)S(1)}, u32[]{:S(2)}, u32[]{:S(2)}) collective-permute-start(bf16[144,1024]{1,0:T(8,128)(2,1)S(1)} %copy-done), channel_id=1, source_target_pairs={{0,4},{2,6},{4,0},{6,2},{1,5},{3,7},{5,1},{7,3},{8,12},{10,14},{12... | collective-permute-start | bytes 884744 | tf_op jit(solution)/shard_map/ppermute | solution.py:366
  51.7 22.8 %collective-permute-start.3 = (bf16[144,1024]{1,0:T(8,128)(2,1)S(1)}, bf16[144,1024]{1,0:T(8,128)(2,1)S(1)}, u32[]{:S(2)}, u32[]{:S(2)}) collective-permute-start(bf16[144,1024]{1,0:T(8,128)(2,1)S(1)} %copy-done), channel_id=1, source_target_pairs={{0,6},{2,4},{4,2},{6,0},{1,7},{3,5},{5,3},{7,1},{8,14},{10,12},{12... | collective-permute-start | bytes 884744 | tf_op jit(solution)/shard_map/ppermute | solution.py:366
  84.4 13.7 %collective-permute-start.7 = (bf16[512,256]{1,0:T(8,128)(2,1)}, bf16[512,256]{1,0:T(8,128)(2,1)S(1)}, u32[]{:S(2)}, u32[]{:S(2)}) collective-permute-start(bf16[512,256]{1,0:T(8,128)(2,1)} %get-tuple-element.110.refs_1_.refs_2_), channel_id=1, source_target_pairs={{0,2},{2,0},{4,6},{6,4},{1,3},{3,1},{5,7},{7,5},{8,10},{10,8},{12,... | collective-permute-start | bytes 786440 | tf_op jit(solution)/shard_map/ppermute | solution.py:366
  88.7 19.8 %collective-permute-start.8 = (bf16[512,256]{1,0:T(8,128)(2,1)}, bf16[512,256]{1,0:T(8,128)(2,1)S(1)}, u32[]{:S(2)}, u32[]{:S(2)}) collective-permute-start(bf16[512,256]{1,0:T(8,128)(2,1)} %get-tuple-element.110.refs_1_.refs_2_), channel_id=1, source_target_pairs={{0,4},{2,6},{4,0},{6,2},{1,5},{3,7},{5,1},{7,3},{8,12},{10,14},{12... | collective-permute-start | bytes 786440 | tf_op jit(solution)/shard_map/ppermute | solution.py:366
  88.7 19.8 %collective-permute-start.9 = (bf16[512,256]{1,0:T(8,128)(2,1)}, bf16[512,256]{1,0:T(8,128)(2,1)S(1)}, u32[]{:S(2)}, u32[]{:S(2)}) collective-permute-start(bf16[512,256]{1,0:T(8,128)(2,1)} %get-tuple-element.110.refs_1_.refs_2_), channel_id=1, source_target_pairs={{0,6},{2,4},{4,2},{6,0},{1,7},{3,5},{5,3},{7,1},{8,14},{10,12},{12... | collective-permute-start | bytes 786440 | tf_op jit(solution)/shard_map/ppermute | solution.py:366
  121.4 14.4 %collective-permute-start.13 = (bf16[128,1024]{1,0:T(8,128)(2,1)}, bf16[128,1024]{1,0:T(8,128)(2,1)S(1)}, u32[]{:S(2)}, u32[]{:S(2)}) collective-permute-start(bf16[128,1024]{1,0:T(8,128)(2,1)} %get-tuple-element.119), channel_id=1, source_target_pairs={{0,2},{2,0},{4,6},{6,4},{1,3},{3,1},{5,7},{7,5},{8,10},{10,8},{12,... | collective-permute-start | bytes 786440 | tf_op jit(solution)/shard_map/ppermute | solution.py:366
  126.5 21.3 %collective-permute-start.14 = (bf16[128,1024]{1,0:T(8,128)(2,1)}, bf16[128,1024]{1,0:T(8,128)(2,1)S(1)}, u32[]{:S(2)}, u32[]{:S(2)}) collective-permute-start(bf16[128,1024]{1,0:T(8,128)(2,1)} %get-tuple-element.120), channel_id=1, source_target_pairs={{0,4},{2,6},{4,0},{6,2},{1,5},{3,7},{5,1},{7,3},{8,12},{10,14},{12... | collective-permute-start | bytes 786440 | tf_op jit(solution)/shard_map/ppermute | solution.py:366
  126.5 21.3 %collective-permute-start.15 = (bf16[128,1024]{1,0:T(8,128)(2,1)}, bf16[128,1024]{1,0:T(8,128)(2,1)S(1)}, u32[]{:S(2)}, u32[]{:S(2)}) collective-permute-start(bf16[128,1024]{1,0:T(8,128)(2,1)} %get-tuple-element.121), channel_id=1, source_target_pairs={{0,6},{2,4},{4,2},{6,0},{1,7},{3,5},{5,3},{7,1},{8,14},{10,12},{12... | collective-permute-start | bytes 786440 | tf_op jit(solution)/shard_map/ppermute | solution.py:366
  151.5 13.2 %collective-permute-start.18 = (bf16[128,1024]{1,0:T(8,128)(2,1)}, bf16[128,1024]{1,0:T(8,128)(2,1)S(1)}, u32[]{:S(2)}, u32[]{:S(2)}) collective-permute-start(bf16[128,1024]{1,0:T(8,128)(2,1)} %get-tuple-element.127.refs_1_), channel_id=1, source_target_pairs={{0,2},{2,0},{4,6},{6,4},{1,3},{3,1},{5,7},{7,5},{8,10},{10,8},{12,... | collective-permute-start | bytes 786440 | tf_op jit(solution)/shard_map/ppermute | solution.py:366
  155.7 20.4 %collective-permute-start.19 = (bf16[128,1024]{1,0:T(8,128)(2,1)}, bf16[128,1024]{1,0:T(8,128)(2,1)S(1)}, u32[]{:S(2)}, u32[]{:S(2)}) collective-permute-start(bf16[128,1024]{1,0:T(8,128)(2,1)} %get-tuple-element.127.refs_1_), channel_id=1, source_target_pairs={{0,4},{2,6},{4,0},{6,2},{1,5},{3,7},{5,1},{7,3},{8,12},{10,14},{12... | collective-permute-start | bytes 786440 | tf_op jit(solution)/shard_map/ppermute | solution.py:366
  155.7 20.4 %collective-permute-start.20 = (bf16[128,1024]{1,0:T(8,128)(2,1)}, bf16[128,1024]{1,0:T(8,128)(2,1)S(1)}, u32[]{:S(2)}, u32[]{:S(2)}) collective-permute-start(bf16[128,1024]{1,0:T(8,128)(2,1)} %get-tuple-element.127.refs_1_), channel_id=1, source_target_pairs={{0,6},{2,4},{4,2},{6,0},{1,7},{3,5},{5,3},{7,1},{8,14},{10,12},{12... | collective-permute-start | bytes 786440 | tf_op jit(solution)/shard_map/ppermute | solution.py:366
  194.9 107.0 %reduce-scatter.3.cloned.1.call-start = ((), (), s32[]{:S(2)}) async-start(), calls=%async_computation.4 | async-start | bytes 2064384 | tf_op jit(solution)/shard_map/reduce_scatter | solution.py:1013
  195.8 12.9 %collective-permute-start.21 = (bf16[128,1024]{1,0:T(8,128)(2,1)S(1)}, bf16[128,1024]{1,0:T(8,128)(2,1)S(1)}, u32[]{:S(2)}, u32[]{:S(2)}) collective-permute-start(bf16[128,1024]{1,0:T(8,128)(2,1)S(1)} %copy-done.44), channel_id=1, source_target_pairs={{0,2},{2,0},{4,6},{6,4},{1,3},{3,1},{5,7},{7,5},{8,10},{10,8},{12,... | collective-permute-start | bytes 786440 | tf_op jit(solution)/shard_map/ppermute | solution.py:366
  199.9 20.1 %collective-permute-start.22 = (bf16[128,1024]{1,0:T(8,128)(2,1)S(1)}, bf16[128,1024]{1,0:T(8,128)(2,1)S(1)}, u32[]{:S(2)}, u32[]{:S(2)}) collective-permute-start(bf16[128,1024]{1,0:T(8,128)(2,1)S(1)} %copy-done.43), channel_id=1, source_target_pairs={{0,4},{2,6},{4,0},{6,2},{1,5},{3,7},{5,1},{7,3},{8,12},{10,14},{12... | collective-permute-start | bytes 786440 | tf_op jit(solution)/shard_map/ppermute | solution.py:366
  199.9 20.1 %collective-permute-start.23 = (bf16[128,1024]{1,0:T(8,128)(2,1)S(1)}, bf16[128,1024]{1,0:T(8,128)(2,1)S(1)}, u32[]{:S(2)}, u32[]{:S(2)}) collective-permute-start(bf16[128,1024]{1,0:T(8,128)(2,1)S(1)} %copy-done.42), channel_id=1, source_target_pairs={{0,6},{2,4},{4,2},{6,0},{1,7},{3,5},{5,3},{7,1},{8,14},{10,12},{12... | collective-permute-start | bytes 786440 | tf_op jit(solution)/shard_map/ppermute | solution.py:366
  227.2 7.8 %collective-permute-start.24 = (bf16[128,256]{1,0:T(8,128)(2,1)}, bf16[128,256]{1,0:T(8,128)(2,1)S(1)}, u32[]{:S(2)}, u32[]{:S(2)}) collective-permute-start(bf16[128,256]{1,0:T(8,128)(2,1)} %get-tuple-element.139), channel_id=1, source_target_pairs={{0,2},{2,0},{4,6},{6,4},{1,3},{3,1},{5,7},{7,5},{8,10},{10,8},{12,... | collective-permute-start | bytes 196616 | tf_op jit(solution)/shard_map/ppermute | solution.py:366
  256.8 13.6 %collective-permute-start.27 = (bf16[128,1024]{1,0:T(8,128)(2,1)S(1)}, bf16[128,1024]{1,0:T(8,128)(2,1)S(1)}, u32[]{:S(2)}, u32[]{:S(2)}) collective-permute-start(bf16[128,1024]{1,0:T(8,128)(2,1)S(1)} %copy-done.41), channel_id=1, source_target_pairs={{0,2},{2,0},{4,6},{6,4},{1,3},{3,1},{5,7},{7,5},{8,10},{10,8},{12,... | collective-permute-start | bytes 786440 | tf_op jit(solution)/shard_map/ppermute | solution.py:366
  258.1 21.3 %collective-permute-start.28 = (bf16[128,1024]{1,0:T(8,128)(2,1)S(1)}, bf16[128,1024]{1,0:T(8,128)(2,1)S(1)}, u32[]{:S(2)}, u32[]{:S(2)}) collective-permute-start(bf16[128,1024]{1,0:T(8,128)(2,1)S(1)} %copy-done.40), channel_id=1, source_target_pairs={{0,4},{2,6},{4,0},{6,2},{1,5},{3,7},{5,1},{7,3},{8,12},{10,14},{12... | collective-permute-start | bytes 786440 | tf_op jit(solution)/shard_map/ppermute | solution.py:366
  259.8 19.6 %collective-permute-start.29 = (bf16[128,1024]{1,0:T(8,128)(2,1)S(1)}, bf16[128,1024]{1,0:T(8,128)(2,1)S(1)}, u32[]{:S(2)}, u32[]{:S(2)}) collective-permute-start(bf16[128,1024]{1,0:T(8,128)(2,1)S(1)} %copy-done.39), channel_id=1, source_target_pairs={{0,6},{2,4},{4,2},{6,0},{1,7},{3,5},{5,3},{7,1},{8,14},{10,12},{12... | collective-permute-start | bytes 786440 | tf_op jit(solution)/shard_map/ppermute | solution.py:366
  264.9 14.6 %collective-permute-start.32 = (bf16[128,1024]{1,0:T(8,128)(2,1)}, bf16[128,1024]{1,0:T(8,128)(2,1)S(1)}, u32[]{:S(2)}, u32[]{:S(2)}) collective-permute-start(bf16[128,1024]{1,0:T(8,128)(2,1)} %get-tuple-element.168), channel_id=1, source_target_pairs={{0,8},{8,0},{16,24},{24,16},{1,9},{9,1},{17,25},{25,17},{2,10},{10... | collective-permute-start | bytes 786440 | tf_op jit(solution)/shard_map/ppermute | solution.py:366
  266.4 13.4 %collective-permute-start.33 = (bf16[128,1024]{1,0:T(8,128)(2,1)}, bf16[128,1024]{1,0:T(8,128)(2,1)S(1)}, u32[]{:S(2)}, u32[]{:S(2)}) collective-permute-start(bf16[128,1024]{1,0:T(8,128)(2,1)} %get-tuple-element.169), channel_id=1, source_target_pairs={{0,16},{8,24},{16,0},{24,8},{1,17},{9,25},{17,1},{25,9},{2,18},{10... | collective-permute-start | bytes 786440 | tf_op jit(solution)/shard_map/ppermute | solution.py:366
  270.4 9.3 %collective-permute-start.34 = (bf16[128,1024]{1,0:T(8,128)(2,1)}, bf16[128,1024]{1,0:T(8,128)(2,1)S(1)}, u32[]{:S(2)}, u32[]{:S(2)}) collective-permute-start(bf16[128,1024]{1,0:T(8,128)(2,1)} %get-tuple-element.170), channel_id=1, source_target_pairs={{0,24},{8,16},{16,8},{24,0},{1,25},{9,17},{17,9},{25,1},{2,26},{10... | collective-permute-start | bytes 786440 | tf_op jit(solution)/shard_map/ppermute | solution.py:366
  283.0 18.9 %collective-permute-start.35 = (bf16[32,3072]{1,0:T(8,128)(2,1)}, bf16[32,3072]{1,0:T(8,128)(2,1)S(1)}, u32[]{:S(2)}, u32[]{:S(2)}) collective-permute-start(bf16[32,3072]{1,0:T(8,128)(2,1)} %get-tuple-element.172), channel_id=1, source_target_pairs={{0,2},{2,0},{4,6},{6,4},{1,3},{3,1},{5,7},{7,5},{8,10},{10,8},{12,... | collective-permute-start | bytes 589832 | tf_op jit(solution)/shard_map/ppermute | solution.py:366
  288.3 20.3 %collective-permute-start.39 = (bf16[32,3072]{1,0:T(8,128)(2,1)}, bf16[32,3072]{1,0:T(8,128)(2,1)S(1)}, u32[]{:S(2)}, u32[]{:S(2)}) collective-permute-start(bf16[32,3072]{1,0:T(8,128)(2,1)} %get-tuple-element.181), channel_id=1, source_target_pairs={{0,4},{2,6},{4,0},{6,2},{1,5},{3,7},{5,1},{7,3},{8,12},{10,14},{12... | collective-permute-start | bytes 589832 | tf_op jit(solution)/shard_map/ppermute | solution.py:366
  288.8 19.9 %collective-permute-start.40 = (bf16[32,3072]{1,0:T(8,128)(2,1)}, bf16[32,3072]{1,0:T(8,128)(2,1)S(1)}, u32[]{:S(2)}, u32[]{:S(2)}) collective-permute-start(bf16[32,3072]{1,0:T(8,128)(2,1)} %get-tuple-element.182), channel_id=1, source_target_pairs={{0,6},{2,4},{4,2},{6,0},{1,7},{3,5},{5,3},{7,1},{8,14},{10,12},{12... | collective-permute-start | bytes 589832 | tf_op jit(solution)/shard_map/ppermute | solution.py:366
  (65 other events, 268.6 us)
Sparse Core Ops, SparseCore 0:
  23.6 24.0 all-gather.2
  49.7 54.3 all-gather.4
  195.0 63.5 reduce-scatter.4
  262.2 39.6 reduce-scatter.2

commit v2 on v1

--- a/solution.py
+++ b/solution.py
@@ -850,6 +850,34 @@
         d_att_parts, (dh_low, d_x_direct, g_alpha_attn) = outs[:nline], outs[nline:]
         d_att = exchange(d_att_parts, line, nline)
 
+        def outer_out(rk, dh, *refs):
+            parts, outs, (g_ref, sems) = refs[:nline], refs[nline : nline + 2], refs[nline + 2 :]
+            for k in range(nline):
+                spot = pl.ds(pl.multiple_of((rk[6] ^ k) * hc, hc), hc)
+                own = parts[k][k * tk : (k + 1) * tk, :]
+                g_ref[spot, :] = tdot(own, dh[...]).astype(BF)
+            copies = []
+            for cr in range(nc):
+                for a in range(nyx):
+                    for b in range(nline):
+                        row = ((rk[5] ^ a) * nline + (rk[6] ^ b)) * nc + (rk[4] ^ cr)
+                        src = g_ref.at[pl.ds(pl.multiple_of(row * rows, 32), rows)]
+                        dst = outs[cr].at[pl.ds((a * nline + b) * rows, rows)]
+                        copies.append(pltpu.make_async_copy(src, dst, sems.at[len(copies)]))
+            for copy in copies:
+                copy.start()
+            for copy in copies:
+                copy.wait()
+
+        keep, send = call(
+            outer_out,
+            [((dm // nc, dm), BF)] * nc,
+            (ranks, dh_low, *att_got),
+            hbm_out=(0, 1),
+            scratch=[pltpu.VMEM((dm, dm), BF), pltpu.SemaphoreType.DMA((ndev,))],
+            flops=2 * tk * dm * dm,
+        )
+
         def attn_back(rk, late, *refs):
             d_refs, refs = refs[:nline], refs[nline:]
             w_ref, rq_ref, rk_ref, q_ref, k_ref, v_ref, bias_ref, cs_ref, gain = refs[:9]
@@ -909,34 +937,6 @@
 
         wide = 3 * hc + ffb
 
-        def outer_out(rk, dh, *refs):
-            parts, outs, (g_ref, sems) = refs[:nline], refs[nline : nline + 2], refs[nline + 2 :]
-            for k in range(nline):
-                spot = pl.ds(pl.multiple_of((rk[6] ^ k) * hc, hc), hc)
-                own = parts[k][k * tk : (k + 1) * tk, :]
-                g_ref[spot, :] = tdot(own, dh[...]).astype(BF)
-            copies = []
-            for cr in range(nc):
-                for a in range(nyx):
-                    for b in range(nline):
-                        row = ((rk[5] ^ a) * nline + (rk[6] ^ b)) * nc + (rk[4] ^ cr)
-                        src = g_ref.at[pl.ds(pl.multiple_of(row * rows, 32), rows)]
-                        dst = outs[cr].at[pl.ds((a * nline + b) * rows, rows)]
-                        copies.append(pltpu.make_async_copy(src, dst, sems.at[len(copies)]))
-            for copy in copies:
-                copy.start()
-            for copy in copies:
-                copy.wait()
-
-        keep, send = call(
-            outer_out,
-            [((dm // nc, dm), BF)] * nc,
-            (ranks, dh_low, *att_got),
-            hbm_out=(0, 1),
-            scratch=[pltpu.VMEM((dm, dm), BF), pltpu.SemaphoreType.DMA((ndev,))],
-            flops=2 * tk * dm * dm,
-        )
-
         def core_add(rk, a, b, *outs):
             for i in range(nyx):
                 here = slice(i * ffb, (i + 1) * ffb)
@@ -999,6 +999,7 @@
             + (x_all, vecs),
             hbm=late_back,
             hbm_out=(nline,),
+            after=(keep,),
             scratch=[
                 pltpu.VMEM((nt, 3 * hc), BF), pltpu.VMEM((1, hc), F32),
                 pltpu.VMEM((nt, hc), BF), pltpu.VMEM((nt, hc), F32), pltpu.VMEM((nt, hc), F32),

time: 324 us -> 324 us (level)
    unnamed x105 -> x107, local copies, waits for them, and re-layouts: 12.5 us -> 13.7 us
  transfers between devices with their start and end apart: 45 -> 45, of which waited for: 24 -> 22; matrix products, arithmetic and copies ran while one was open for 2% -> 2% of each run, Pallas kernels for 18% -> 18%
where the time goes in v2:
time: 324 us; the launch traced here: 323 us
  waiting for transfers between devices  121 us (37%)
  Pallas kernels  95.5 us (29%)
  starting transfers between devices  72 us (22%)
  local copies, waits for them, and re-layouts  16.9 us (5%)
  between operations  14.2 us (4%)
  other arithmetic  3.41 us (1%)
    ppermute x41, waiting for transfers between devices, swap(): return lax.ppermute(value, axes, [(i, i ^ k) for i in range(count)])  115 us
    pallas_call x22, Pallas kernels, call(): pl.pallas_call(run, out_shape=[jax.ShapeDtypeStruct(s, d) for s, d in out...  95.5 us
    ppermute x41, starting transfers between devices, swap(): return lax.ppermute(value, axes, [(i, i ^ k) for i in range(count)])  71.9 us
    unnamed x107, local copies, waits for them, and re-layouts  13.7 us
  transfers between devices with their start and end apart: 45, of which 22 were waited for; matrix products, arithmetic and copies ran while one was open for 2% of the time, Pallas kernels for 18%

profile of v2, /device:TPU:0, one launch (start us, length us, event | category | flops | bytes accessed | tf_op | source)
XLA Modules:
  0.0 323.2 jit_solution(8145950460339780766)
XLA Ops:
  9.6 3.0 collective-permute-start.4
  12.6 2.6 collective-permute-start.5
  15.2 3.5 %collective-permute-done.5.refs_3_ = bf16[32,768]{1,0:T(8,128)(2,1)S(1)} collective-permute-done((bf16[32,768]{1,0:T(8,128)(2,1)}, bf16[32,768]{1,0:T(8,128)(2,1)S(1)}, u32[]{:S(2)}, u32[]{:S(2)}) %collective-permute-start.5) | collective-permute-done | bytes 49184 | tf_op jit(solution)/shard_map/ppermute | solution.py:366
  30.1 3.1 collective-permute-start.12
  38.0 7.3 %collective-permute-done.11.refs_3_ = bf16[32,3072]{1,0:T(8,128)(2,1)S(1)} collective-permute-done((bf16[32,3072]{1,0:T(8,128)(2,1)}, bf16[32,3072]{1,0:T(8,128)(2,1)S(1)}, u32[]{:S(2)}, u32[]{:S(2)}) %collective-permute-start.11) | collective-permute-done | bytes 196640 | tf_op jit(solution)/shard_map/ppermute | solution.py:366
  48.6 3.0 collective-permute-start.1
  56.9 5.3 %collective-permute-done.1.refs_2_ = bf16[144,1024]{1,0:T(8,128)(2,1)S(1)} collective-permute-done((bf16[144,1024]{1,0:T(8,128)(2,1)S(1)}, bf16[144,1024]{1,0:T(8,128)(2,1)S(1)}, u32[]{:S(2)}, u32[]{:S(2)}) %collective-permute-start.1) | collective-permute-done | bytes 294944 | tf_op jit(solution)/shard_map/ppermute | solution.py:366
  62.2 12.3 %collective-permute-done.2.refs_3_ = bf16[144,1024]{1,0:T(8,128)(2,1)S(1)} collective-permute-done((bf16[144,1024]{1,0:T(8,128)(2,1)S(1)}, bf16[144,1024]{1,0:T(8,128)(2,1)S(1)}, u32[]{:S(2)}, u32[]{:S(2)}) %collective-permute-start.2) | collective-permute-done | bytes 294944 | tf_op jit(solution)/shard_map/ppermute | solution.py:366
  75.2 9.1 %shard_map.259 = (bf16[512,256]{1,0:T(8,128)(2,1)}, bf16[512,1024]{1,0:T(8,128)(2,1)}, bf16[1024,768]{1,0:T(8,128)(2,1)}, f32[512,256]{1,0:T(8,128)}, f32[512,25...) custom-call(s32[7]{0:T(128)} %stack.39.refs_0_, ...), custom_call_target="tpu_custom_call" | custom-call | flops 1073741824 | bytes 9831452 | tf_op jit(solution)/shard_map/pallas_call | solution.py:339
  84.4 4.3 %collective-permute-start.7 = (bf16[512,256]{1,0:T(8,128)(2,1)}, bf16[512,256]{1,0:T(8,128)(2,1)S(1)}, u32[]{:S(2)}, u32[]{:S(2)}) collective-permute-start(bf16[512,256]{1,0:T(8,128)(2,1)} %get-tuple-element.110.refs_1_.refs_2_), channel_id=1, source_target_pairs={{0,2},{2,0},{4,6},{6,4},{1,3},{3,1},{5,7},{7,5},{8,10},{10,8},{12,... | collective-permute-start | bytes 786440 | tf_op jit(solution)/shard_map/ppermute | solution.py:366
  91.2 6.9 %collective-permute-done.7.refs_2_.refs_3_ = bf16[512,256]{1,0:T(8,128)(2,1)S(1)} collective-permute-done((bf16[512,256]{1,0:T(8,128)(2,1)}, bf16[512,256]{1,0:T(8,128)(2,1)S(1)}, u32[]{:S(2)}, u32[]{:S(2)}) %collective-permute-start.7) | collective-permute-done | bytes 262176 | tf_op jit(solution)/shard_map/ppermute | solution.py:366
  98.1 10.4 %collective-permute-done.8.refs_3_.refs_4_ = bf16[512,256]{1,0:T(8,128)(2,1)S(1)} collective-permute-done((bf16[512,256]{1,0:T(8,128)(2,1)}, bf16[512,256]{1,0:T(8,128)(2,1)S(1)}, u32[]{:S(2)}, u32[]{:S(2)}) %collective-permute-start.8) | collective-permute-done | bytes 262176 | tf_op jit(solution)/shard_map/ppermute | solution.py:366
  109.3 12.1 %shard_map.261 = (f32[128,1024]{1,0:T(8,128)}, bf16[128,1024]{1,0:T(8,128)(2,1)}, bf16[128,1024]{1,0:T(8,128)(2,1)}, bf16[128,1024]{1,0:T(8,128)(2,1)}, bf16[512...) custom-call(s32[7]{0:T(128)} %stack.39.refs_0_, ...), custom_call_target="tpu_custom_call" | custom-call | flops 4294967296 | bytes 17051676 | tf_op jit(solution)/shard_map/pallas_call | solution.py:339
  121.4 5.1 %collective-permute-start.13 = (bf16[128,1024]{1,0:T(8,128)(2,1)}, bf16[128,1024]{1,0:T(8,128)(2,1)S(1)}, u32[]{:S(2)}, u32[]{:S(2)}) collective-permute-start(bf16[128,1024]{1,0:T(8,128)(2,1)} %get-tuple-element.119), channel_id=1, source_target_pairs={{0,2},{2,0},{4,6},{6,4},{1,3},{3,1},{5,7},{7,5},{8,10},{10,8},{12,... | collective-permute-start | bytes 786440 | tf_op jit(solution)/shard_map/ppermute | solution.py:366
  132.2 3.6 %collective-permute-done.13.refs_2_ = bf16[128,1024]{1,0:T(8,128)(2,1)S(1)} collective-permute-done((bf16[128,1024]{1,0:T(8,128)(2,1)}, bf16[128,1024]{1,0:T(8,128)(2,1)S(1)}, u32[]{:S(2)}, u32[]{:S(2)}) %collective-permute-start.13) | collective-permute-done | bytes 262176 | tf_op jit(solution)/shard_map/ppermute | solution.py:366
  135.8 12.0 %collective-permute-done.14.refs_3_ = bf16[128,1024]{1,0:T(8,128)(2,1)S(1)} collective-permute-done((bf16[128,1024]{1,0:T(8,128)(2,1)}, bf16[128,1024]{1,0:T(8,128)(2,1)S(1)}, u32[]{:S(2)}, u32[]{:S(2)}) %collective-permute-start.14) | collective-permute-done | bytes 262176 | tf_op jit(solution)/shard_map/ppermute | solution.py:366
  148.6 3.0 shard_map.263
  151.6 4.2 %collective-permute-start.18 = (bf16[128,1024]{1,0:T(8,128)(2,1)}, bf16[128,1024]{1,0:T(8,128)(2,1)S(1)}, u32[]{:S(2)}, u32[]{:S(2)}) collective-permute-start(bf16[128,1024]{1,0:T(8,128)(2,1)} %get-tuple-element.127.refs_1_), channel_id=1, source_target_pairs={{0,2},{2,0},{4,6},{6,4},{1,3},{3,1},{5,7},{7,5},{8,10},{10,8},{12,... | collective-permute-start | bytes 786440 | tf_op jit(solution)/shard_map/ppermute | solution.py:366
  158.2 6.5 %collective-permute-done.18.refs_2_ = bf16[128,1024]{1,0:T(8,128)(2,1)S(1)} collective-permute-done((bf16[128,1024]{1,0:T(8,128)(2,1)}, bf16[128,1024]{1,0:T(8,128)(2,1)S(1)}, u32[]{:S(2)}, u32[]{:S(2)}) %collective-permute-start.18) | collective-permute-done | bytes 262176 | tf_op jit(solution)/shard_map/ppermute | solution.py:366
  164.7 11.5 %collective-permute-done.19.refs_3_ = bf16[128,1024]{1,0:T(8,128)(2,1)S(1)} collective-permute-done((bf16[128,1024]{1,0:T(8,128)(2,1)}, bf16[128,1024]{1,0:T(8,128)(2,1)S(1)}, u32[]{:S(2)}, u32[]{:S(2)}) %collective-permute-start.19) | collective-permute-done | bytes 262176 | tf_op jit(solution)/shard_map/ppermute | solution.py:366
  177.0 17.8 %shard_map.265 = (f32[128,1024]{1,0:T(8,128)}, bf16[128,1024]{1,0:T(8,128)(2,1)}, bf16[128,1024]{1,0:T(8,128)(2,1)}, bf16[128,1024]{1,0:T(8,128)(2,1)}, f32[1,10...) custom-call(s32[7]{0:T(128)} %stack.39.refs_0_, bf16[128,1024]{1,0:T(8,128)(2,1)} %get-tuple-element.127.refs_1_, ...), custom_call_target="tpu_custom_call" | custom-call | flops 6442450944 | bytes 21250076 | tf_op jit(solution)/shard_map/pallas_call | solution.py:339
  195.8 4.2 %collective-permute-start.21 = (bf16[128,1024]{1,0:T(8,128)(2,1)S(1)}, bf16[128,1024]{1,0:T(8,128)(2,1)S(1)}, u32[]{:S(2)}, u32[]{:S(2)}) collective-permute-start(bf16[128,1024]{1,0:T(8,128)(2,1)S(1)} %copy-done.45), channel_id=1, source_target_pairs={{0,2},{2,0},{4,6},{6,4},{1,3},{3,1},{5,7},{7,5},{8,10},{10,8},{12,... | collective-permute-start | bytes 786440 | tf_op jit(solution)/shard_map/ppermute | solution.py:366
  202.6 6.0 %collective-permute-done.21.refs_2_ = bf16[128,1024]{1,0:T(8,128)(2,1)S(1)} collective-permute-done((bf16[128,1024]{1,0:T(8,128)(2,1)S(1)}, bf16[128,1024]{1,0:T(8,128)(2,1)S(1)}, u32[]{:S(2)}, u32[]{:S(2)}) %collective-permute-start.21) | collective-permute-done | bytes 262176 | tf_op jit(solution)/shard_map/ppermute | solution.py:366
  208.7 11.4 %collective-permute-done.22.refs_3_ = bf16[128,1024]{1,0:T(8,128)(2,1)S(1)} collective-permute-done((bf16[128,1024]{1,0:T(8,128)(2,1)S(1)}, bf16[128,1024]{1,0:T(8,128)(2,1)S(1)}, u32[]{:S(2)}, u32[]{:S(2)}) %collective-permute-start.22) | collective-permute-done | bytes 262176 | tf_op jit(solution)/shard_map/ppermute | solution.py:366
  220.9 5.5 %shard_map.266 = (bf16[128,256]{1,0:T(8,128)(2,1)}, bf16[128,256]{1,0:T(8,128)(2,1)}, bf16[128,256]{1,0:T(8,128)(2,1)}, bf16[128,256]{1,0:T(8,128)(2,1)}, bf16[1...) custom-call(s32[7]{0:T(128)} %stack.39.refs_0_, f32[128,1024]{1,0:T(8,128)} %get-tuple-element.132.refs_1_, ...), custom_call_target="tpu_custom_call" | custom-call | flops 268435456 | bytes 12623900 | tf_op jit(solution)/shard_map/pallas_call | solution.py:339
  227.1 4.0 %collective-permute-start.24 = (bf16[128,256]{1,0:T(8,128)(2,1)}, bf16[128,256]{1,0:T(8,128)(2,1)S(1)}, u32[]{:S(2)}, u32[]{:S(2)}) collective-permute-start(bf16[128,256]{1,0:T(8,128)(2,1)} %get-tuple-element.139), channel_id=1, source_target_pairs={{0,2},{2,0},{4,6},{6,4},{1,3},{3,1},{5,7},{7,5},{8,10},{10,8},{12,... | collective-permute-start | bytes 196616 | tf_op jit(solution)/shard_map/ppermute | solution.py:366
  234.4 3.6 %shard_map.267 = (bf16[512,1024]{1,0:T(8,128)(2,1)}, bf16[512,1024]{1,0:T(8,128)(2,1)}) custom-call(s32[7]{0:T(128)} %stack.39.refs_0_, bf16[128,1024]{1,0:T(8,128)(2,1)} %get-tuple-element.156.refs_1_, bf16[512,256]{1,0:T(8,128)(2,1)} %get-tuple-element.110.refs_1_.refs_2_, bf16[512,256]{1,0:T(8,128)(2,1)} %copy-done.6, bf16[512,256]{1,0:T(8,128)(2,1)} %copy-done.7, ...), custom_call_target="tpu_custom_call" | custom-call | flops 268435456 | bytes 3407900 | tf_op jit(solution)/shard_map/pallas_call | solution.py:339
  238.8 14.7 %shard_map.268 = (f32[128,1024]{1,0:T(8,128)}, bf16[128,1024]{1,0:T(8,128)(2,1)}, bf16[128,1024]{1,0:T(8,128)(2,1)}, bf16[128,1024]{1,0:T(8,128)(2,1)}, bf16[1024,896]{1,0:T(8,128)(2,1)}) custom-call(s32[7]{0:T(128)} %stack.39.refs_0_, bf16[128,256]{1,0:T(8,128)(2,1)} %get-tuple-element.138.refs_1_, bf16[128,256]{1,0:T(8,128)(2,1)} %copy-done.50, ...), custom_call_target="tpu_custom_call" | custom-call | flops 2281701376 | bytes 9962524 | tf_op jit(solution)/shard_map/pallas_call | solution.py:339
  260.2 2.6 shard_map.271
  270.5 6.7 %collective-permute-done.28.refs_3_.refs_7_ = bf16[128,1024]{1,0:T(8,128)(2,1)S(1)} collective-permute-done((bf16[128,1024]{1,0:T(8,128)(2,1)S(1)}, bf16[128,1024]{1,0:T(8,128)(2,1)S(1)}, u32[]{:S(2)}, u32[]{:S(2)}) %collective-permute-start.28) | collective-permute-done | bytes 262176 | tf_op jit(solution)/shard_map/ppermute | solution.py:366
  281.0 5.2 %collective-permute-start.35 = (bf16[32,3072]{1,0:T(8,128)(2,1)}, bf16[32,3072]{1,0:T(8,128)(2,1)S(1)}, u32[]{:S(2)}, u32[]{:S(2)}) collective-permute-start(bf16[32,3072]{1,0:T(8,128)(2,1)} %get-tuple-element.172), channel_id=1, source_target_pairs={{0,2},{2,0},{4,6},{6,4},{1,3},{3,1},{5,7},{7,5},{8,10},{10,8},{12,... | collective-permute-start | bytes 589832 | tf_op jit(solution)/shard_map/ppermute | solution.py:366
  296.2 5.7 %reduce-scatter.3.cloned.1.call-done.refs_1_ = bf16[128,896]{1,0:T(8,128)(2,1)} async-done(((bf16[1024,896]{1,0:T(8,128)(2,1)}), bf16[128,896]{1,0:T(8,128)(2,1)}) %reduce-scatter.3.cloned.1.call-update) | async-done | bytes 229392 | tf_op jit(solution)/shard_map/reduce_scatter | solution.py:1014
  (212 shorter events, 92.7 us)
Async XLA Ops:
  7.2 67.3 %all-gather.3.cloned.1.call-start = ((), (), s32[]{:S(2)}) async-start(), calls=%async_computation.2 | async-start | bytes 1769472 | tf_op jit(solution)/shard_map/all_gather | solution.py:461
  23.5 85.0 %all-gather.5.cloned.1.call-start = ((), (), s32[]{:S(2)}) async-start(), calls=%async_computation.3 | async-start | bytes 9437184 | tf_op jit(solution)/shard_map/all_gather | solution.py:475
  28.8 9.2 %collective-permute-start.10 = (bf16[32,3072]{1,0:T(8,128)(2,1)}, bf16[32,3072]{1,0:T(8,128)(2,1)S(1)}, u32[]{:S(2)}, u32[]{:S(2)}) collective-permute-start(bf16[32,3072]{1,0:T(8,128)(2,1)} %get-tuple-element.113), channel_id=1, source_target_pairs={{0,2},{2,0},{4,6},{6,4},{1,3},{3,1},{5,7},{7,5},{8,10},{10,8},{12,... | collective-permute-start | bytes 589832 | tf_op jit(solution)/shard_map/ppermute | solution.py:366
  28.8 16.4 %collective-permute-start.11 = (bf16[32,3072]{1,0:T(8,128)(2,1)}, bf16[32,3072]{1,0:T(8,128)(2,1)S(1)}, u32[]{:S(2)}, u32[]{:S(2)}) collective-permute-start(bf16[32,3072]{1,0:T(8,128)(2,1)} %get-tuple-element.114), channel_id=1, source_target_pairs={{0,4},{2,6},{4,0},{6,2},{1,5},{3,7},{5,1},{7,3},{8,12},{10,14},{12... | collective-permute-start | bytes 589832 | tf_op jit(solution)/shard_map/ppermute | solution.py:366
  30.1 15.1 %collective-permute-start.12 = (bf16[32,3072]{1,0:T(8,128)(2,1)}, bf16[32,3072]{1,0:T(8,128)(2,1)S(1)}, u32[]{:S(2)}, u32[]{:S(2)}) collective-permute-start(bf16[32,3072]{1,0:T(8,128)(2,1)} %get-tuple-element.115), channel_id=1, source_target_pairs={{0,6},{2,4},{4,2},{6,0},{1,7},{3,5},{5,3},{7,1},{8,14},{10,12},{12... | collective-permute-start | bytes 589832 | tf_op jit(solution)/shard_map/ppermute | solution.py:366
  48.5 229.2 %reduce-scatter.5.cloned.1.call-start = ((), (), s32[]{:S(2)}) async-start(), calls=%async_computation.5 | async-start | bytes 7077888 | tf_op jit(solution)/shard_map/reduce_scatter | solution.py:815
  48.6 13.6 %collective-permute-start.1 = (bf16[144,1024]{1,0:T(8,128)(2,1)S(1)}, bf16[144,1024]{1,0:T(8,128)(2,1)S(1)}, u32[]{:S(2)}, u32[]{:S(2)}) collective-permute-start(bf16[144,1024]{1,0:T(8,128)(2,1)S(1)} %copy-done), channel_id=1, source_target_pairs={{0,2},{2,0},{4,6},{6,4},{1,3},{3,1},{5,7},{7,5},{8,10},{10,8},{12,... | collective-permute-start | bytes 884744 | tf_op jit(solution)/shard_map/ppermute | solution.py:366
  51.6 22.8 %collective-permute-start.2 = (bf16[144,1024]{1,0:T(8,128)(2,1)S(1)}, bf16[144,1024]{1,0:T(8,128)(2,1)S(1)}, u32[]{:S(2)}, u32[]{:S(2)}) collective-permute-start(bf16[144,1024]{1,0:T(8,128)(2,1)S(1)} %copy-done), channel_id=1, source_target_pairs={{0,4},{2,6},{4,0},{6,2},{1,5},{3,7},{5,1},{7,3},{8,12},{10,14},{12... | collective-permute-start | bytes 884744 | tf_op jit(solution)/shard_map/ppermute | solution.py:366
  51.7 22.8 %collective-permute-start.3 = (bf16[144,1024]{1,0:T(8,128)(2,1)S(1)}, bf16[144,1024]{1,0:T(8,128)(2,1)S(1)}, u32[]{:S(2)}, u32[]{:S(2)}) collective-permute-start(bf16[144,1024]{1,0:T(8,128)(2,1)S(1)} %copy-done), channel_id=1, source_target_pairs={{0,6},{2,4},{4,2},{6,0},{1,7},{3,5},{5,3},{7,1},{8,14},{10,12},{12... | collective-permute-start | bytes 884744 | tf_op jit(solution)/shard_map/ppermute | solution.py:366
  84.4 13.7 %collective-permute-start.7 = (bf16[512,256]{1,0:T(8,128)(2,1)}, bf16[512,256]{1,0:T(8,128)(2,1)S(1)}, u32[]{:S(2)}, u32[]{:S(2)}) collective-permute-start(bf16[512,256]{1,0:T(8,128)(2,1)} %get-tuple-element.110.refs_1_.refs_2_), channel_id=1, source_target_pairs={{0,2},{2,0},{4,6},{6,4},{1,3},{3,1},{5,7},{7,5},{8,10},{10,8},{12,... | collective-permute-start | bytes 786440 | tf_op jit(solution)/shard_map/ppermute | solution.py:366
  88.7 19.8 %collective-permute-start.8 = (bf16[512,256]{1,0:T(8,128)(2,1)}, bf16[512,256]{1,0:T(8,128)(2,1)S(1)}, u32[]{:S(2)}, u32[]{:S(2)}) collective-permute-start(bf16[512,256]{1,0:T(8,128)(2,1)} %get-tuple-element.110.refs_1_.refs_2_), channel_id=1, source_target_pairs={{0,4},{2,6},{4,0},{6,2},{1,5},{3,7},{5,1},{7,3},{8,12},{10,14},{12... | collective-permute-start | bytes 786440 | tf_op jit(solution)/shard_map/ppermute | solution.py:366
  88.7 19.8 %collective-permute-start.9 = (bf16[512,256]{1,0:T(8,128)(2,1)}, bf16[512,256]{1,0:T(8,128)(2,1)S(1)}, u32[]{:S(2)}, u32[]{:S(2)}) collective-permute-start(bf16[512,256]{1,0:T(8,128)(2,1)} %get-tuple-element.110.refs_1_.refs_2_), channel_id=1, source_target_pairs={{0,6},{2,4},{4,2},{6,0},{1,7},{3,5},{5,3},{7,1},{8,14},{10,12},{12... | collective-permute-start | bytes 786440 | tf_op jit(solution)/shard_map/ppermute | solution.py:366
  121.4 14.4 %collective-permute-start.13 = (bf16[128,1024]{1,0:T(8,128)(2,1)}, bf16[128,1024]{1,0:T(8,128)(2,1)S(1)}, u32[]{:S(2)}, u32[]{:S(2)}) collective-permute-start(bf16[128,1024]{1,0:T(8,128)(2,1)} %get-tuple-element.119), channel_id=1, source_target_pairs={{0,2},{2,0},{4,6},{6,4},{1,3},{3,1},{5,7},{7,5},{8,10},{10,8},{12,... | collective-permute-start | bytes 786440 | tf_op jit(solution)/shard_map/ppermute | solution.py:366
  126.5 21.3 %collective-permute-start.14 = (bf16[128,1024]{1,0:T(8,128)(2,1)}, bf16[128,1024]{1,0:T(8,128)(2,1)S(1)}, u32[]{:S(2)}, u32[]{:S(2)}) collective-permute-start(bf16[128,1024]{1,0:T(8,128)(2,1)} %get-tuple-element.120), channel_id=1, source_target_pairs={{0,4},{2,6},{4,0},{6,2},{1,5},{3,7},{5,1},{7,3},{8,12},{10,14},{12... | collective-permute-start | bytes 786440 | tf_op jit(solution)/shard_map/ppermute | solution.py:366
  126.5 21.3 %collective-permute-start.15 = (bf16[128,1024]{1,0:T(8,128)(2,1)}, bf16[128,1024]{1,0:T(8,128)(2,1)S(1)}, u32[]{:S(2)}, u32[]{:S(2)}) collective-permute-start(bf16[128,1024]{1,0:T(8,128)(2,1)} %get-tuple-element.121), channel_id=1, source_target_pairs={{0,6},{2,4},{4,2},{6,0},{1,7},{3,5},{5,3},{7,1},{8,14},{10,12},{12... | collective-permute-start | bytes 786440 | tf_op jit(solution)/shard_map/ppermute | solution.py:366
  151.6 13.2 %collective-permute-start.18 = (bf16[128,1024]{1,0:T(8,128)(2,1)}, bf16[128,1024]{1,0:T(8,128)(2,1)S(1)}, u32[]{:S(2)}, u32[]{:S(2)}) collective-permute-start(bf16[128,1024]{1,0:T(8,128)(2,1)} %get-tuple-element.127.refs_1_), channel_id=1, source_target_pairs={{0,2},{2,0},{4,6},{6,4},{1,3},{3,1},{5,7},{7,5},{8,10},{10,8},{12,... | collective-permute-start | bytes 786440 | tf_op jit(solution)/shard_map/ppermute | solution.py:366
  155.8 20.4 %collective-permute-start.19 = (bf16[128,1024]{1,0:T(8,128)(2,1)}, bf16[128,1024]{1,0:T(8,128)(2,1)S(1)}, u32[]{:S(2)}, u32[]{:S(2)}) collective-permute-start(bf16[128,1024]{1,0:T(8,128)(2,1)} %get-tuple-element.127.refs_1_), channel_id=1, source_target_pairs={{0,4},{2,6},{4,0},{6,2},{1,5},{3,7},{5,1},{7,3},{8,12},{10,14},{12... | collective-permute-start | bytes 786440 | tf_op jit(solution)/shard_map/ppermute | solution.py:366
  155.8 20.4 %collective-permute-start.20 = (bf16[128,1024]{1,0:T(8,128)(2,1)}, bf16[128,1024]{1,0:T(8,128)(2,1)S(1)}, u32[]{:S(2)}, u32[]{:S(2)}) collective-permute-start(bf16[128,1024]{1,0:T(8,128)(2,1)} %get-tuple-element.127.refs_1_), channel_id=1, source_target_pairs={{0,6},{2,4},{4,2},{6,0},{1,7},{3,5},{5,3},{7,1},{8,14},{10,12},{12... | collective-permute-start | bytes 786440 | tf_op jit(solution)/shard_map/ppermute | solution.py:366
  194.9 107.0 %reduce-scatter.3.cloned.1.call-start = ((), (), s32[]{:S(2)}) async-start(), calls=%async_computation.4 | async-start | bytes 2064384 | tf_op jit(solution)/shard_map/reduce_scatter | solution.py:1014
  195.8 12.9 %collective-permute-start.21 = (bf16[128,1024]{1,0:T(8,128)(2,1)S(1)}, bf16[128,1024]{1,0:T(8,128)(2,1)S(1)}, u32[]{:S(2)}, u32[]{:S(2)}) collective-permute-start(bf16[128,1024]{1,0:T(8,128)(2,1)S(1)} %copy-done.45), channel_id=1, source_target_pairs={{0,2},{2,0},{4,6},{6,4},{1,3},{3,1},{5,7},{7,5},{8,10},{10,8},{12,... | collective-permute-start | bytes 786440 | tf_op jit(solution)/shard_map/ppermute | solution.py:366
  200.0 20.1 %collective-permute-start.22 = (bf16[128,1024]{1,0:T(8,128)(2,1)S(1)}, bf16[128,1024]{1,0:T(8,128)(2,1)S(1)}, u32[]{:S(2)}, u32[]{:S(2)}) collective-permute-start(bf16[128,1024]{1,0:T(8,128)(2,1)S(1)} %copy-done.44), channel_id=1, source_target_pairs={{0,4},{2,6},{4,0},{6,2},{1,5},{3,7},{5,1},{7,3},{8,12},{10,14},{12... | collective-permute-start | bytes 786440 | tf_op jit(solution)/shard_map/ppermute | solution.py:366
  200.0 20.1 %collective-permute-start.23 = (bf16[128,1024]{1,0:T(8,128)(2,1)S(1)}, bf16[128,1024]{1,0:T(8,128)(2,1)S(1)}, u32[]{:S(2)}, u32[]{:S(2)}) collective-permute-start(bf16[128,1024]{1,0:T(8,128)(2,1)S(1)} %copy-done.43), channel_id=1, source_target_pairs={{0,6},{2,4},{4,2},{6,0},{1,7},{3,5},{5,3},{7,1},{8,14},{10,12},{12... | collective-permute-start | bytes 786440 | tf_op jit(solution)/shard_map/ppermute | solution.py:366
  227.1 10.9 %collective-permute-start.24 = (bf16[128,256]{1,0:T(8,128)(2,1)}, bf16[128,256]{1,0:T(8,128)(2,1)S(1)}, u32[]{:S(2)}, u32[]{:S(2)}) collective-permute-start(bf16[128,256]{1,0:T(8,128)(2,1)} %get-tuple-element.139), channel_id=1, source_target_pairs={{0,2},{2,0},{4,6},{6,4},{1,3},{3,1},{5,7},{7,5},{8,10},{10,8},{12,... | collective-permute-start | bytes 196616 | tf_op jit(solution)/shard_map/ppermute | solution.py:366
  254.7 13.2 %collective-permute-start.27 = (bf16[128,1024]{1,0:T(8,128)(2,1)S(1)}, bf16[128,1024]{1,0:T(8,128)(2,1)S(1)}, u32[]{:S(2)}, u32[]{:S(2)}) collective-permute-start(bf16[128,1024]{1,0:T(8,128)(2,1)S(1)} %copy-done.42), channel_id=1, source_target_pairs={{0,2},{2,0},{4,6},{6,4},{1,3},{3,1},{5,7},{7,5},{8,10},{10,8},{12,... | collective-permute-start | bytes 786440 | tf_op jit(solution)/shard_map/ppermute | solution.py:366
  255.8 21.3 %collective-permute-start.28 = (bf16[128,1024]{1,0:T(8,128)(2,1)S(1)}, bf16[128,1024]{1,0:T(8,128)(2,1)S(1)}, u32[]{:S(2)}, u32[]{:S(2)}) collective-permute-start(bf16[128,1024]{1,0:T(8,128)(2,1)S(1)} %copy-done.41), channel_id=1, source_target_pairs={{0,4},{2,6},{4,0},{6,2},{1,5},{3,7},{5,1},{7,3},{8,12},{10,14},{12... | collective-permute-start | bytes 786440 | tf_op jit(solution)/shard_map/ppermute | solution.py:366
  257.2 19.9 %collective-permute-start.29 = (bf16[128,1024]{1,0:T(8,128)(2,1)S(1)}, bf16[128,1024]{1,0:T(8,128)(2,1)S(1)}, u32[]{:S(2)}, u32[]{:S(2)}) collective-permute-start(bf16[128,1024]{1,0:T(8,128)(2,1)S(1)} %copy-done.40), channel_id=1, source_target_pairs={{0,6},{2,4},{4,2},{6,0},{1,7},{3,5},{5,3},{7,1},{8,14},{10,12},{12... | collective-permute-start | bytes 786440 | tf_op jit(solution)/shard_map/ppermute | solution.py:366
  262.8 14.4 %collective-permute-start.32 = (bf16[128,1024]{1,0:T(8,128)(2,1)}, bf16[128,1024]{1,0:T(8,128)(2,1)S(1)}, u32[]{:S(2)}, u32[]{:S(2)}) collective-permute-start(bf16[128,1024]{1,0:T(8,128)(2,1)} %get-tuple-element.168), channel_id=1, source_target_pairs={{0,8},{8,0},{16,24},{24,16},{1,9},{9,1},{17,25},{25,17},{2,10},{10... | collective-permute-start | bytes 786440 | tf_op jit(solution)/shard_map/ppermute | solution.py:366
  264.3 13.4 %collective-permute-start.33 = (bf16[128,1024]{1,0:T(8,128)(2,1)}, bf16[128,1024]{1,0:T(8,128)(2,1)S(1)}, u32[]{:S(2)}, u32[]{:S(2)}) collective-permute-start(bf16[128,1024]{1,0:T(8,128)(2,1)} %get-tuple-element.169), channel_id=1, source_target_pairs={{0,16},{8,24},{16,0},{24,8},{1,17},{9,25},{17,1},{25,9},{2,18},{10... | collective-permute-start | bytes 786440 | tf_op jit(solution)/shard_map/ppermute | solution.py:366
  268.0 9.7 %collective-permute-start.34 = (bf16[128,1024]{1,0:T(8,128)(2,1)}, bf16[128,1024]{1,0:T(8,128)(2,1)S(1)}, u32[]{:S(2)}, u32[]{:S(2)}) collective-permute-start(bf16[128,1024]{1,0:T(8,128)(2,1)} %get-tuple-element.170), channel_id=1, source_target_pairs={{0,24},{8,16},{16,8},{24,0},{1,25},{9,17},{17,9},{25,1},{2,26},{10... | collective-permute-start | bytes 786440 | tf_op jit(solution)/shard_map/ppermute | solution.py:366
  281.0 20.9 %collective-permute-start.35 = (bf16[32,3072]{1,0:T(8,128)(2,1)}, bf16[32,3072]{1,0:T(8,128)(2,1)S(1)}, u32[]{:S(2)}, u32[]{:S(2)}) collective-permute-start(bf16[32,3072]{1,0:T(8,128)(2,1)} %get-tuple-element.172), channel_id=1, source_target_pairs={{0,2},{2,0},{4,6},{6,4},{1,3},{3,1},{5,7},{7,5},{8,10},{10,8},{12,... | collective-permute-start | bytes 589832 | tf_op jit(solution)/shard_map/ppermute | solution.py:366
  286.2 22.4 %collective-permute-start.39 = (bf16[32,3072]{1,0:T(8,128)(2,1)}, bf16[32,3072]{1,0:T(8,128)(2,1)S(1)}, u32[]{:S(2)}, u32[]{:S(2)}) collective-permute-start(bf16[32,3072]{1,0:T(8,128)(2,1)} %get-tuple-element.181), channel_id=1, source_target_pairs={{0,4},{2,6},{4,0},{6,2},{1,5},{3,7},{5,1},{7,3},{8,12},{10,14},{12... | collective-permute-start | bytes 589832 | tf_op jit(solution)/shard_map/ppermute | solution.py:366
  286.2 22.4 %collective-permute-start.40 = (bf16[32,3072]{1,0:T(8,128)(2,1)}, bf16[32,3072]{1,0:T(8,128)(2,1)S(1)}, u32[]{:S(2)}, u32[]{:S(2)}) collective-permute-start(bf16[32,3072]{1,0:T(8,128)(2,1)} %get-tuple-element.182), channel_id=1, source_target_pairs={{0,6},{2,4},{4,2},{6,0},{1,7},{3,5},{5,3},{7,1},{8,14},{10,12},{12... | collective-permute-start | bytes 589832 | tf_op jit(solution)/shard_map/ppermute | solution.py:366
  (66 other events, 260.8 us)
Sparse Core Ops, SparseCore 0:
  23.6 24.0 all-gather.2
  49.6 54.3 all-gather.4
  195.0 63.5 reduce-scatter.4
  262.2 39.6 reduce-scatter.2

commit v3 on v2

--- a/solution.py
+++ b/solution.py
@@ -387,7 +387,7 @@
         pad = 16
         ext = seg + pad
         scale = math.sqrt(HEAD_DIM)
-        tile = 256
+        tile = 512
 
         at = [lax.axis_index(a) for a in "yxwzc"]
         ranks = jnp.stack(at + [lax.axis_index(yx), lax.axis_index(line)])

time: 324 us -> 324 us (level)
  no operation moved by 1% of the time
where the time goes in v3:
time: 324 us; the launch traced here: 323 us
  waiting for transfers between devices  122 us (38%)
  Pallas kernels  94.5 us (29%)
  starting transfers between devices  72 us (22%)
  local copies, waits for them, and re-layouts  16.9 us (5%)
  between operations  14.2 us (4%)
  other arithmetic  3.41 us (1%)
    ppermute x41, waiting for transfers between devices, swap(): return lax.ppermute(value, axes, [(i, i ^ k) for i in range(count)])  115 us
    pallas_call x22, Pallas kernels, call(): pl.pallas_call(run, out_shape=[jax.ShapeDtypeStruct(s, d) for s, d in out...  94.5 us
    ppermute x41, starting transfers between devices, swap(): return lax.ppermute(value, axes, [(i, i ^ k) for i in range(count)])  71.8 us
    unnamed x107, local copies, waits for them, and re-layouts  13.6 us
    reduce_scatter x1, waiting for transfers between devices, body(): g_last = lax.psum_scatter(g_last, dpc, scatter_dimension=0, tiled=True)  6.59 us
  transfers between devices with their start and end apart: 45, of which 22 were waited for; matrix products, arithmetic and copies ran while one was open for 2% of the time, Pallas kernels for 18%

profile of v3, /device:TPU:0, one launch (start us, length us, event | category | flops | bytes accessed | tf_op | source)
XLA Modules:
  0.0 322.8 jit_solution(10598492664518588945)
XLA Ops:
  9.6 3.0 collective-permute-start.4
  12.6 2.6 collective-permute-start.5
  15.2 3.5 %collective-permute-done.5.refs_3_ = bf16[32,768]{1,0:T(8,128)(2,1)S(1)} collective-permute-done((bf16[32,768]{1,0:T(8,128)(2,1)}, bf16[32,768]{1,0:T(8,128)(2,1)S(1)}, u32[]{:S(2)}, u32[]{:S(2)}) %collective-permute-start.5) | collective-permute-done | bytes 49184 | tf_op jit(solution)/shard_map/ppermute | solution.py:366
  30.1 3.1 collective-permute-start.12
  38.0 7.3 %collective-permute-done.11.refs_3_ = bf16[32,3072]{1,0:T(8,128)(2,1)S(1)} collective-permute-done((bf16[32,3072]{1,0:T(8,128)(2,1)}, bf16[32,3072]{1,0:T(8,128)(2,1)S(1)}, u32[]{:S(2)}, u32[]{:S(2)}) %collective-permute-start.11) | collective-permute-done | bytes 196640 | tf_op jit(solution)/shard_map/ppermute | solution.py:366
  48.6 3.0 collective-permute-start.1
  56.9 5.3 %collective-permute-done.1.refs_2_ = bf16[144,1024]{1,0:T(8,128)(2,1)S(1)} collective-permute-done((bf16[144,1024]{1,0:T(8,128)(2,1)S(1)}, bf16[144,1024]{1,0:T(8,128)(2,1)S(1)}, u32[]{:S(2)}, u32[]{:S(2)}) %collective-permute-start.1) | collective-permute-done | bytes 294944 | tf_op jit(solution)/shard_map/ppermute | solution.py:366
  62.2 12.3 %collective-permute-done.2.refs_3_ = bf16[144,1024]{1,0:T(8,128)(2,1)S(1)} collective-permute-done((bf16[144,1024]{1,0:T(8,128)(2,1)S(1)}, bf16[144,1024]{1,0:T(8,128)(2,1)S(1)}, u32[]{:S(2)}, u32[]{:S(2)}) %collective-permute-start.2) | collective-permute-done | bytes 294944 | tf_op jit(solution)/shard_map/ppermute | solution.py:366
  75.2 9.1 %shard_map.259 = (bf16[512,256]{1,0:T(8,128)(2,1)}, bf16[512,1024]{1,0:T(8,128)(2,1)}, bf16[1024,768]{1,0:T(8,128)(2,1)}, f32[512,256]{1,0:T(8,128)}, f32[512,25...) custom-call(s32[7]{0:T(128)} %stack.39.refs_0_, ...), custom_call_target="tpu_custom_call" | custom-call | flops 1073741824 | bytes 9831452 | tf_op jit(solution)/shard_map/pallas_call | solution.py:339
  84.4 4.3 %collective-permute-start.7 = (bf16[512,256]{1,0:T(8,128)(2,1)}, bf16[512,256]{1,0:T(8,128)(2,1)S(1)}, u32[]{:S(2)}, u32[]{:S(2)}) collective-permute-start(bf16[512,256]{1,0:T(8,128)(2,1)} %get-tuple-element.110.refs_1_.refs_2_), channel_id=1, source_target_pairs={{0,2},{2,0},{4,6},{6,4},{1,3},{3,1},{5,7},{7,5},{8,10},{10,8},{12,... | collective-permute-start | bytes 786440 | tf_op jit(solution)/shard_map/ppermute | solution.py:366
  91.2 6.9 %collective-permute-done.7.refs_2_.refs_3_ = bf16[512,256]{1,0:T(8,128)(2,1)S(1)} collective-permute-done((bf16[512,256]{1,0:T(8,128)(2,1)}, bf16[512,256]{1,0:T(8,128)(2,1)S(1)}, u32[]{:S(2)}, u32[]{:S(2)}) %collective-permute-start.7) | collective-permute-done | bytes 262176 | tf_op jit(solution)/shard_map/ppermute | solution.py:366
  98.1 10.4 %collective-permute-done.8.refs_3_.refs_4_ = bf16[512,256]{1,0:T(8,128)(2,1)S(1)} collective-permute-done((bf16[512,256]{1,0:T(8,128)(2,1)}, bf16[512,256]{1,0:T(8,128)(2,1)S(1)}, u32[]{:S(2)}, u32[]{:S(2)}) %collective-permute-start.8) | collective-permute-done | bytes 262176 | tf_op jit(solution)/shard_map/ppermute | solution.py:366
  109.3 12.3 %shard_map.261 = (f32[128,1024]{1,0:T(8,128)}, bf16[128,1024]{1,0:T(8,128)(2,1)}, bf16[128,1024]{1,0:T(8,128)(2,1)}, bf16[128,1024]{1,0:T(8,128)(2,1)}, bf16[512...) custom-call(s32[7]{0:T(128)} %stack.39.refs_0_, ...), custom_call_target="tpu_custom_call" | custom-call | flops 4294967296 | bytes 17051676 | tf_op jit(solution)/shard_map/pallas_call | solution.py:339
  121.6 5.1 %collective-permute-start.13 = (bf16[128,1024]{1,0:T(8,128)(2,1)}, bf16[128,1024]{1,0:T(8,128)(2,1)S(1)}, u32[]{:S(2)}, u32[]{:S(2)}) collective-permute-start(bf16[128,1024]{1,0:T(8,128)(2,1)} %get-tuple-element.119), channel_id=1, source_target_pairs={{0,2},{2,0},{4,6},{6,4},{1,3},{3,1},{5,7},{7,5},{8,10},{10,8},{12,... | collective-permute-start | bytes 786440 | tf_op jit(solution)/shard_map/ppermute | solution.py:366
  132.4 3.6 %collective-permute-done.13.refs_2_ = bf16[128,1024]{1,0:T(8,128)(2,1)S(1)} collective-permute-done((bf16[128,1024]{1,0:T(8,128)(2,1)}, bf16[128,1024]{1,0:T(8,128)(2,1)S(1)}, u32[]{:S(2)}, u32[]{:S(2)}) %collective-permute-start.13) | collective-permute-done | bytes 262176 | tf_op jit(solution)/shard_map/ppermute | solution.py:366
  136.0 12.0 %collective-permute-done.14.refs_3_ = bf16[128,1024]{1,0:T(8,128)(2,1)S(1)} collective-permute-done((bf16[128,1024]{1,0:T(8,128)(2,1)}, bf16[128,1024]{1,0:T(8,128)(2,1)S(1)}, u32[]{:S(2)}, u32[]{:S(2)}) %collective-permute-start.14) | collective-permute-done | bytes 262176 | tf_op jit(solution)/shard_map/ppermute | solution.py:366
  148.8 3.0 shard_map.263
  151.7 4.2 %collective-permute-start.18 = (bf16[128,1024]{1,0:T(8,128)(2,1)}, bf16[128,1024]{1,0:T(8,128)(2,1)S(1)}, u32[]{:S(2)}, u32[]{:S(2)}) collective-permute-start(bf16[128,1024]{1,0:T(8,128)(2,1)} %get-tuple-element.127.refs_1_), channel_id=1, source_target_pairs={{0,2},{2,0},{4,6},{6,4},{1,3},{3,1},{5,7},{7,5},{8,10},{10,8},{12,... | collective-permute-start | bytes 786440 | tf_op jit(solution)/shard_map/ppermute | solution.py:366
  158.3 6.4 %collective-permute-done.18.refs_2_ = bf16[128,1024]{1,0:T(8,128)(2,1)S(1)} collective-permute-done((bf16[128,1024]{1,0:T(8,128)(2,1)}, bf16[128,1024]{1,0:T(8,128)(2,1)S(1)}, u32[]{:S(2)}, u32[]{:S(2)}) %collective-permute-start.18) | collective-permute-done | bytes 262176 | tf_op jit(solution)/shard_map/ppermute | solution.py:366
  164.8 11.5 %collective-permute-done.19.refs_3_ = bf16[128,1024]{1,0:T(8,128)(2,1)S(1)} collective-permute-done((bf16[128,1024]{1,0:T(8,128)(2,1)}, bf16[128,1024]{1,0:T(8,128)(2,1)S(1)}, u32[]{:S(2)}, u32[]{:S(2)}) %collective-permute-start.19) | collective-permute-done | bytes 262176 | tf_op jit(solution)/shard_map/ppermute | solution.py:366
  177.1 17.3 %shard_map.265 = (f32[128,1024]{1,0:T(8,128)}, bf16[128,1024]{1,0:T(8,128)(2,1)}, bf16[128,1024]{1,0:T(8,128)(2,1)}, bf16[128,1024]{1,0:T(8,128)(2,1)}, f32[1,10...) custom-call(s32[7]{0:T(128)} %stack.39.refs_0_, bf16[128,1024]{1,0:T(8,128)(2,1)} %get-tuple-element.127.refs_1_, ...), custom_call_target="tpu_custom_call" | custom-call | flops 6442450944 | bytes 21250076 | tf_op jit(solution)/shard_map/pallas_call | solution.py:339
  195.4 4.2 %collective-permute-start.21 = (bf16[128,1024]{1,0:T(8,128)(2,1)S(1)}, bf16[128,1024]{1,0:T(8,128)(2,1)S(1)}, u32[]{:S(2)}, u32[]{:S(2)}) collective-permute-start(bf16[128,1024]{1,0:T(8,128)(2,1)S(1)} %copy-done.45), channel_id=1, source_target_pairs={{0,2},{2,0},{4,6},{6,4},{1,3},{3,1},{5,7},{7,5},{8,10},{10,8},{12,... | collective-permute-start | bytes 786440 | tf_op jit(solution)/shard_map/ppermute | solution.py:366
  202.2 6.0 %collective-permute-done.21.refs_2_ = bf16[128,1024]{1,0:T(8,128)(2,1)S(1)} collective-permute-done((bf16[128,1024]{1,0:T(8,128)(2,1)S(1)}, bf16[128,1024]{1,0:T(8,128)(2,1)S(1)}, u32[]{:S(2)}, u32[]{:S(2)}) %collective-permute-start.21) | collective-permute-done | bytes 262176 | tf_op jit(solution)/shard_map/ppermute | solution.py:366
  208.2 11.5 %collective-permute-done.22.refs_3_ = bf16[128,1024]{1,0:T(8,128)(2,1)S(1)} collective-permute-done((bf16[128,1024]{1,0:T(8,128)(2,1)S(1)}, bf16[128,1024]{1,0:T(8,128)(2,1)S(1)}, u32[]{:S(2)}, u32[]{:S(2)}) %collective-permute-start.22) | collective-permute-done | bytes 262176 | tf_op jit(solution)/shard_map/ppermute | solution.py:366
  220.5 5.5 %shard_map.266 = (bf16[128,256]{1,0:T(8,128)(2,1)}, bf16[128,256]{1,0:T(8,128)(2,1)}, bf16[128,256]{1,0:T(8,128)(2,1)}, bf16[128,256]{1,0:T(8,128)(2,1)}, bf16[1...) custom-call(s32[7]{0:T(128)} %stack.39.refs_0_, f32[128,1024]{1,0:T(8,128)} %get-tuple-element.132.refs_1_, ...), custom_call_target="tpu_custom_call" | custom-call | flops 268435456 | bytes 12623900 | tf_op jit(solution)/shard_map/pallas_call | solution.py:339
  226.7 4.0 %collective-permute-start.24 = (bf16[128,256]{1,0:T(8,128)(2,1)}, bf16[128,256]{1,0:T(8,128)(2,1)S(1)}, u32[]{:S(2)}, u32[]{:S(2)}) collective-permute-start(bf16[128,256]{1,0:T(8,128)(2,1)} %get-tuple-element.139), channel_id=1, source_target_pairs={{0,2},{2,0},{4,6},{6,4},{1,3},{3,1},{5,7},{7,5},{8,10},{10,8},{12,... | collective-permute-start | bytes 196616 | tf_op jit(solution)/shard_map/ppermute | solution.py:366
  234.0 3.6 %shard_map.267 = (bf16[512,1024]{1,0:T(8,128)(2,1)}, bf16[512,1024]{1,0:T(8,128)(2,1)}) custom-call(s32[7]{0:T(128)} %stack.39.refs_0_, bf16[128,1024]{1,0:T(8,128)(2,1)} %get-tuple-element.156.refs_1_, bf16[512,256]{1,0:T(8,128)(2,1)} %get-tuple-element.110.refs_1_.refs_2_, bf16[512,256]{1,0:T(8,128)(2,1)} %copy-done.6, bf16[512,256]{1,0:T(8,128)(2,1)} %copy-done.7, ...), custom_call_target="tpu_custom_call" | custom-call | flops 268435456 | bytes 3407900 | tf_op jit(solution)/shard_map/pallas_call | solution.py:339
  238.3 14.0 %shard_map.268 = (f32[128,1024]{1,0:T(8,128)}, bf16[128,1024]{1,0:T(8,128)(2,1)}, bf16[128,1024]{1,0:T(8,128)(2,1)}, bf16[128,1024]{1,0:T(8,128)(2,1)}, bf16[1024,896]{1,0:T(8,128)(2,1)}) custom-call(s32[7]{0:T(128)} %stack.39.refs_0_, bf16[128,256]{1,0:T(8,128)(2,1)} %get-tuple-element.138.refs_1_, bf16[128,256]{1,0:T(8,128)(2,1)} %copy-done.50, ...), custom_call_target="tpu_custom_call" | custom-call | flops 2281701376 | bytes 9962524 | tf_op jit(solution)/shard_map/pallas_call | solution.py:339
  259.0 2.6 shard_map.271
  269.4 6.6 %collective-permute-done.28.refs_3_.refs_7_ = bf16[128,1024]{1,0:T(8,128)(2,1)S(1)} collective-permute-done((bf16[128,1024]{1,0:T(8,128)(2,1)S(1)}, bf16[128,1024]{1,0:T(8,128)(2,1)S(1)}, u32[]{:S(2)}, u32[]{:S(2)}) %collective-permute-start.28) | collective-permute-done | bytes 262176 | tf_op jit(solution)/shard_map/ppermute | solution.py:366
  279.9 5.1 %collective-permute-start.35 = (bf16[32,3072]{1,0:T(8,128)(2,1)}, bf16[32,3072]{1,0:T(8,128)(2,1)S(1)}, u32[]{:S(2)}, u32[]{:S(2)}) collective-permute-start(bf16[32,3072]{1,0:T(8,128)(2,1)} %get-tuple-element.172), channel_id=1, source_target_pairs={{0,2},{2,0},{4,6},{6,4},{1,3},{3,1},{5,7},{7,5},{8,10},{10,8},{12,... | collective-permute-start | bytes 589832 | tf_op jit(solution)/shard_map/ppermute | solution.py:366
  294.9 6.6 %reduce-scatter.3.cloned.1.call-done.refs_1_ = bf16[128,896]{1,0:T(8,128)(2,1)} async-done(((bf16[1024,896]{1,0:T(8,128)(2,1)}), bf16[128,896]{1,0:T(8,128)(2,1)}) %reduce-scatter.3.cloned.1.call-update) | async-done | bytes 229392 | tf_op jit(solution)/shard_map/reduce_scatter | solution.py:1014
  (212 shorter events, 92.8 us)
Async XLA Ops:
  7.2 67.3 %all-gather.3.cloned.1.call-start = ((), (), s32[]{:S(2)}) async-start(), calls=%async_computation.2 | async-start | bytes 1769472 | tf_op jit(solution)/shard_map/all_gather | solution.py:461
  23.5 85.0 %all-gather.5.cloned.1.call-start = ((), (), s32[]{:S(2)}) async-start(), calls=%async_computation.3 | async-start | bytes 9437184 | tf_op jit(solution)/shard_map/all_gather | solution.py:475
  28.8 9.2 %collective-permute-start.10 = (bf16[32,3072]{1,0:T(8,128)(2,1)}, bf16[32,3072]{1,0:T(8,128)(2,1)S(1)}, u32[]{:S(2)}, u32[]{:S(2)}) collective-permute-start(bf16[32,3072]{1,0:T(8,128)(2,1)} %get-tuple-element.113), channel_id=1, source_target_pairs={{0,2},{2,0},{4,6},{6,4},{1,3},{3,1},{5,7},{7,5},{8,10},{10,8},{12,... | collective-permute-start | bytes 589832 | tf_op jit(solution)/shard_map/ppermute | solution.py:366
  28.8 16.4 %collective-permute-start.11 = (bf16[32,3072]{1,0:T(8,128)(2,1)}, bf16[32,3072]{1,0:T(8,128)(2,1)S(1)}, u32[]{:S(2)}, u32[]{:S(2)}) collective-permute-start(bf16[32,3072]{1,0:T(8,128)(2,1)} %get-tuple-element.114), channel_id=1, source_target_pairs={{0,4},{2,6},{4,0},{6,2},{1,5},{3,7},{5,1},{7,3},{8,12},{10,14},{12... | collective-permute-start | bytes 589832 | tf_op jit(solution)/shard_map/ppermute | solution.py:366
  30.1 15.1 %collective-permute-start.12 = (bf16[32,3072]{1,0:T(8,128)(2,1)}, bf16[32,3072]{1,0:T(8,128)(2,1)S(1)}, u32[]{:S(2)}, u32[]{:S(2)}) collective-permute-start(bf16[32,3072]{1,0:T(8,128)(2,1)} %get-tuple-element.115), channel_id=1, source_target_pairs={{0,6},{2,4},{4,2},{6,0},{1,7},{3,5},{5,3},{7,1},{8,14},{10,12},{12... | collective-permute-start | bytes 589832 | tf_op jit(solution)/shard_map/ppermute | solution.py:366
  48.5 228.0 %reduce-scatter.5.cloned.1.call-start = ((), (), s32[]{:S(2)}) async-start(), calls=%async_computation.5 | async-start | bytes 7077888 | tf_op jit(solution)/shard_map/reduce_scatter | solution.py:815
  48.6 13.6 %collective-permute-start.1 = (bf16[144,1024]{1,0:T(8,128)(2,1)S(1)}, bf16[144,1024]{1,0:T(8,128)(2,1)S(1)}, u32[]{:S(2)}, u32[]{:S(2)}) collective-permute-start(bf16[144,1024]{1,0:T(8,128)(2,1)S(1)} %copy-done), channel_id=1, source_target_pairs={{0,2},{2,0},{4,6},{6,4},{1,3},{3,1},{5,7},{7,5},{8,10},{10,8},{12,... | collective-permute-start | bytes 884744 | tf_op jit(solution)/shard_map/ppermute | solution.py:366
  51.6 22.8 %collective-permute-start.2 = (bf16[144,1024]{1,0:T(8,128)(2,1)S(1)}, bf16[144,1024]{1,0:T(8,128)(2,1)S(1)}, u32[]{:S(2)}, u32[]{:S(2)}) collective-permute-start(bf16[144,1024]{1,0:T(8,128)(2,1)S(1)} %copy-done), channel_id=1, source_target_pairs={{0,4},{2,6},{4,0},{6,2},{1,5},{3,7},{5,1},{7,3},{8,12},{10,14},{12... | collective-permute-start | bytes 884744 | tf_op jit(solution)/shard_map/ppermute | solution.py:366
  51.7 22.8 %collective-permute-start.3 = (bf16[144,1024]{1,0:T(8,128)(2,1)S(1)}, bf16[144,1024]{1,0:T(8,128)(2,1)S(1)}, u32[]{:S(2)}, u32[]{:S(2)}) collective-permute-start(bf16[144,1024]{1,0:T(8,128)(2,1)S(1)} %copy-done), channel_id=1, source_target_pairs={{0,6},{2,4},{4,2},{6,0},{1,7},{3,5},{5,3},{7,1},{8,14},{10,12},{12... | collective-permute-start | bytes 884744 | tf_op jit(solution)/shard_map/ppermute | solution.py:366
  84.4 13.7 %collective-permute-start.7 = (bf16[512,256]{1,0:T(8,128)(2,1)}, bf16[512,256]{1,0:T(8,128)(2,1)S(1)}, u32[]{:S(2)}, u32[]{:S(2)}) collective-permute-start(bf16[512,256]{1,0:T(8,128)(2,1)} %get-tuple-element.110.refs_1_.refs_2_), channel_id=1, source_target_pairs={{0,2},{2,0},{4,6},{6,4},{1,3},{3,1},{5,7},{7,5},{8,10},{10,8},{12,... | collective-permute-start | bytes 786440 | tf_op jit(solution)/shard_map/ppermute | solution.py:366
  88.7 19.8 %collective-permute-start.8 = (bf16[512,256]{1,0:T(8,128)(2,1)}, bf16[512,256]{1,0:T(8,128)(2,1)S(1)}, u32[]{:S(2)}, u32[]{:S(2)}) collective-permute-start(bf16[512,256]{1,0:T(8,128)(2,1)} %get-tuple-element.110.refs_1_.refs_2_), channel_id=1, source_target_pairs={{0,4},{2,6},{4,0},{6,2},{1,5},{3,7},{5,1},{7,3},{8,12},{10,14},{12... | collective-permute-start | bytes 786440 | tf_op jit(solution)/shard_map/ppermute | solution.py:366
  88.7 19.8 %collective-permute-start.9 = (bf16[512,256]{1,0:T(8,128)(2,1)}, bf16[512,256]{1,0:T(8,128)(2,1)S(1)}, u32[]{:S(2)}, u32[]{:S(2)}) collective-permute-start(bf16[512,256]{1,0:T(8,128)(2,1)} %get-tuple-element.110.refs_1_.refs_2_), channel_id=1, source_target_pairs={{0,6},{2,4},{4,2},{6,0},{1,7},{3,5},{5,3},{7,1},{8,14},{10,12},{12... | collective-permute-start | bytes 786440 | tf_op jit(solution)/shard_map/ppermute | solution.py:366
  121.6 14.4 %collective-permute-start.13 = (bf16[128,1024]{1,0:T(8,128)(2,1)}, bf16[128,1024]{1,0:T(8,128)(2,1)S(1)}, u32[]{:S(2)}, u32[]{:S(2)}) collective-permute-start(bf16[128,1024]{1,0:T(8,128)(2,1)} %get-tuple-element.119), channel_id=1, source_target_pairs={{0,2},{2,0},{4,6},{6,4},{1,3},{3,1},{5,7},{7,5},{8,10},{10,8},{12,... | collective-permute-start | bytes 786440 | tf_op jit(solution)/shard_map/ppermute | solution.py:366
  126.7 21.3 %collective-permute-start.14 = (bf16[128,1024]{1,0:T(8,128)(2,1)}, bf16[128,1024]{1,0:T(8,128)(2,1)S(1)}, u32[]{:S(2)}, u32[]{:S(2)}) collective-permute-start(bf16[128,1024]{1,0:T(8,128)(2,1)} %get-tuple-element.120), channel_id=1, source_target_pairs={{0,4},{2,6},{4,0},{6,2},{1,5},{3,7},{5,1},{7,3},{8,12},{10,14},{12... | collective-permute-start | bytes 786440 | tf_op jit(solution)/shard_map/ppermute | solution.py:366
  126.7 21.3 %collective-permute-start.15 = (bf16[128,1024]{1,0:T(8,128)(2,1)}, bf16[128,1024]{1,0:T(8,128)(2,1)S(1)}, u32[]{:S(2)}, u32[]{:S(2)}) collective-permute-start(bf16[128,1024]{1,0:T(8,128)(2,1)} %get-tuple-element.121), channel_id=1, source_target_pairs={{0,6},{2,4},{4,2},{6,0},{1,7},{3,5},{5,3},{7,1},{8,14},{10,12},{12... | collective-permute-start | bytes 786440 | tf_op jit(solution)/shard_map/ppermute | solution.py:366
  151.7 13.1 %collective-permute-start.18 = (bf16[128,1024]{1,0:T(8,128)(2,1)}, bf16[128,1024]{1,0:T(8,128)(2,1)S(1)}, u32[]{:S(2)}, u32[]{:S(2)}) collective-permute-start(bf16[128,1024]{1,0:T(8,128)(2,1)} %get-tuple-element.127.refs_1_), channel_id=1, source_target_pairs={{0,2},{2,0},{4,6},{6,4},{1,3},{3,1},{5,7},{7,5},{8,10},{10,8},{12,... | collective-permute-start | bytes 786440 | tf_op jit(solution)/shard_map/ppermute | solution.py:366
  155.9 20.4 %collective-permute-start.19 = (bf16[128,1024]{1,0:T(8,128)(2,1)}, bf16[128,1024]{1,0:T(8,128)(2,1)S(1)}, u32[]{:S(2)}, u32[]{:S(2)}) collective-permute-start(bf16[128,1024]{1,0:T(8,128)(2,1)} %get-tuple-element.127.refs_1_), channel_id=1, source_target_pairs={{0,4},{2,6},{4,0},{6,2},{1,5},{3,7},{5,1},{7,3},{8,12},{10,14},{12... | collective-permute-start | bytes 786440 | tf_op jit(solution)/shard_map/ppermute | solution.py:366
  155.9 20.4 %collective-permute-start.20 = (bf16[128,1024]{1,0:T(8,128)(2,1)}, bf16[128,1024]{1,0:T(8,128)(2,1)S(1)}, u32[]{:S(2)}, u32[]{:S(2)}) collective-permute-start(bf16[128,1024]{1,0:T(8,128)(2,1)} %get-tuple-element.127.refs_1_), channel_id=1, source_target_pairs={{0,6},{2,4},{4,2},{6,0},{1,7},{3,5},{5,3},{7,1},{8,14},{10,12},{12... | collective-permute-start | bytes 786440 | tf_op jit(solution)/shard_map/ppermute | solution.py:366
  194.5 107.0 %reduce-scatter.3.cloned.1.call-start = ((), (), s32[]{:S(2)}) async-start(), calls=%async_computation.4 | async-start | bytes 2064384 | tf_op jit(solution)/shard_map/reduce_scatter | solution.py:1014
  195.4 12.9 %collective-permute-start.21 = (bf16[128,1024]{1,0:T(8,128)(2,1)S(1)}, bf16[128,1024]{1,0:T(8,128)(2,1)S(1)}, u32[]{:S(2)}, u32[]{:S(2)}) collective-permute-start(bf16[128,1024]{1,0:T(8,128)(2,1)S(1)} %copy-done.45), channel_id=1, source_target_pairs={{0,2},{2,0},{4,6},{6,4},{1,3},{3,1},{5,7},{7,5},{8,10},{10,8},{12,... | collective-permute-start | bytes 786440 | tf_op jit(solution)/shard_map/ppermute | solution.py:366
  199.5 20.2 %collective-permute-start.22 = (bf16[128,1024]{1,0:T(8,128)(2,1)S(1)}, bf16[128,1024]{1,0:T(8,128)(2,1)S(1)}, u32[]{:S(2)}, u32[]{:S(2)}) collective-permute-start(bf16[128,1024]{1,0:T(8,128)(2,1)S(1)} %copy-done.44), channel_id=1, source_target_pairs={{0,4},{2,6},{4,0},{6,2},{1,5},{3,7},{5,1},{7,3},{8,12},{10,14},{12... | collective-permute-start | bytes 786440 | tf_op jit(solution)/shard_map/ppermute | solution.py:366
  199.5 20.2 %collective-permute-start.23 = (bf16[128,1024]{1,0:T(8,128)(2,1)S(1)}, bf16[128,1024]{1,0:T(8,128)(2,1)S(1)}, u32[]{:S(2)}, u32[]{:S(2)}) collective-permute-start(bf16[128,1024]{1,0:T(8,128)(2,1)S(1)} %copy-done.43), channel_id=1, source_target_pairs={{0,6},{2,4},{4,2},{6,0},{1,7},{3,5},{5,3},{7,1},{8,14},{10,12},{12... | collective-permute-start | bytes 786440 | tf_op jit(solution)/shard_map/ppermute | solution.py:366
  226.7 10.9 %collective-permute-start.24 = (bf16[128,256]{1,0:T(8,128)(2,1)}, bf16[128,256]{1,0:T(8,128)(2,1)S(1)}, u32[]{:S(2)}, u32[]{:S(2)}) collective-permute-start(bf16[128,256]{1,0:T(8,128)(2,1)} %get-tuple-element.139), channel_id=1, source_target_pairs={{0,2},{2,0},{4,6},{6,4},{1,3},{3,1},{5,7},{7,5},{8,10},{10,8},{12,... | collective-permute-start | bytes 196616 | tf_op jit(solution)/shard_map/ppermute | solution.py:366
  253.6 13.3 %collective-permute-start.27 = (bf16[128,1024]{1,0:T(8,128)(2,1)S(1)}, bf16[128,1024]{1,0:T(8,128)(2,1)S(1)}, u32[]{:S(2)}, u32[]{:S(2)}) collective-permute-start(bf16[128,1024]{1,0:T(8,128)(2,1)S(1)} %copy-done.42), channel_id=1, source_target_pairs={{0,2},{2,0},{4,6},{6,4},{1,3},{3,1},{5,7},{7,5},{8,10},{10,8},{12,... | collective-permute-start | bytes 786440 | tf_op jit(solution)/shard_map/ppermute | solution.py:366
  254.7 21.3 %collective-permute-start.28 = (bf16[128,1024]{1,0:T(8,128)(2,1)S(1)}, bf16[128,1024]{1,0:T(8,128)(2,1)S(1)}, u32[]{:S(2)}, u32[]{:S(2)}) collective-permute-start(bf16[128,1024]{1,0:T(8,128)(2,1)S(1)} %copy-done.41), channel_id=1, source_target_pairs={{0,4},{2,6},{4,0},{6,2},{1,5},{3,7},{5,1},{7,3},{8,12},{10,14},{12... | collective-permute-start | bytes 786440 | tf_op jit(solution)/shard_map/ppermute | solution.py:366
  256.0 20.0 %collective-permute-start.29 = (bf16[128,1024]{1,0:T(8,128)(2,1)S(1)}, bf16[128,1024]{1,0:T(8,128)(2,1)S(1)}, u32[]{:S(2)}, u32[]{:S(2)}) collective-permute-start(bf16[128,1024]{1,0:T(8,128)(2,1)S(1)} %copy-done.40), channel_id=1, source_target_pairs={{0,6},{2,4},{4,2},{6,0},{1,7},{3,5},{5,3},{7,1},{8,14},{10,12},{12... | collective-permute-start | bytes 786440 | tf_op jit(solution)/shard_map/ppermute | solution.py:366
  261.6 14.4 %collective-permute-start.32 = (bf16[128,1024]{1,0:T(8,128)(2,1)}, bf16[128,1024]{1,0:T(8,128)(2,1)S(1)}, u32[]{:S(2)}, u32[]{:S(2)}) collective-permute-start(bf16[128,1024]{1,0:T(8,128)(2,1)} %get-tuple-element.168), channel_id=1, source_target_pairs={{0,8},{8,0},{16,24},{24,16},{1,9},{9,1},{17,25},{25,17},{2,10},{10... | collective-permute-start | bytes 786440 | tf_op jit(solution)/shard_map/ppermute | solution.py:366
  263.1 13.4 %collective-permute-start.33 = (bf16[128,1024]{1,0:T(8,128)(2,1)}, bf16[128,1024]{1,0:T(8,128)(2,1)S(1)}, u32[]{:S(2)}, u32[]{:S(2)}) collective-permute-start(bf16[128,1024]{1,0:T(8,128)(2,1)} %get-tuple-element.169), channel_id=1, source_target_pairs={{0,16},{8,24},{16,0},{24,8},{1,17},{9,25},{17,1},{25,9},{2,18},{10... | collective-permute-start | bytes 786440 | tf_op jit(solution)/shard_map/ppermute | solution.py:366
  266.9 9.7 %collective-permute-start.34 = (bf16[128,1024]{1,0:T(8,128)(2,1)}, bf16[128,1024]{1,0:T(8,128)(2,1)S(1)}, u32[]{:S(2)}, u32[]{:S(2)}) collective-permute-start(bf16[128,1024]{1,0:T(8,128)(2,1)} %get-tuple-element.170), channel_id=1, source_target_pairs={{0,24},{8,16},{16,8},{24,0},{1,25},{9,17},{17,9},{25,1},{2,26},{10... | collective-permute-start | bytes 786440 | tf_op jit(solution)/shard_map/ppermute | solution.py:366
  279.9 21.6 %collective-permute-start.35 = (bf16[32,3072]{1,0:T(8,128)(2,1)}, bf16[32,3072]{1,0:T(8,128)(2,1)S(1)}, u32[]{:S(2)}, u32[]{:S(2)}) collective-permute-start(bf16[32,3072]{1,0:T(8,128)(2,1)} %get-tuple-element.172), channel_id=1, source_target_pairs={{0,2},{2,0},{4,6},{6,4},{1,3},{3,1},{5,7},{7,5},{8,10},{10,8},{12,... | collective-permute-start | bytes 589832 | tf_op jit(solution)/shard_map/ppermute | solution.py:366
  284.9 23.3 %collective-permute-start.39 = (bf16[32,3072]{1,0:T(8,128)(2,1)}, bf16[32,3072]{1,0:T(8,128)(2,1)S(1)}, u32[]{:S(2)}, u32[]{:S(2)}) collective-permute-start(bf16[32,3072]{1,0:T(8,128)(2,1)} %get-tuple-element.181), channel_id=1, source_target_pairs={{0,4},{2,6},{4,0},{6,2},{1,5},{3,7},{5,1},{7,3},{8,12},{10,14},{12... | collective-permute-start | bytes 589832 | tf_op jit(solution)/shard_map/ppermute | solution.py:366
  285.1 23.2 %collective-permute-start.40 = (bf16[32,3072]{1,0:T(8,128)(2,1)}, bf16[32,3072]{1,0:T(8,128)(2,1)S(1)}, u32[]{:S(2)}, u32[]{:S(2)}) collective-permute-start(bf16[32,3072]{1,0:T(8,128)(2,1)} %get-tuple-element.182), channel_id=1, source_target_pairs={{0,6},{2,4},{4,2},{6,0},{1,7},{3,5},{5,3},{7,1},{8,14},{10,12},{12... | collective-permute-start | bytes 589832 | tf_op jit(solution)/shard_map/ppermute | solution.py:366
  (66 other events, 260.6 us)
Sparse Core Ops, SparseCore 0:
  23.6 24.0 all-gather.2
  49.6 54.3 all-gather.4
  194.6 63.5 reduce-scatter.4
  261.8 39.6 reduce-scatter.2
